TPU v7x, 32 devices: a whole 2x2x4 slice. The times are simulated.
32 devices in a mesh: lon: 8 (over z, x), lat: 4 (over y, core).
Axes of the slice: x: 2, y: 2, z: 4, core: 2. Of those that a mesh axis runs over, the one named last changes fastest.
Arguments:
- ensemble: bfloat16 [40, 2, 512, 2048], P(None, None, 'lat', 'lon'), may hold values from -6 to 6
- gradient: bfloat16 [2, 512, 2048], P(None, 'lat', 'lon'), may hold values from -6 to 6
Outputs:
- control: bfloat16 [40, 2, 512, 2048], P(None, None, 'lat', 'lon')
All inputs are finite; a program needn't handle non-finite values.
Results may differ from a plain program's by a relative error of at most 0.0073.
Values may be sent and summed in bfloat16 or wider, within the bound.
No kernel may reach another device: no remote copies, remote signals or barrier semaphores. Data moves between devices by JAX's collectives and lax.ppermute only.
A program may use at most 128 MiB of HBM per device.

v0:
```python
import jax
import jax.numpy as jnp
from jax import lax
from jax.sharding import PartitionSpec as P

HALF = 30


def padded(block, sides, width, periodic):
    for axis, dim in sides:
        count = lax.axis_size(axis)
        forward = [(i, i + 1) for i in range(count - 1)]
        if periodic:
            forward.append((count - 1, 0))
        backward = [(target, source) for source, target in forward]
        low = lax.ppermute(
            lax.slice_in_dim(block, block.shape[dim] - width, None, axis=dim), axis, forward
        )
        high = lax.ppermute(lax.slice_in_dim(block, 0, width, axis=dim), axis, backward)
        block = jnp.concatenate([low, block, high], axis=dim)
    return block


def kernel_matrix(block_len, half_width):
    spread = 1.0 * half_width
    row_index = jnp.arange(block_len + 2 * half_width)[:, None]
    col_index = jnp.arange(block_len)[None, :]
    offset = (row_index - col_index - half_width).astype(jnp.float32)
    offsets = jnp.arange(-half_width, half_width + 1).astype(jnp.float32)
    normalizer = jnp.sqrt(jnp.sum(jnp.exp(-offsets * offsets / (spread * spread))))
    weights = (
        jnp.where(
            jnp.abs(offset) <= half_width, jnp.exp(-offset * offset / (2.0 * spread * spread)), 0.0
        )
        / normalizer
    )
    return weights.astype(jnp.bfloat16)


def shards(ensemble, gradient):
    lat_rows = ensemble.shape[2]
    lon_width = ensemble.shape[3]
    product = (ensemble.astype(jnp.float32) * gradient.astype(jnp.float32)[None]).astype(
        jnp.bfloat16
    )
    lon_kernel = kernel_matrix(lon_width, HALF)
    lat_kernel = kernel_matrix(lat_rows, HALF)
    widened = padded(product, (("lon", 3),), HALF, True)
    lon_done = jnp.einsum(
        "mlap,pq->mlaq", widened, lon_kernel, preferred_element_type=jnp.float32
    ).astype(jnp.bfloat16)
    widened_lat = padded(lon_done, (("lat", 2),), HALF, False)
    return jnp.einsum(
        "mlpc,pq->mlqc", widened_lat, lat_kernel, preferred_element_type=jnp.float32
    ).astype(jnp.bfloat16)


def solution(mesh):
    placed = (P(None, None, "lat", "lon"), P(None, "lat", "lon"))
    return jax.shard_map(
        shards, mesh=mesh, in_specs=placed, out_specs=P(None, None, "lat", "lon"), check_vma=False
    )
```

profile of v0, /device:TPU:1, one launch (start us, length us, event | category | flops | bytes accessed | tf_op | source)
XLA Modules:
  0.0 78.1 jit_solution(13073275682719717758)
XLA Ops:
  0.0 1.0 %copy.6 = f32[2,128,256]{1,2,0:T(8,128)S(1)} copy(bf16[2,128,256]{2,1,0:T(8,128)(2,1)} %param.3) | data formatting | bytes 393216 | tf_op jit(solution)/shard_map/convert_element_type | solution.py:43
  1.0 7.9 %copy.5 = bf16[40,2,128,256]{2,3,1,0:T(8,128)(2,1)} copy(bf16[40,2,128,256]{3,2,1,0:T(8,128)(2,1)} %param.2) | data formatting | bytes 10485760 | tf_op args[0]
  8.9 4.0 %multiply_convert_fusion = bf16[40,2,128,256]{2,3,1,0:T(8,128)(2,1)S(1)} fusion(bf16[40,2,128,256]{2,3,1,0:T(8,128)(2,1)} %copy.5, f32[2,128,256]{1,2,0:T(8,128)S(1)} %copy.6), kind=kLoop, calls=%fused_computation | loop fusion | flops 7864320 | bytes 10747904 | tf_op jit(solution)/shard_map/convert_element_type | solution.py:43
  12.9 2.3 %copy-done = bf16[40,2,128,256]{2,3,1,0:T(8,128)(2,1)} copy-done((bf16[40,2,128,256]{2,3,1,0:T(8,128)(2,1)}, bf16[40,2,128,256]{2,3,1,0:T(8,128)(2,1)S(1)}, u32[]{:S(2)}) %copy-start) | copy-done | bytes 5242904
  15.3 0.4 fusion.55
  15.7 0.4 copy.8
  16.1 5.1 %collective-permute-start.1 = (bf16[40,2,128,30]{2,0,3,1:T(8,128)(2,1)S(1)}, bf16[40,2,128,30]{2,0,3,1:T(8,128)(2,1)S(1)}, u32[]{:S(2)}, u32[]{:S(2)}) collective-permute-start(bf16[40,2,128,30]{2,0,3,1:T(8,128)(2,1)S(1)} %copy.8), channel_id=1, source_target_pairs={{4,0},{8,4},{12,8},{16,12},{20,16},{24,20},{28,24},{0,28},{5,1},{9... | collective-permute-start | bytes 1843208 | tf_op jit(solution)/shard_map/ppermute | solution.py:19
  21.2 0.4 copy.7
  21.7 0.6 fusion.43
  22.9 21.9 %collective-permute-done.1 = bf16[40,2,128,30]{2,0,3,1:T(8,128)(2,1)S(1)} collective-permute-done((bf16[40,2,128,30]{2,0,3,1:T(8,128)(2,1)S(1)}, bf16[40,2,128,30]{2,0,3,1:T(8,128)(2,1)S(1)}, u32[]{:S(2)}, u32[]{:S(2)}) %collective-permute-start.1) | collective-permute-done | bytes 614432 | tf_op jit(solution)/shard_map/ppermute | solution.py:19
  44.9 0.2 copy.10
  45.1 0.7 collective-permute-done
  45.8 0.2 copy.9
  46.0 5.2 %fusion.12 = bf16[40,2,128,256]{3,2,1,0:T(8,128)(2,1)S(1)} fusion(bf16[40,2,128,30]{2,3,1,0:T(8,128)(2,1)S(1)} %copy.10, bf16[40,2,128,256]{2,3,1,0:T(8,128)(2,1)} %copy-done, bf16[40,2,128,30]{2,3,1,0:T(8,128)(2,1)S(1)} %copy.9, f32[]{:T(128)S(6)} %sqrt.4), kind=kOutput, calls=%fused_computation.14 | convolution fusion | flops 1679676416 | bytes 11714564 | tf_op jit(solution)/shard_map/mlap,pq->mlaq/dot_general | solution.py:49
  51.2 0.7 fusion.54
  51.9 0.7 copy.12
  52.6 2.4 %collective-permute-start.3 = (bf16[40,2,30,256]{3,0,2,1:T(8,128)(2,1)S(1)}, bf16[40,2,30,256]{3,0,2,1:T(8,128)(2,1)S(1)}, u32[]{:S(2)}, u32[]{:S(2)}) collective-permute-start(bf16[40,2,30,256]{3,0,2,1:T(8,128)(2,1)S(1)} %copy.12), channel_id=1, source_target_pairs={{1,0},{2,1},{3,2},{5,4},{6,5},{7,6},{9,8},{10,9},{11,10},{13,12},{... | collective-permute-start | bytes 3686408 | tf_op jit(solution)/shard_map/ppermute | solution.py:19
  55.0 0.7 copy.11
  55.7 3.3 %collective-permute-start.2 = (bf16[40,2,30,256]{3,0,2,1:T(8,128)(2,1)S(1)}, bf16[40,2,30,256]{3,0,2,1:T(8,128)(2,1)S(1)}, u32[]{:S(2)}, u32[]{:S(2)}) collective-permute-start(bf16[40,2,30,256]{3,0,2,1:T(8,128)(2,1)S(1)} %copy.11), channel_id=1, source_target_pairs={{0,1},{1,2},{2,3},{4,5},{5,6},{6,7},{8,9},{9,10},{10,11},{12,13},{... | collective-permute-start | bytes 3686408 | tf_op jit(solution)/shard_map/ppermute | solution.py:16
  59.0 11.8 %collective-permute-done.3 = bf16[40,2,30,256]{3,0,2,1:T(8,128)(2,1)S(1)} collective-permute-done((bf16[40,2,30,256]{3,0,2,1:T(8,128)(2,1)S(1)}, bf16[40,2,30,256]{3,0,2,1:T(8,128)(2,1)S(1)}, u32[]{:S(2)}, u32[]{:S(2)}) %collective-permute-start.3) | collective-permute-done | bytes 1228832 | tf_op jit(solution)/shard_map/ppermute | solution.py:19
  70.8 0.3 copy.14
  71.1 1.6 %collective-permute-done.2 = bf16[40,2,30,256]{3,0,2,1:T(8,128)(2,1)S(1)} collective-permute-done((bf16[40,2,30,256]{3,0,2,1:T(8,128)(2,1)S(1)}, bf16[40,2,30,256]{3,0,2,1:T(8,128)(2,1)S(1)}, u32[]{:S(2)}, u32[]{:S(2)}) %collective-permute-start.2) | collective-permute-done | bytes 1228832 | tf_op jit(solution)/shard_map/ppermute | solution.py:16
  72.7 0.3 copy.13
  73.0 5.1 %convert_bitcast_fusion = bf16[40,2,128,256]{3,2,1,0:T(8,128)(2,1)} fusion(bf16[40,2,30,256]{3,2,1,0:T(8,128)(2,1)S(1)} %copy.14, bf16[40,2,128,256]{3,2,1,0:T(8,128)(2,1)S(1)} %fusion.12, bf16[40,2,30,256]{3,2,1,0:T(8,128)(2,1)S(1)} %copy.13, f32[]{:T(128)S(6)} %sqrt.4), kind=kOutput, calls=%fused_computation.13 | convolution fusion | flops 1011649024 | bytes 12943364 | tf_op jit(solution)/shard_map/mlpc,pq->mlqc/dot_general | solution.py:53
  (2 shorter events, 0.1 us)
Async XLA Ops:
  12.9 2.4 %copy-start = (bf16[40,2,128,256]{2,3,1,0:T(8,128)(2,1)}, bf16[40,2,128,256]{2,3,1,0:T(8,128)(2,1)S(1)}, u32[]{:S(2)}) copy-start(bf16[40,2,128,256]{2,3,1,0:T(8,128)(2,1)S(1)} %multiply_convert_fusion) | copy-start | bytes 15728644
  16.1 28.8 %collective-permute-start.1 = (bf16[40,2,128,30]{2,0,3,1:T(8,128)(2,1)S(1)}, bf16[40,2,128,30]{2,0,3,1:T(8,128)(2,1)S(1)}, u32[]{:S(2)}, u32[]{:S(2)}) collective-permute-start(bf16[40,2,128,30]{2,0,3,1:T(8,128)(2,1)S(1)} %copy.8), channel_id=1, source_target_pairs={{4,0},{8,4},{12,8},{16,12},{20,16},{24,20},{28,24},{0,28},{5,1},{9... | collective-permute-start | bytes 1843208 | tf_op jit(solution)/shard_map/ppermute | solution.py:19
  21.6 24.2 %collective-permute-start = (bf16[40,2,128,30]{2,0,3,1:T(8,128)(2,1)S(1)}, bf16[40,2,128,30]{2,0,3,1:T(8,128)(2,1)S(1)}, u32[]{:S(2)}, u32[]{:S(2)}) collective-permute-start(bf16[40,2,128,30]{2,0,3,1:T(8,128)(2,1)S(1)} %copy.7), channel_id=1, source_target_pairs={{0,4},{4,8},{8,12},{12,16},{16,20},{20,24},{24,28},{28,0},{1,5},{5... | collective-permute-start | bytes 1843208 | tf_op jit(solution)/shard_map/ppermute | solution.py:16
  52.6 18.2 %collective-permute-start.3 = (bf16[40,2,30,256]{3,0,2,1:T(8,128)(2,1)S(1)}, bf16[40,2,30,256]{3,0,2,1:T(8,128)(2,1)S(1)}, u32[]{:S(2)}, u32[]{:S(2)}) collective-permute-start(bf16[40,2,30,256]{3,0,2,1:T(8,128)(2,1)S(1)} %copy.12), channel_id=1, source_target_pairs={{1,0},{2,1},{3,2},{5,4},{6,5},{7,6},{9,8},{10,9},{11,10},{13,12},{... | collective-permute-start | bytes 3686408 | tf_op jit(solution)/shard_map/ppermute | solution.py:19
  55.7 17.0 %collective-permute-start.2 = (bf16[40,2,30,256]{3,0,2,1:T(8,128)(2,1)S(1)}, bf16[40,2,30,256]{3,0,2,1:T(8,128)(2,1)S(1)}, u32[]{:S(2)}, u32[]{:S(2)}) collective-permute-start(bf16[40,2,30,256]{3,0,2,1:T(8,128)(2,1)S(1)} %copy.11), channel_id=1, source_target_pairs={{0,1},{1,2},{2,3},{4,5},{5,6},{6,7},{8,9},{9,10},{10,11},{12,13},{... | collective-permute-start | bytes 3686408 | tf_op jit(solution)/shard_map/ppermute | solution.py:16
where the time goes:
time: 79.2 us; the launch traced here: 78.1 us
  waiting for transfers between devices  36 us (45%)
  local copies, waits for them, and re-layouts  15.4 us (19%)
  starting transfers between devices  10.9 us (14%)
  matrix products  10.4 us (13%)
  other arithmetic  4.6 us (6%)
    ppermute x2, waiting for transfers between devices, padded(): lax.ppermute(lax.slice_in_dim(block, 0, width, axis=dim), axis, backward)  33.7 us
    unnamed x3, local copies, waits for them, and re-layouts  10.3 us
    ppermute x2, starting transfers between devices, padded(): lax.ppermute(lax.slice_in_dim(block, 0, width, axis=dim), axis, backward)  7.55 us
    dot_general x1, matrix products, shards(): jnp.einsum('mlap,pq->mlaq', widened, lon_kernel, preferred_element_type=j...  5.23 us
    dot_general x1, matrix products, shards(): jnp.einsum('mlpc,pq->mlqc', widened_lat, lat_kernel, preferred_element_ty...  5.14 us
    convert_element_type x1, other arithmetic, shards(): (ensemble.astype(jnp.float32) * gradient.astype(jnp.float32)[None]).astyp...  3.98 us
    ppermute x2, starting transfers between devices, padded(): lax.ppermute(lax.slice_in_dim(block, block.shape[dim] - width, None, axis...  3.35 us
    ppermute x2, waiting for transfers between devices, padded(): lax.ppermute(lax.slice_in_dim(block, block.shape[dim] - width, None, axis...  2.29 us
  transfers between devices with their start and end apart: 4, of which 4 were waited for; matrix products, arithmetic and copies ran while one was open for 3% of the time, Pallas kernels for 0%

commit v1 on v0

v1 whole, which is shorter than its diff:
```python
import jax
import jax.numpy as jnp
import numpy as np
from jax import lax
from jax.experimental import pallas as pl
from jax.experimental.pallas import tpu as pltpu
from jax.sharding import PartitionSpec as P

HALF = 30
LANES = 128
EDGE = 32
GROUP = 17
VMEM = 48 * 1024 * 1024


def taps():
    offsets = np.arange(-HALF, HALF + 1).astype(np.float32)
    spread = np.float32(HALF)
    norm = np.sqrt(np.sum(np.exp(-offsets * offsets / (spread * spread)), dtype=np.float32))
    return (np.exp(-offsets * offsets / (2 * spread * spread)) / norm).astype(jnp.bfloat16)


def band(block_len, margin):
    k = taps()
    out = np.zeros((block_len + 2 * margin, block_len), jnp.bfloat16)
    for q in range(block_len):
        out[q + margin - HALF : q + margin + HALF + 1, q] = k
    return out


def lane_of(slot, j):
    if slot < 4:
        return HALF * slot + j
    lane = j - 8 * (slot - 4)
    return 120 + lane if 0 <= lane < 8 else None


def lon_constants(width):
    lon = band(width, HALF)
    select = np.zeros((8, width, 2 * LANES), jnp.bfloat16)
    spread = np.zeros((8, 2 * LANES, width), jnp.bfloat16)
    for s in range(8):
        for j in range(HALF):
            lane = lane_of(s, j)
            if lane is None:
                continue
            select[s, width - HALF + j, lane] = 1
            select[s, j, LANES + lane] = 1
            spread[s, lane] = lon[j]
            spread[s, LANES + lane] = lon[width + HALF + j]
    return select, spread, lon[HALF : HALF + width]


def dot(a, b):
    return jnp.dot(a, b, preferred_element_type=jnp.float32)


def product(ens, grad):
    return (ens.astype(jnp.float32) * grad.astype(jnp.float32)).astype(jnp.bfloat16)


def products(ens_ref, grad_ref, first, count):
    grads = [grad_ref[0], grad_ref[1]]
    even = lax.rem(first, 2) == 0
    flip = [jnp.where(even, grads[0], grads[1]), jnp.where(even, grads[1], grads[0])]
    return [product(ens_ref[i], flip[i % 2]) for i in range(count)]


def pack_group(fields, select_ref, right_ref, left_ref):
    rows = fields[0].shape[0]
    extra = dot(fields[16], select_ref[4])
    extras = [extra] + [dot(fields[16], select_ref[4 + t]) for t in range(1, 4)]
    acc = jnp.concatenate(extras, axis=0)
    for s in range(4):
        acc += dot(jnp.concatenate(fields[4 * s : 4 * s + 4], axis=0), select_ref[s])
    acc = acc.astype(jnp.bfloat16)
    for t in range(4):
        tile = acc[t * rows : (t + 1) * rows]
        right_ref[t] = tile[:, :LANES]
        left_ref[t] = tile[:, LANES:]


def spread_group(fields, low_ref, high_ref, center, spread_ref):
    rows = fields[0].shape[0]
    tiles = [jnp.concatenate([low_ref[t], high_ref[t]], axis=1) for t in range(4)]
    halo = jnp.concatenate(tiles, axis=0)
    out = []
    for s in range(4):
        block = dot(jnp.concatenate(fields[4 * s : 4 * s + 4], axis=0), center)
        block = (block + dot(halo, spread_ref[s])).astype(jnp.bfloat16)
        out += [block[t * rows : (t + 1) * rows] for t in range(4)]
    last = dot(fields[16], center)
    for t in range(4):
        last += dot(tiles[t], spread_ref[4 + t])
    return out + [last.astype(jnp.bfloat16)]


def pack_kernel(ens_ref, grad_ref, select_ref, right_ref, left_ref):
    fields = products(ens_ref, grad_ref, pl.program_id(0) * GROUP, GROUP)
    pack_group(fields, select_ref, right_ref, left_ref)


def rows_kernel(first, head_ref, tail_ref, ghead_ref, gtail_ref, up_ref, down_ref):
    start = first + pl.program_id(0) * head_ref.shape[0]
    for i, v in enumerate(products(head_ref, ghead_ref, start, head_ref.shape[0])):
        down_ref[i] = v
    for i, v in enumerate(products(tail_ref, gtail_ref, start, head_ref.shape[0])):
        up_ref[i] = v


def lat_group(fields, low_ref, high_ref, lat):
    out = []
    for i, v in enumerate(fields):
        wide = jnp.concatenate([low_ref[i], v, high_ref[i]], axis=0)
        out.append(dot(lat, wide).astype(jnp.bfloat16))
    return out


def lat_pack_kernel(first, ens_ref, grad_ref, low_ref, high_ref, lat_ref, select_ref, done_ref, right_ref, left_ref):
    start = first + pl.program_id(0) * GROUP
    fields = products(ens_ref, grad_ref, start, GROUP)
    fields = lat_group(fields, low_ref, high_ref, lat_ref[...])
    for i, v in enumerate(fields):
        done_ref[i] = v
    pack_group(fields, select_ref, right_ref, left_ref)


def lat_pack4_kernel(first, ens_ref, grad_ref, low_ref, high_ref, lat_ref, select_ref, done_ref, right_ref, left_ref):
    fields = products(ens_ref, grad_ref, jnp.int32(first), 4)
    fields = lat_group(fields, low_ref, high_ref, lat_ref[...])
    acc = None
    for s, v in enumerate(fields):
        done_ref[s] = v
        part = dot(v, select_ref[s])
        acc = part if acc is None else acc + part
    acc = acc.astype(jnp.bfloat16)
    right_ref[0] = acc[:, :LANES]
    left_ref[0] = acc[:, LANES:]


def lon_kernel(ens_ref, grad_ref, low_ref, high_ref, center_ref, spread_ref, done_ref, up_ref, down_ref):
    fields = products(ens_ref, grad_ref, pl.program_id(0) * GROUP, GROUP)
    for i, v in enumerate(spread_group(fields, low_ref, high_ref, center_ref[...], spread_ref)):
        done_ref[i] = v
        down_ref[i] = v[:EDGE]
        up_ref[i] = v[v.shape[0] - EDGE :]


def lat_kernel(done_ref, low_ref, high_ref, lat_ref, out_ref):
    fields = [done_ref[i] for i in range(GROUP)]
    for i, v in enumerate(lat_group(fields, low_ref, high_ref, lat_ref[...])):
        out_ref[i] = v


def last_kernel(done_ref, low_ref, high_ref, center_ref, spread_ref, whole_ref, out_ref):
    del whole_ref
    fields = [done_ref[i] for i in range(GROUP)]
    for i, v in enumerate(spread_group(fields, low_ref, high_ref, center_ref[...], spread_ref)):
        out_ref[i] = v


def last4_kernel(done_ref, low_ref, high_ref, center_ref, spread_ref, whole_ref, out_ref):
    del whole_ref
    halo = jnp.concatenate([low_ref[0], high_ref[0]], axis=1)
    for s in range(4):
        out_ref[s] = (dot(done_ref[s], center_ref[...]) + dot(halo, spread_ref[s])).astype(jnp.bfloat16)


def neighbours(axis, periodic):
    count = lax.axis_size(axis)
    forward = [(i, i + 1) for i in range(count - 1)]
    if periodic:
        forward.append((count - 1, 0))
    return forward, [(b, a) for a, b in forward]


def exchange(up, down, axis, periodic):
    forward, backward = neighbours(axis, periodic)
    return lax.ppermute(up, axis, forward), lax.ppermute(down, axis, backward)


def whole(*shape):
    return pl.BlockSpec(shape, lambda b: (0,) * len(shape))


def params():
    return pltpu.CompilerParams(vmem_limit_bytes=VMEM)


def cost(fields, passes, size):
    return pl.CostEstimate(
        flops=int(fields * passes * 2 * 128 * 256 * 256), bytes_accessed=int(size), transcendentals=0
    )


def shards(ensemble, gradient):
    members, levels, rows, width = ensemble.shape
    total = members * levels
    ens = ensemble.reshape(total, rows, width)
    bf = jnp.bfloat16
    n_p = 2
    n_q = 2
    rest = (total - GROUP * (n_p + n_q)) // 4
    p_end = GROUP * n_p
    q_end = p_end + GROUP * n_q
    select, spread, center = lon_constants(width)
    lat = band(rows, EDGE).T.copy()
    select, spread, center, lat = map(jnp.asarray, (select, spread, center, lat))
    select4, spread4 = select[:4], spread[:4]

    def block(n, r, c, shift=0):
        return pl.BlockSpec((n, r, c), lambda b: (b + shift, 0, 0))

    grad_spec = whole(levels, rows, width)
    select_spec = whole(8, width, 2 * LANES)
    spread_spec = whole(8, 2 * LANES, width)
    center_spec = whole(width, width)
    lat_spec = whole(rows, rows + 2 * EDGE)
    tile = block(4, rows, LANES)
    field_bytes = rows * width * 2

    p_right, p_left = pl.pallas_call(
        pack_kernel,
        grid=(n_p,),
        in_specs=[block(GROUP, rows, width), grad_spec, select_spec],
        out_specs=[tile, tile],
        out_shape=[jax.ShapeDtypeStruct((4 * n_p, rows, LANES), bf)] * 2,
        compiler_params=params(),
        cost_estimate=cost(p_end, 1, p_end * field_bytes),
        name="pack_edges",
    )(ens, gradient, select)
    p_low, p_high = exchange(p_right, p_left, "lon", True)

    n_rows = total - p_end
    step = 2
    last = rows // EDGE - 1
    q_up, q_down = pl.pallas_call(
        lambda *refs: rows_kernel(p_end, *refs),
        grid=(n_rows // step,),
        in_specs=[
            pl.BlockSpec((step, EDGE, width), lambda b: (b + p_end // step, 0, 0)),
            pl.BlockSpec((step, EDGE, width), lambda b: (b + p_end // step, last, 0)),
            pl.BlockSpec((levels, EDGE, width), lambda b: (0, 0, 0)),
            pl.BlockSpec((levels, EDGE, width), lambda b: (0, last, 0)),
        ],
        out_specs=[block(step, EDGE, width)] * 2,
        out_shape=[jax.ShapeDtypeStruct((n_rows, EDGE, width), bf)] * 2,
        compiler_params=params(),
        cost_estimate=cost(0, 0, n_rows * field_bytes),
        name="edge_rows",
    )(ens, ens, gradient, gradient)
    q_low, q_high = exchange(q_up, q_down, "lat", False)

    halo = block(GROUP, EDGE, width)
    q_done, q_right, q_left = pl.pallas_call(
        lambda *refs: lat_pack_kernel(p_end, *refs),
        grid=(n_q,),
        in_specs=[block(GROUP, rows, width, n_p), grad_spec, halo, halo, lat_spec, select_spec],
        out_specs=[block(GROUP, rows, width), tile, tile],
        out_shape=[jax.ShapeDtypeStruct((GROUP * n_q, rows, width), bf)]
        + [jax.ShapeDtypeStruct((4 * n_q, rows, LANES), bf)] * 2,
        compiler_params=params(),
        cost_estimate=cost(GROUP * n_q, 3, GROUP * n_q * field_bytes * 2),
        name="lat_then_pack",
    )(ens, gradient, q_low, q_high, lat, select)
    q_in = exchange(q_right, q_left, "lon", True)

    shift = q_end // 4
    halo4 = pl.BlockSpec((4, EDGE, width), lambda b: (b, 0, 0))
    r_done, r_right, r_left = pl.pallas_call(
        lambda *refs: lat_pack4_kernel(q_end, *refs),
        grid=(rest,),
        in_specs=[
            block(4, rows, width, shift),
            grad_spec,
            halo4,
            halo4,
            lat_spec,
            whole(4, width, 2 * LANES),
        ],
        out_specs=[block(4, rows, width), block(1, rows, LANES), block(1, rows, LANES)],
        out_shape=[jax.ShapeDtypeStruct((4 * rest, rows, width), bf)]
        + [jax.ShapeDtypeStruct((rest, rows, LANES), bf)] * 2,
        compiler_params=params(),
        cost_estimate=cost(4 * rest, 3, 4 * rest * field_bytes * 2),
        name="lat_then_pack_rest",
    )(ens, gradient, q_low[GROUP * n_q :], q_high[GROUP * n_q :], lat, select4)
    r_in = exchange(r_right, r_left, "lon", True)

    p_done, p_up, p_down = pl.pallas_call(
        lon_kernel,
        grid=(n_p,),
        in_specs=[block(GROUP, rows, width), grad_spec, tile, tile, center_spec, spread_spec],
        out_specs=[block(GROUP, rows, width), halo, halo],
        out_shape=[jax.ShapeDtypeStruct((p_end, rows, width), bf)]
        + [jax.ShapeDtypeStruct((p_end, EDGE, width), bf)] * 2,
        compiler_params=params(),
        cost_estimate=cost(p_end, 2, p_end * field_bytes * 2),
        name="lon_sums",
    )(ens, gradient, p_low, p_high, center, spread)
    lat_low, lat_high = exchange(p_up, p_down, "lat", False)

    out_shape = jax.ShapeDtypeStruct((total, rows, width), bf)
    out = pl.pallas_call(
        lat_kernel,
        grid=(n_p,),
        in_specs=[block(GROUP, rows, width), halo, halo, lat_spec],
        out_specs=block(GROUP, rows, width),
        out_shape=out_shape,
        compiler_params=params(),
        cost_estimate=cost(p_end, 1, p_end * field_bytes * 2),
        name="lat_sums",
    )(p_done, lat_low, lat_high, lat)

    out = pl.pallas_call(
        last_kernel,
        grid=(n_q,),
        in_specs=[
            block(GROUP, rows, width),
            tile,
            tile,
            center_spec,
            spread_spec,
            pl.BlockSpec(memory_space=pl.ANY),
        ],
        out_specs=block(GROUP, rows, width, n_p),
        out_shape=out_shape,
        input_output_aliases={5: 0},
        compiler_params=params(),
        cost_estimate=cost(GROUP * n_q, 2, GROUP * n_q * field_bytes * 2),
        name="lon_sums_last",
    )(q_done, *q_in, center, spread, out)

    out = pl.pallas_call(
        last4_kernel,
        grid=(rest,),
        in_specs=[
            block(4, rows, width),
            block(1, rows, LANES),
            block(1, rows, LANES),
            center_spec,
            whole(4, 2 * LANES, width),
            pl.BlockSpec(memory_space=pl.ANY),
        ],
        out_specs=block(4, rows, width, shift),
        out_shape=out_shape,
        input_output_aliases={5: 0},
        compiler_params=params(),
        cost_estimate=cost(4 * rest, 2, 4 * rest * field_bytes * 2),
        name="lon_sums_rest",
    )(r_done, *r_in, center, spread4, out)
    return out.reshape(members, levels, rows, width)


def solution(mesh):
    placed = (P(None, None, "lat", "lon"), P(None, "lat", "lon"))
    return jax.shard_map(
        shards, mesh=mesh, in_specs=placed, out_specs=P(None, None, "lat", "lon"), check_vma=False
    )
```

time: 79.2 us -> 67.6 us (0.85)
  Pallas kernels: 0 us -> 27.6 us
  waiting for transfers between devices: 36 us -> 12.3 us
  local copies, waits for them, and re-layouts: 15.4 us -> 0.97 us
  starting transfers between devices: 10.9 us -> 25.3 us
  matrix products: 10.4 us -> 0 us
  other arithmetic: 4.6 us -> 0 us
    pallas_call x0 -> x8, Pallas kernels: none -> 27.6 us  [the longest x1 9.97 us: shards(): pl.pallas_call(lambda *refs: rows_kernel(p_end, *refs), grid=(n_rows // s...]
    ppermute x4 -> x10, waiting for transfers between devices: 36 us -> 12.3 us  [exchange(): return (lax.ppermute(up, axis, forward), lax.ppermute(down, axis, backward))]
    ppermute x4 -> x10, starting transfers between devices: 10.9 us -> 25.3 us  [exchange(): return (lax.ppermute(up, axis, forward), lax.ppermute(down, axis, backward))]
    dot_general x2 -> x0, matrix products: 10.4 us -> none  [the longest x1 5.23 us: shards(): jnp.einsum('mlap,pq->mlaq', widened, lon_kernel, preferred_element_type=j...]
    unnamed x3 -> x14, local copies, waits for them, and re-layouts: 10.3 us -> 0.94 us
    convert_element_type x1 -> x0, other arithmetic: 3.98 us -> none  [shards(): (ensemble.astype(jnp.float32) * gradient.astype(jnp.float32)[None]).astyp...]
    slice x6 -> x2, local copies, waits for them, and re-layouts: 3.25 us -> 0.03 us  [the longest x1 0.01 us: shards(): q_high[GROUP * n_q:]]
    convert_element_type x1 -> x0, local copies, waits for them, and re-layouts: 1 us -> none  [shards(): gradient.astype(jnp.float32)[None]]
  transfers between devices with their start and end apart: 4 -> 10, of which waited for: 4 -> 4; matrix products, arithmetic and copies ran while one was open for 3% -> 0% of each run, Pallas kernels for 0% -> 24%
where the time goes in v1:
time: 67.6 us; the launch traced here: 66.4 us
  Pallas kernels  27.6 us (41%)
  starting transfers between devices  25.3 us (37%)
  waiting for transfers between devices  12.3 us (18%)
  local copies, waits for them, and re-layouts  0.97 us (1%)
    ppermute x10, starting transfers between devices, exchange(): return (lax.ppermute(up, axis, forward), lax.ppermute(down, axis, backward))  25.3 us
    ppermute x10, waiting for transfers between devices, exchange(): return (lax.ppermute(up, axis, forward), lax.ppermute(down, axis, backward))  12.3 us
    pallas_call x1, Pallas kernels, shards(): pl.pallas_call(lambda *refs: rows_kernel(p_end, *refs), grid=(n_rows // s...  9.97 us
    pallas_call x1, Pallas kernels, shards(): pl.pallas_call(lambda *refs: lat_pack_kernel(p_end, *refs), grid=(n_q,),...  3.16 us
    pallas_call x1, Pallas kernels, shards(): pl.pallas_call(lon_kernel, grid=(n_p,), in_specs=[block(GROUP, rows, widt...  2.9 us
    pallas_call x1, Pallas kernels, shards(): pl.pallas_call(lambda *refs: lat_pack4_kernel(q_end, *refs), grid=(rest,)...  2.69 us
    pallas_call x1, Pallas kernels, shards(): pl.pallas_call(last_kernel, grid=(n_q,), in_specs=[block(GROUP, rows, wid...  2.62 us
    pallas_call x1, Pallas kernels, shards(): pl.pallas_call(pack_kernel, grid=(n_p,), in_specs=[block(GROUP, rows, wid...  2.32 us
  transfers between devices with their start and end apart: 10, of which 4 were waited for; matrix products, arithmetic and copies ran while one was open for 0% of the time, Pallas kernels for 24%

profile of v1, /device:TPU:1, one launch (start us, length us, event | category | flops | bytes accessed | tf_op | source)
XLA Modules:
  0.0 66.4 jit_solution(11664640288431218864)
XLA Ops:
  0.0 0.9 %copy-done = bf16[2,128,256]{2,1,0:T(8,128)(2,1)S(1)} copy-done((bf16[2,128,256]{2,1,0:T(8,128)(2,1)S(1)}, bf16[2,128,256]{2,1,0:T(8,128)(2,1)}, u32[]{:S(2)}) %copy-start) | copy-done | bytes 131096
  0.9 10.0 %edge_rows.1 = (bf16[46,32,256]{2,1,0:T(8,128)(2,1)S(1)}, bf16[46,32,256]{2,1,0:T(8,128)(2,1)S(1)}) custom-call(bf16[80,128,256]{2,1,0:T(8,128)(2,1)} %bitcast.2, bf16[80,128,256]{2,1,0:T(8,128)(2,1)} %bitcast.3, bf16[2,128,256]{2,1,0:T(8,128)(2,1)S(1)} %copy-done, bf16[2,128,256]{2,1,0:T(8,128)(2,1)S(1)} %copy-done), custom_call_target="tpu_custom_call" | custom-call | bytes 3014656 | tf_op jit(solution)/shard_map/edge_rows/pallas_call | solution.py:237
  10.9 0.0 copy-start.1
  10.9 4.7 %collective-permute-start = (bf16[46,32,256]{2,1,0:T(8,128)(2,1)S(1)}, bf16[46,32,256]{2,1,0:T(8,128)(2,1)S(1)}, u32[]{:S(2)}, u32[]{:S(2)}) collective-permute-start(bf16[46,32,256]{2,1,0:T(8,128)(2,1)S(1)} %get-tuple-element.18), channel_id=1, source_target_pairs={{0,1},{1,2},{2,3},{4,5},{5,6},{6,7},{8,9},{9,10},{10,11},{12,13},{... | collective-permute-start | bytes 2261000 | tf_op jit(solution)/shard_map/ppermute | solution.py:179
  15.6 2.1 %collective-permute-start.1 = (bf16[46,32,256]{2,1,0:T(8,128)(2,1)S(1)}, bf16[46,32,256]{2,1,0:T(8,128)(2,1)S(1)}, u32[]{:S(2)}, u32[]{:S(2)}) collective-permute-start(bf16[46,32,256]{2,1,0:T(8,128)(2,1)S(1)} %get-tuple-element.19), channel_id=1, source_target_pairs={{1,0},{2,1},{3,2},{5,4},{6,5},{7,6},{9,8},{10,9},{11,10},{13,12},{... | collective-permute-start | bytes 2261000 | tf_op jit(solution)/shard_map/ppermute | solution.py:179
  17.7 2.3 %pack_edges.1 = (bf16[8,128,128]{2,1,0:T(8,128)(2,1)S(1)}, bf16[8,128,128]{2,1,0:T(8,128)(2,1)S(1)}) custom-call(bf16[80,128,256]{2,1,0:T(8,128)(2,1)} %bitcast.4, bf16[2,128,256]{2,1,0:T(8,128)(2,1)S(1)} %copy-done, bf16[8,256,256]{2,1,0:T(8,128)(2,1)S(1)} %copy-done.2), custom_call_target="tpu_custom_call" | custom-call | flops 570425344 | bytes 2228224 | tf_op jit(solution)/shard_map/pack_edges/pallas_call | solution.py:222
  20.0 1.3 %collective-permute-start.6 = (bf16[8,128,128]{2,1,0:T(8,128)(2,1)S(1)}, bf16[8,128,128]{2,1,0:T(8,128)(2,1)S(1)}, u32[]{:S(2)}, u32[]{:S(2)}) collective-permute-start(bf16[8,128,128]{2,1,0:T(8,128)(2,1)S(1)} %get-tuple-element.26), channel_id=1, source_target_pairs={{0,4},{4,8},{8,12},{12,16},{16,20},{20,24},{24,28},{28,0},{1,5},{5... | collective-permute-start | bytes 786440 | tf_op jit(solution)/shard_map/ppermute | solution.py:179
  21.3 3.1 %collective-permute-start.7 = (bf16[8,128,128]{2,1,0:T(8,128)(2,1)S(1)}, bf16[8,128,128]{2,1,0:T(8,128)(2,1)S(1)}, u32[]{:S(2)}, u32[]{:S(2)}) collective-permute-start(bf16[8,128,128]{2,1,0:T(8,128)(2,1)S(1)} %get-tuple-element.27), channel_id=1, source_target_pairs={{4,0},{8,4},{12,8},{16,12},{20,16},{24,20},{28,24},{0,28},{5,1},{9... | collective-permute-start | bytes 786440 | tf_op jit(solution)/shard_map/ppermute | solution.py:179
  24.4 7.2 %collective-permute-done.6.low_ref = bf16[8,128,128]{2,1,0:T(8,128)(2,1)S(1)} collective-permute-done((bf16[8,128,128]{2,1,0:T(8,128)(2,1)S(1)}, bf16[8,128,128]{2,1,0:T(8,128)(2,1)S(1)}, u32[]{:S(2)}, u32[]{:S(2)}) %collective-permute-start.6) | collective-permute-done | bytes 262176 | tf_op jit(solution)/shard_map/ppermute | solution.py:179
  31.6 2.2 %collective-permute-done.7.high_ref = bf16[8,128,128]{2,1,0:T(8,128)(2,1)S(1)} collective-permute-done((bf16[8,128,128]{2,1,0:T(8,128)(2,1)S(1)}, bf16[8,128,128]{2,1,0:T(8,128)(2,1)S(1)}, u32[]{:S(2)}, u32[]{:S(2)}) %collective-permute-start.7) | collective-permute-done | bytes 262176 | tf_op jit(solution)/shard_map/ppermute | solution.py:179
  33.8 2.9 %lon_sums.1 = (bf16[34,128,256]{2,1,0:T(8,128)(2,1)S(1)}, bf16[34,32,256]{2,1,0:T(8,128)(2,1)S(1)}, bf16[34,32,256]{2,1,0:T(8,128)(2,1)S(1)}) custom-call(bf16[80,128,256]{2,1,0:T(8,128)(2,1)} %bitcast.5, bf16[2,128,256]{2,1,0:T(8,128)(2,1)S(1)} %copy-done, bf16[8,128,128]{2,1,0:T(8,128)(2,1)S(1)} %collective-permute-done.6.low_ref, ...), custom_call_target="tpu_custom_call" | custom-call | flops 1140850688 | bytes 4456448 | tf_op jit(solution)/shard_map/lon_sums/pallas_call | solution.py:290
  36.7 3.9 %collective-permute-start.8 = (bf16[34,32,256]{2,1,0:T(8,128)(2,1)S(1)}, bf16[34,32,256]{2,1,0:T(8,128)(2,1)S(1)}, u32[]{:S(2)}, u32[]{:S(2)}) collective-permute-start(bf16[34,32,256]{2,1,0:T(8,128)(2,1)S(1)} %get-tuple-element.29), channel_id=1, source_target_pairs={{0,1},{1,2},{2,3},{4,5},{5,6},{6,7},{8,9},{9,10},{10,11},{12,13},{... | collective-permute-start | bytes 1671176 | tf_op jit(solution)/shard_map/ppermute | solution.py:179
  40.6 1.9 %collective-permute-start.9 = (bf16[34,32,256]{2,1,0:T(8,128)(2,1)S(1)}, bf16[34,32,256]{2,1,0:T(8,128)(2,1)S(1)}, u32[]{:S(2)}, u32[]{:S(2)}) collective-permute-start(bf16[34,32,256]{2,1,0:T(8,128)(2,1)S(1)} %get-tuple-element.30), channel_id=1, source_target_pairs={{1,0},{2,1},{3,2},{5,4},{6,5},{7,6},{9,8},{10,9},{11,10},{13,12},{... | collective-permute-start | bytes 1671176 | tf_op jit(solution)/shard_map/ppermute | solution.py:179
  42.6 3.2 %lat_then_pack.1 = (bf16[34,128,256]{2,1,0:T(8,128)(2,1)S(1)}, bf16[8,128,128]{2,1,0:T(8,128)(2,1)S(1)}, bf16[8,128,128]{2,1,0:T(8,128)(2,1)S(1)}) custom-call(bf16[80,128,256]{2,1,0:T(8,128)(2,1)} %bitcast.6, bf16[2,128,256]{2,1,0:T(8,128)(2,1)S(1)} %copy-done, bf16[46,32,256]{2,1,0:T(8,128)(2,1)S(1)} %collective-permute-done.refs_2_, ...), custom_call_target="tpu_custom_call" | custom-call | flops 1711276032 | bytes 4456448 | tf_op jit(solution)/shard_map/lat_then_pack/pallas_call | solution.py:255
  45.8 0.1 collective-permute-start.4
  45.8 4.1 %collective-permute-start.5 = (bf16[8,128,128]{2,1,0:T(8,128)(2,1)S(1)}, bf16[8,128,128]{2,1,0:T(8,128)(2,1)S(1)}, u32[]{:S(2)}, u32[]{:S(2)}) collective-permute-start(bf16[8,128,128]{2,1,0:T(8,128)(2,1)S(1)} %get-tuple-element.25), channel_id=1, source_target_pairs={{4,0},{8,4},{12,8},{16,12},{20,16},{24,20},{28,24},{0,28},{5,1},{9... | collective-permute-start | bytes 786440 | tf_op jit(solution)/shard_map/ppermute | solution.py:179
  50.0 2.7 %lat_then_pack_rest.1 = (bf16[12,128,256]{2,1,0:T(8,128)(2,1)S(1)}, bf16[3,128,128]{2,1,0:T(8,128)(2,1)S(1)}, bf16[3,128,128]{2,1,0:T(8,128)(2,1)S(1)}) custom-call(bf16[80,128,256]{2,1,0:T(8,128)(2,1)} %bitcast.7, bf16[2,128,256]{2,1,0:T(8,128)(2,1)S(1)} %copy-done, bf16[12,32,256]{2,1,0:T(8,128)(2,1)S(1)} %slice.16.refs_2_, ...), custom_call_target="tpu_custom_call" | custom-call | flops 603979776 | bytes 1572864 | tf_op jit(solution)/shard_map/lat_then_pack_rest/pallas_call | solution.py:270
  52.7 0.1 collective-permute-start.2
  52.8 4.1 %collective-permute-start.3 = (bf16[3,128,128]{2,1,0:T(8,128)(2,1)S(1)}, bf16[3,128,128]{2,1,0:T(8,128)(2,1)S(1)}, u32[]{:S(2)}, u32[]{:S(2)}) collective-permute-start(bf16[3,128,128]{2,1,0:T(8,128)(2,1)S(1)} %get-tuple-element.22), channel_id=1, source_target_pairs={{4,0},{8,4},{12,8},{16,12},{20,16},{24,20},{28,24},{0,28},{5,1},{9... | collective-permute-start | bytes 294920 | tf_op jit(solution)/shard_map/ppermute | solution.py:179
  56.9 1.9 %lat_sums.1.whole_ref = bf16[80,128,256]{2,1,0:T(8,128)(2,1)} custom-call(bf16[34,128,256]{2,1,0:T(8,128)(2,1)S(1)} %get-tuple-element.28.done_ref, bf16[34,32,256]{2,1,0:T(8,128)(2,1)S(1)} %collective-permute-done.8.low_ref, bf16[34,32,256]{2,1,0:T(8,128)(2,1)S(1)} %collective-permute-done.9.high_ref, bf16[128,192]{1,0:T(8,128)(2,1)S(1)} %copy-done.4), custom_call_target="tpu_custom_call" | custom-call | flops 570425344 | bytes 4456448 | tf_op jit(solution)/shard_map/lat_sums/pallas_call | solution.py:304
  58.8 0.1 collective-permute-done.4.low_ref
  59.0 2.8 %collective-permute-done.5.high_ref = bf16[8,128,128]{2,1,0:T(8,128)(2,1)S(1)} collective-permute-done((bf16[8,128,128]{2,1,0:T(8,128)(2,1)S(1)}, bf16[8,128,128]{2,1,0:T(8,128)(2,1)S(1)}, u32[]{:S(2)}, u32[]{:S(2)}) %collective-permute-start.5) | collective-permute-done | bytes 262176 | tf_op jit(solution)/shard_map/ppermute | solution.py:179
  61.7 2.6 %lon_sums_last.1.whole_ref = bf16[80,128,256]{2,1,0:T(8,128)(2,1)} custom-call(bf16[34,128,256]{2,1,0:T(8,128)(2,1)S(1)} %get-tuple-element.23.done_ref, bf16[8,128,128]{2,1,0:T(8,128)(2,1)S(1)} %collective-permute-done.4.low_ref, bf16[8,128,128]{2,1,0:T(8,128)(2,1)S(1)} %collective-permute-done.5.high_ref, ...), custom_call_target="tpu_custom_call", output_to_operand_aliasing={{}: (5, {})} | custom-call | flops 1140850688 | bytes 4456448 | tf_op jit(solution)/shard_map/lon_sums_last/pallas_call | solution.py:315
  64.4 2.0 %lon_sums_rest.1 = bf16[80,128,256]{2,1,0:T(8,128)(2,1)} custom-call(bf16[12,128,256]{2,1,0:T(8,128)(2,1)S(1)} %get-tuple-element.20.done_ref, bf16[3,128,128]{2,1,0:T(8,128)(2,1)S(1)} %collective-permute-done.2.low_ref, bf16[3,128,128]{2,1,0:T(8,128)(2,1)S(1)} %collective-permute-done.3.high_ref, ...), custom_call_target="tpu_custom_call", output_to_operand_aliasing={{}: (5, {})} | custom-call | flops 402653184 | bytes 1572864 | tf_op jit(solution)/shard_map/lon_sums_rest/pallas_call | solution.py:334
  (20 shorter events, 0.1 us)
Async XLA Ops:
  0.0 0.9 %copy-start = (bf16[2,128,256]{2,1,0:T(8,128)(2,1)S(1)}, bf16[2,128,256]{2,1,0:T(8,128)(2,1)}, u32[]{:S(2)}) copy-start(bf16[2,128,256]{2,1,0:T(8,128)(2,1)} %grad_ref.3) | copy-start | bytes 393220
  0.9 16.8 %copy-start.2 = (bf16[8,256,256]{2,1,0:T(8,128)(2,1)S(1)}, bf16[8,256,256]{2,1,0:T(8,128)(2,1)}, u32[]{:S(2)}) copy-start(bf16[8,256,256]{2,1,0:T(8,128)(2,1)} %constant.8.clone.refs_5_.select_ref) | copy-start | bytes 3145732
  10.9 22.9 %copy-start.1 = (bf16[8,256,256]{2,1,0:T(8,128)(2,1)S(1)}, bf16[8,256,256]{2,1,0:T(8,128)(2,1)}, u32[]{:S(2)}) copy-start(bf16[8,256,256]{2,1,0:T(8,128)(2,1)} %constant.9.clone.spread_ref) | copy-start | bytes 3145732
  10.9 22.9 %copy-start.3 = (bf16[256,256]{1,0:T(8,128)(2,1)S(1)}, bf16[256,256]{1,0:T(8,128)(2,1)}, u32[]{:S(2)}) copy-start(bf16[256,256]{1,0:T(8,128)(2,1)} %constant.10.clone.center_ref) | copy-start | bytes 393220
  10.9 31.6 %collective-permute-start = (bf16[46,32,256]{2,1,0:T(8,128)(2,1)S(1)}, bf16[46,32,256]{2,1,0:T(8,128)(2,1)S(1)}, u32[]{:S(2)}, u32[]{:S(2)}) collective-permute-start(bf16[46,32,256]{2,1,0:T(8,128)(2,1)S(1)} %get-tuple-element.18), channel_id=1, source_target_pairs={{0,1},{1,2},{2,3},{4,5},{5,6},{6,7},{8,9},{9,10},{10,11},{12,13},{... | collective-permute-start | bytes 2261000 | tf_op jit(solution)/shard_map/ppermute | solution.py:179
  15.6 27.0 %copy-start.4 = (bf16[128,192]{1,0:T(8,128)(2,1)S(1)}, bf16[128,192]{1,0:T(8,128)(2,1)}, u32[]{:S(2)}) copy-start(bf16[128,192]{1,0:T(8,128)(2,1)} %constant.11.clone.refs_4_.lat_ref) | copy-start | bytes 147460
  15.6 27.0 %collective-permute-start.1 = (bf16[46,32,256]{2,1,0:T(8,128)(2,1)S(1)}, bf16[46,32,256]{2,1,0:T(8,128)(2,1)S(1)}, u32[]{:S(2)}, u32[]{:S(2)}) collective-permute-start(bf16[46,32,256]{2,1,0:T(8,128)(2,1)S(1)} %get-tuple-element.19), channel_id=1, source_target_pairs={{1,0},{2,1},{3,2},{5,4},{6,5},{7,6},{9,8},{10,9},{11,10},{13,12},{... | collective-permute-start | bytes 2261000 | tf_op jit(solution)/shard_map/ppermute | solution.py:179
  20.0 11.6 %collective-permute-start.6 = (bf16[8,128,128]{2,1,0:T(8,128)(2,1)S(1)}, bf16[8,128,128]{2,1,0:T(8,128)(2,1)S(1)}, u32[]{:S(2)}, u32[]{:S(2)}) collective-permute-start(bf16[8,128,128]{2,1,0:T(8,128)(2,1)S(1)} %get-tuple-element.26), channel_id=1, source_target_pairs={{0,4},{4,8},{8,12},{12,16},{16,20},{20,24},{24,28},{28,0},{1,5},{5... | collective-permute-start | bytes 786440 | tf_op jit(solution)/shard_map/ppermute | solution.py:179
  21.3 12.5 %collective-permute-start.7 = (bf16[8,128,128]{2,1,0:T(8,128)(2,1)S(1)}, bf16[8,128,128]{2,1,0:T(8,128)(2,1)S(1)}, u32[]{:S(2)}, u32[]{:S(2)}) collective-permute-start(bf16[8,128,128]{2,1,0:T(8,128)(2,1)S(1)} %get-tuple-element.27), channel_id=1, source_target_pairs={{4,0},{8,4},{12,8},{16,12},{20,16},{24,20},{28,24},{0,28},{5,1},{9... | collective-permute-start | bytes 786440 | tf_op jit(solution)/shard_map/ppermute | solution.py:179
  36.7 13.3 %copy-start.6 = (bf16[4,256,256]{2,1,0:T(8,128)(2,1)S(1)}, bf16[4,256,256]{2,1,0:T(8,128)(2,1)}, u32[]{:S(2)}) copy-start(bf16[4,256,256]{2,1,0:T(8,128)(2,1)} %constant.12.refs_5_) | copy-start | bytes 1572868
  36.7 16.1 %collective-permute-start.8 = (bf16[34,32,256]{2,1,0:T(8,128)(2,1)S(1)}, bf16[34,32,256]{2,1,0:T(8,128)(2,1)S(1)}, u32[]{:S(2)}, u32[]{:S(2)}) collective-permute-start(bf16[34,32,256]{2,1,0:T(8,128)(2,1)S(1)} %get-tuple-element.29), channel_id=1, source_target_pairs={{0,1},{1,2},{2,3},{4,5},{5,6},{6,7},{8,9},{9,10},{10,11},{12,13},{... | collective-permute-start | bytes 1671176 | tf_op jit(solution)/shard_map/ppermute | solution.py:179
  40.6 16.3 %collective-permute-start.9 = (bf16[34,32,256]{2,1,0:T(8,128)(2,1)S(1)}, bf16[34,32,256]{2,1,0:T(8,128)(2,1)S(1)}, u32[]{:S(2)}, u32[]{:S(2)}) collective-permute-start(bf16[34,32,256]{2,1,0:T(8,128)(2,1)S(1)} %get-tuple-element.30), channel_id=1, source_target_pairs={{1,0},{2,1},{3,2},{5,4},{6,5},{7,6},{9,8},{10,9},{11,10},{13,12},{... | collective-permute-start | bytes 1671176 | tf_op jit(solution)/shard_map/ppermute | solution.py:179
  45.8 13.2 %collective-permute-start.4 = (bf16[8,128,128]{2,1,0:T(8,128)(2,1)S(1)}, bf16[8,128,128]{2,1,0:T(8,128)(2,1)S(1)}, u32[]{:S(2)}, u32[]{:S(2)}) collective-permute-start(bf16[8,128,128]{2,1,0:T(8,128)(2,1)S(1)} %get-tuple-element.24), channel_id=1, source_target_pairs={{0,4},{4,8},{8,12},{12,16},{16,20},{20,24},{24,28},{28,0},{1,5},{5... | collective-permute-start | bytes 786440 | tf_op jit(solution)/shard_map/ppermute | solution.py:179
  45.8 15.9 %collective-permute-start.5 = (bf16[8,128,128]{2,1,0:T(8,128)(2,1)S(1)}, bf16[8,128,128]{2,1,0:T(8,128)(2,1)S(1)}, u32[]{:S(2)}, u32[]{:S(2)}) collective-permute-start(bf16[8,128,128]{2,1,0:T(8,128)(2,1)S(1)} %get-tuple-element.25), channel_id=1, source_target_pairs={{4,0},{8,4},{12,8},{16,12},{20,16},{24,20},{28,24},{0,28},{5,1},{9... | collective-permute-start | bytes 786440 | tf_op jit(solution)/shard_map/ppermute | solution.py:179
  52.7 11.6 %collective-permute-start.2 = (bf16[3,128,128]{2,1,0:T(8,128)(2,1)S(1)}, bf16[3,128,128]{2,1,0:T(8,128)(2,1)S(1)}, u32[]{:S(2)}, u32[]{:S(2)}) collective-permute-start(bf16[3,128,128]{2,1,0:T(8,128)(2,1)S(1)} %get-tuple-element.21), channel_id=1, source_target_pairs={{0,4},{4,8},{8,12},{12,16},{16,20},{20,24},{24,28},{28,0},{1,5},{5... | collective-permute-start | bytes 294920 | tf_op jit(solution)/shard_map/ppermute | solution.py:179
  52.8 11.6 %collective-permute-start.3 = (bf16[3,128,128]{2,1,0:T(8,128)(2,1)S(1)}, bf16[3,128,128]{2,1,0:T(8,128)(2,1)S(1)}, u32[]{:S(2)}, u32[]{:S(2)}) collective-permute-start(bf16[3,128,128]{2,1,0:T(8,128)(2,1)S(1)} %get-tuple-element.22), channel_id=1, source_target_pairs={{4,0},{8,4},{12,8},{16,12},{20,16},{24,20},{28,24},{0,28},{5,1},{9... | collective-permute-start | bytes 294920 | tf_op jit(solution)/shard_map/ppermute | solution.py:179
  61.7 2.6 %copy-start.5 = (bf16[4,256,256]{2,1,0:T(8,128)(2,1)S(1)}, bf16[4,256,256]{2,1,0:T(8,128)(2,1)}, u32[]{:S(2)}) copy-start(bf16[4,256,256]{2,1,0:T(8,128)(2,1)} %constant.13.spread_ref) | copy-start | bytes 1572868

commit v2 on v0

v2 whole, which is shorter than its diff:
```python
import functools

import jax
import jax.numpy as jnp
import numpy as np
from jax import lax
from jax.experimental import pallas as pl
from jax.experimental.pallas import tpu as pltpu
from jax.sharding import PartitionSpec as P

HALF = 30
LANES = 128
EDGE = 32
GROUP = 17
VMEM_LIMIT = 16 * 1024 * 1024
FIRST = 42
HEAVY = 200_000_000_000
BF = jnp.bfloat16


def taps():
    offsets = np.arange(-HALF, HALF + 1).astype(np.float32)
    spread = np.float32(HALF)
    norm = np.sqrt(np.sum(np.exp(-offsets * offsets / (spread * spread)), dtype=np.float32))
    return (np.exp(-offsets * offsets / (2 * spread * spread)) / norm).astype(BF)


def band(block_len, margin):
    k = taps()
    out = np.zeros((block_len + 2 * margin, block_len), BF)
    for q in range(block_len):
        out[q + margin - HALF : q + margin + HALF + 1, q] = k
    return out


def lon_weights(width):
    lon = band(width, HALF)
    spread = np.zeros((8, 2 * LANES, width), BF)
    for s in range(8):
        for j in range(HALF):
            lane = HALF * s + j if s < 4 else 120 + j - 8 * (s - 4)
            if s >= 4 and not 120 <= lane < 128:
                continue
            spread[s, lane] = lon[j]
            spread[s, LANES + lane] = lon[width + HALF + j]
    return lon[HALF : HALF + width].copy(), spread


def odd(axis):
    return lax.rem(lax.axis_index(axis), 2)


def fill_select(select_ref):
    width = select_ref.shape[1]
    side = odd("lon")
    row = lax.broadcasted_iota(jnp.int32, (width, 2 * LANES), 0)
    col = lax.broadcasted_iota(jnp.int32, (width, 2 * LANES), 1)
    diff = row - col
    end_tile, start_tile = side * LANES, (1 - side) * LANES
    for s in range(8):
        shift, lo, hi = (-HALF * s, HALF * s, HALF * s + HALF) if s < 4 else (8 * (s - 4) - 120, 120, 128)
        end = (diff == width - HALF + shift - end_tile) & (col >= end_tile + lo) & (col < end_tile + hi)
        start = (diff == shift - start_tile) & (col >= start_tile + lo) & (col < start_tile + hi) & (row < HALF)
        select_ref[s] = jnp.where(end | start, 1.0, 0.0).astype(BF)


def dot(a, b):
    return jnp.dot(a, b, preferred_element_type=jnp.float32)


def units(count):
    out, first = [], 0
    while count - first >= GROUP:
        out.append((first, 4, True))
        first += GROUP
    if count > first:
        out.append((first, (count - first) // 4, False))
    return out


def tiles_of(count):
    return sum(t for _, t, _ in units(count))


def stack(ref, first, count):
    return ref[first : first + count].reshape(count * ref.shape[1], ref.shape[2])


def pack(src_ref, unit, select_ref):
    first, n, extra = unit
    rows = src_ref.shape[1]
    acc = None
    for s in range(4):
        part = dot(stack(src_ref, first + s * n, n), select_ref[s])
        acc = part if acc is None else acc + part
    if extra:
        field = src_ref[first + 4 * n]
        acc += jnp.concatenate([dot(field, select_ref[4 + t]) for t in range(n)], axis=0)
    return acc.astype(BF).reshape(n, rows, 2 * LANES)


def multiply(raw_ref, number, gvm_ref, prod_ref):
    for f in range(prod_ref.shape[0]):
        grad = gvm_ref[(number + f) % gvm_ref.shape[0]].astype(jnp.float32)
        prod_ref[f] = (raw_ref[f].astype(jnp.float32) * grad).astype(BF)


def packed_units(src_ref, select_ref):
    tile = 0
    for unit in units(src_ref.shape[0]):
        yield pl.ds(tile, unit[1]), pack(src_ref, unit, select_ref)
        tile += unit[1]


def first_kernel(ens_ref, grad_ref, a_ref, b_ref, prod_ref, select_ref, gvm_ref, buf, sems):
    count = prod_ref.shape[0]
    copies = [
        pltpu.make_async_copy(grad_ref, gvm_ref, sems.at[0]),
        pltpu.make_async_copy(ens_ref.at[pl.ds(0, count)], buf, sems.at[1]),
    ]
    for c in copies:
        c.start()
    fill_select(select_ref)
    for c in copies:
        c.wait()
    multiply(buf, 0, gvm_ref, prod_ref)
    for at, tiles in packed_units(prod_ref, select_ref):
        a_ref[at] = tiles[:, :, :LANES]
        b_ref[at] = tiles[:, :, LANES:]


def edge_rows(ref, rows):
    side = odd("lat")
    head, tail = 0, rows - EDGE
    return (
        pl.ds(pl.multiple_of((1 - side) * tail, EDGE), EDGE),
        pl.ds(pl.multiple_of(side * tail, EDGE), EDGE),
    )


def second_kernel(
    before, ens_ref, gvm_ref, select_ref, b_first_ref, prod_ref, a_ref, b_ref, near_ref, far_ref, buf, sem
):
    count, rows = prod_ref.shape[:2]
    copy = pltpu.make_async_copy(ens_ref.at[pl.ds(before, count)], buf, sem)
    copy.start()
    copy.wait()
    multiply(buf, before, gvm_ref, prod_ref)
    for at, tiles in packed_units(prod_ref, select_ref):
        a_ref[at] = tiles[:, :, :LANES]
        b_ref[at] = tiles[:, :, LANES:]
    near, far = edge_rows(b_ref, rows)
    start = 0
    for ref in (b_first_ref, b_ref):
        to = pl.ds(start, ref.shape[0])
        near_ref[to] = ref[:, near]
        far_ref[to] = ref[:, far]
        start += ref.shape[0]


def pair(ref, t):
    if t + 1 < ref.shape[0]:
        return jnp.concatenate([ref[t], ref[t + 1]], axis=1)
    return ref[t]


def lat_field(field, near, far, lat):
    return dot(lat, jnp.concatenate([near, field, far], axis=0))


def lat_tiles(refs, near_ref, far_ref, lat, emit):
    start = 0
    for ref in refs:
        for t in range(0, ref.shape[0], 2):
            n = min(2, ref.shape[0] - t)
            wide = [jnp.concatenate([r[start + t + i] for i in range(n)], axis=1) for r in (near_ref, far_ref)]
            done = lat_field(pair(ref, t), *wide, lat).astype(BF)
            for i in range(n):
                emit(start + t + i, done[:, i * LANES : (i + 1) * LANES])
        start += ref.shape[0]


def edge_lat_kernel(one_ref, two_ref, near_ref, far_ref, lat_ref, out_ref):
    def emit(t, v):
        out_ref[t] = v

    lat_tiles((one_ref, two_ref), near_ref, far_ref, lat_ref[odd("lat")], emit)


def own_kernel(one_ref, two_ref, center_ref, own_ref, near_ref, far_ref):
    rows, width = own_ref.shape[1:]
    start = 0
    for prod_ref in (one_ref, two_ref):
        count = prod_ref.shape[0]
        for first in range(0, count, 4):
            n = min(4, count - first)
            v = dot(stack(prod_ref, first, n), center_ref[...]).astype(BF).reshape(n, rows, width)
            own_ref[pl.ds(start + first, n)] = v
        start += count
    near, far = edge_rows(own_ref, rows)
    near_ref[...] = own_ref[:, near]
    far_ref[...] = own_ref[:, far]


def tile_rows_kernel(one_ref, two_ref, near_ref, far_ref):
    near, far = edge_rows(one_ref, one_ref.shape[1])
    start = 0
    for ref in (one_ref, two_ref):
        to = pl.ds(start, ref.shape[0])
        near_ref[to] = ref[:, near]
        far_ref[to] = ref[:, far]
        start += ref.shape[0]


def spread_rows(first):
    side = odd("lon") if first else 1 - odd("lon")
    return pl.ds(pl.multiple_of((1 - side) * LANES, LANES), LANES)


def partial_kernel(
    counts, own_ref, near_ref, far_ref, one_ref, two_ref, tnear_ref, tfar_ref, lat_ref, spread_ref, acc_ref, done
):
    lat = lat_ref[odd("lat")]
    rows, width = own_ref.shape[1:]
    at = spread_rows(True)

    def emit(t, v):
        done[t] = v

    lat_tiles((one_ref, two_ref), tnear_ref, tfar_ref, lat, emit)

    def own(first, n):
        return jnp.concatenate(
            [lat_field(own_ref[f], near_ref[f], far_ref[f], lat) for f in range(first, first + n)], axis=0
        )

    for first, n, extra, tile in all_units(counts):
        edges = stack(done, tile, n)
        for s in range(4):
            v = own(first + s * n, n) + dot(edges, spread_ref[s, at])
            acc_ref[pl.ds(first + s * n, n)] = v.reshape(n, rows, width)
        if extra:
            v = own(first + 4 * n, 1)
            for t in range(n):
                v += dot(done[tile + t], spread_ref[4 + t, at])
            acc_ref[first + 4 * n] = v


def last_kernel(counts, acc_ref, tiles_ref, spread_ref, out_ref, buf, sems):
    rows, width = acc_ref.shape[1:]
    at = spread_rows(False)
    copies = []
    for first, n, extra, tile in all_units(counts):
        edges = stack(tiles_ref, tile, n)
        for s in range(4):
            to = pl.ds(first + s * n, n)
            buf[to] = (acc_ref[to] + dot(edges, spread_ref[s, at]).reshape(n, rows, width)).astype(BF)
        if extra:
            v = acc_ref[first + 4 * n]
            for t in range(n):
                v += dot(tiles_ref[tile + t], spread_ref[4 + t, at])
            buf[first + 4 * n] = v.astype(BF)
        to = pl.ds(first, 4 * n + extra)
        copies.append(pltpu.make_async_copy(buf.at[to], out_ref.at[to], sems.at[len(copies)]))
        copies[-1].start()
    for c in copies:
        c.wait()


def all_units(counts):
    out, start, tile = [], 0, 0
    for count in counts:
        for first, n, extra in units(count):
            out.append((start + first, n, extra, tile))
            tile += n
        start += count
    return out


def first_partner(x, axis):
    return lax.ppermute(x, axis, [(i, i ^ 1) for i in range(lax.axis_size(axis))])


def second_partner(x, axis, periodic):
    count = lax.axis_size(axis)
    pairs = []
    for i in range(count):
        j = i + 1 if i % 2 else i - 1
        if periodic or 0 <= j < count:
            pairs.append((i, j % count))
    return lax.ppermute(x, axis, pairs)


def lat_exchange(near, far):
    return first_partner(near, "lat"), second_partner(far, "lat", False)


IN_VMEM = pl.BlockSpec(memory_space=pltpu.VMEM)
ANYWHERE = pl.BlockSpec(memory_space=pl.ANY)


def vm(x):
    return pltpu.with_memory_space_constraint(x, pltpu.VMEM)


def hbm(x):
    return pltpu.with_memory_space_constraint(x, pltpu.HBM)


def call(kernel, name, args, outs, scratch=(), specs=None, out_specs=None, aliases=None, weight=0):
    return pl.pallas_call(
        kernel,
        in_specs=specs or [IN_VMEM] * len(args),
        out_specs=out_specs or [IN_VMEM] * len(outs),
        out_shape=outs,
        scratch_shapes=list(scratch),
        input_output_aliases=aliases or {},
        compiler_params=pltpu.CompilerParams(vmem_limit_bytes=VMEM_LIMIT),
        cost_estimate=pl.CostEstimate(flops=weight, bytes_accessed=weight, transcendentals=0),
        name=name,
    )(*[vm(a) if specs is None or specs[i] is IN_VMEM else a for i, a in enumerate(args)])


def shards(ensemble, gradient):
    members, levels, rows, width = ensemble.shape
    total = members * levels
    ens = hbm(ensemble.reshape(total, rows, width))
    counts = (FIRST, total - FIRST)
    t_one, t_two = map(tiles_of, counts)
    n_tiles = t_one + t_two
    center, spread = map(jnp.asarray, lon_weights(width))
    low, own, high = np.split(band(rows, EDGE).T, [EDGE, EDGE + rows], axis=1)
    lat = jnp.asarray(np.stack([np.concatenate(v, axis=1) for v in ((high, own, low), (low, own, high))]))

    def shape(n, r=rows, c=width):
        return pltpu.VMEM((n, r, c), BF)

    def tiles(n, r=rows):
        return shape(n, r, LANES)

    dma = pltpu.SemaphoreType.DMA
    a_one, b_one, prod_one, select, grad = call(
        first_kernel,
        "pack_first",
        (ens, hbm(gradient)),
        [tiles(t_one), tiles(t_one), shape(counts[0]), shape(8, width, 2 * LANES), shape(levels)],
        scratch=[shape(counts[0]), dma((2,))],
        specs=[ANYWHERE] * 2,
    )
    a_one = first_partner(a_one, "lon")

    prod_two, a_two, b_two, near, far = call(
        functools.partial(second_kernel, counts[0]),
        "pack_second",
        (ens, grad, select, b_one),
        [shape(counts[1]), tiles(t_two), tiles(t_two), tiles(n_tiles, EDGE), tiles(n_tiles, EDGE)],
        scratch=[shape(counts[1]), dma],
        specs=[ANYWHERE, IN_VMEM, IN_VMEM, IN_VMEM],
    )
    a_two = first_partner(a_two, "lon")
    near, far = lat_exchange(near, far)
    (b,) = call(edge_lat_kernel, "edge_lat_sums", (b_one, b_two, near, far, lat), [tiles(n_tiles)])
    b = second_partner(b, "lon", True)

    own, near, far = call(
        own_kernel, "own_lon_sums", (prod_one, prod_two, center), [shape(total)] + [shape(total, EDGE)] * 2
    )
    near, far = lat_exchange(near, far)
    tnear, tfar = call(
        tile_rows_kernel, "tile_rows", (a_one, a_two), [tiles(n_tiles, EDGE)] * 2, weight=HEAVY
    )
    tnear, tfar = lat_exchange(tnear, tfar)
    (acc,) = call(
        functools.partial(partial_kernel, counts),
        "all_but_second",
        (own, near, far, a_one, a_two, tnear, tfar, lat, spread),
        [pltpu.VMEM((total, rows, width), jnp.float32)],
        scratch=[tiles(n_tiles)],
    )
    (result,) = call(
        functools.partial(last_kernel, counts),
        "add_second",
        (acc, b, spread),
        [jax.ShapeDtypeStruct((total, rows, width), BF)],
        scratch=[shape(total), dma((len(all_units(counts)),))],
        out_specs=[ANYWHERE],
    )
    return result.reshape(members, levels, rows, width)


def solution(mesh):
    placed = (P(None, None, "lat", "lon"), P(None, "lat", "lon"))
    return jax.shard_map(
        shards, mesh=mesh, in_specs=placed, out_specs=P(None, None, "lat", "lon"), check_vma=False
    )
```

time: 79.2 us -> 46.6 us (0.59)
  waiting for transfers between devices: 36 us -> 9.64 us
  Pallas kernels: 0 us -> 19.5 us
  local copies, waits for them, and re-layouts: 15.4 us -> 0.02 us
  matrix products: 10.4 us -> 0 us
  starting transfers between devices: 10.9 us -> 17 us
  other arithmetic: 4.6 us -> 0 us
    ppermute x4 -> x9, waiting for transfers between devices: 36 us -> 9.64 us  [the longest x4 9.63 us: second_partner(): return lax.ppermute(x, axis, pairs)]
    pallas_call x0 -> x7, Pallas kernels: none -> 19.5 us  [call(): pl.pallas_call(kernel, in_specs=specs or [IN_VMEM] * len(args), out_specs...]
    dot_general x2 -> x0, matrix products: 10.4 us -> none  [the longest x1 5.23 us: shards(): jnp.einsum('mlap,pq->mlaq', widened, lon_kernel, preferred_element_type=j...]
    unnamed x3 -> x8, local copies, waits for them, and re-layouts: 10.3 us -> 0.02 us
    ppermute x4 -> x9, starting transfers between devices: 10.9 us -> 17 us  [the longest x4 13.7 us: second_partner(): return lax.ppermute(x, axis, pairs)]
    convert_element_type x1 -> x0, other arithmetic: 3.98 us -> none  [shards(): (ensemble.astype(jnp.float32) * gradient.astype(jnp.float32)[None]).astyp...]
    slice x6 -> x0, local copies, waits for them, and re-layouts: 3.25 us -> none  [the longest x4 2.15 us: padded(): lax.slice_in_dim(block, block.shape[dim] - width, None, axis=dim)]
    convert_element_type x1 -> x0, local copies, waits for them, and re-layouts: 1 us -> none  [shards(): gradient.astype(jnp.float32)[None]]
  transfers between devices with their start and end apart: 4 -> 9, of which waited for: 4 -> 1; matrix products, arithmetic and copies ran while one was open for 3% -> 0% of each run, Pallas kernels for 0% -> 27%
where the time goes in v2:
time: 46.6 us; the launch traced here: 46.3 us
  Pallas kernels  19.5 us (42%)
  starting transfers between devices  17 us (36%)
  waiting for transfers between devices  9.64 us (21%)
    pallas_call x7, Pallas kernels, call(): pl.pallas_call(kernel, in_specs=specs or [IN_VMEM] * len(args), out_specs...  19.5 us
    ppermute x4, starting transfers between devices, second_partner(): return lax.ppermute(x, axis, pairs)  13.7 us
    ppermute x4, waiting for transfers between devices, second_partner(): return lax.ppermute(x, axis, pairs)  9.63 us
    ppermute x5, starting transfers between devices, first_partner(): lax.ppermute(x, axis, [(i, i ^ 1) for i in range(lax.axis_size(axis))])  3.27 us
  transfers between devices with their start and end apart: 9, of which 1 were waited for; matrix products, arithmetic and copies ran while one was open for 0% of the time, Pallas kernels for 27%

profile of v2, /device:TPU:1, one launch (start us, length us, event | category | flops | bytes accessed | tf_op | source)
XLA Modules:
  0.0 46.3 jit_solution(3788432785456020346)
XLA Ops:
  0.0 2.9 %pack_first.1 = (bf16[10,128,128]{2,1,0:T(8,128)(2,1)S(1)}, bf16[10,128,128]{2,1,0:T(8,128)(2,1)S(1)}, bf16[42,128,256]{2,1,0:T(8,128)(2,1)S(1)}, bf16[8,256,256...) custom-call(bf16[80,128,256]{2,1,0:T(8,128)(2,1)} %bitcast.2, bf16[2,128,256]{2,1,0:T(8,128)(2,1)} %grad_ref.1), custom_call_target="tpu_custom_call" | custom-call | tf_op jit(solution)/shard_map/pack_first/pallas_call | solution.py:311
  3.0 2.1 %collective-permute-start.2 = (bf16[10,128,128]{2,1,0:T(8,128)(2,1)S(1)}, bf16[10,128,128]{2,1,0:T(8,128)(2,1)S(1)}, u32[]{:S(2)}, u32[]{:S(2)}) collective-permute-start(bf16[10,128,128]{2,1,0:T(8,128)(2,1)S(1)} %get-tuple-element.28), channel_id=1, source_target_pairs={{0,4},{4,0},{8,12},{12,8},{16,20},{20,16},{24,28},{28,24},{1,5},{5... | collective-permute-start | bytes 983048 | tf_op jit(solution)/shard_map/ppermute | solution.py:281
  5.1 2.8 %pack_second.1 = (bf16[38,128,256]{2,1,0:T(8,128)(2,1)S(1)}, bf16[9,128,128]{2,1,0:T(8,128)(2,1)S(1)}, bf16[9,128,128]{2,1,0:T(8,128)(2,1)S(1)}, bf16[19,32,128]...) custom-call(bf16[80,128,256]{2,1,0:T(8,128)(2,1)} %bitcast.3, bf16[2,128,256]{2,1,0:T(8,128)(2,1)S(1)} %get-tuple-element.21.gvm_ref, ...), custom_call_target="tpu_custom_call" | custom-call | tf_op jit(solution)/shard_map/pack_second/pallas_call | solution.py:311
  7.9 0.0 copy-start.1
  7.9 0.1 collective-permute-start.3
  8.0 1.0 %collective-permute-start.6 = (bf16[19,32,128]{2,1,0:T(8,128)(2,1)S(1)}, bf16[19,32,128]{2,1,0:T(8,128)(2,1)S(1)}, u32[]{:S(2)}, u32[]{:S(2)}) collective-permute-start(bf16[19,32,128]{2,1,0:T(8,128)(2,1)S(1)} %get-tuple-element.33), channel_id=1, source_target_pairs={{0,1},{1,0},{2,3},{3,2},{4,5},{5,4},{6,7},{7,6},{8,9},{9,8},{10,11... | collective-permute-start | bytes 466952 | tf_op jit(solution)/shard_map/ppermute | solution.py:281
  9.0 3.5 %collective-permute-start.7 = (bf16[19,32,128]{2,1,0:T(8,128)(2,1)S(1)}, bf16[19,32,128]{2,1,0:T(8,128)(2,1)S(1)}, u32[]{:S(2)}, u32[]{:S(2)}) collective-permute-start(bf16[19,32,128]{2,1,0:T(8,128)(2,1)S(1)} %get-tuple-element.34), channel_id=1, source_target_pairs={{1,2},{2,1},{5,6},{6,5},{9,10},{10,9},{13,14},{14,13},{17,18},{18,... | collective-permute-start | bytes 466952 | tf_op jit(solution)/shard_map/ppermute | solution.py:291
  12.5 3.6 %own_lon_sums.1 = (bf16[80,128,256]{2,1,0:T(8,128)(2,1)S(1)}, bf16[80,32,256]{2,1,0:T(8,128)(2,1)}, bf16[80,32,256]{2,1,0:T(8,128)(2,1)}) custom-call(bf16[42,128,256]{2,1,0:T(8,128)(2,1)S(1)} %get-tuple-element.20.one_ref, bf16[38,128,256]{2,1,0:T(8,128)(2,1)S(1)} %get-tuple-element.24.two_ref, bf16[256,256]{1,0:T(8,128)(2,1)S(1)} %copy-done.3), custom_call_target="tpu_custom_call" | custom-call | tf_op jit(solution)/shard_map/own_lon_sums/pallas_call | solution.py:311
  16.0 0.0 collective-permute-start
  16.0 0.0 collective-permute-done.6.near_ref
  16.0 2.0 %collective-permute-start.1 = (bf16[80,32,256]{2,1,0:T(8,128)(2,1)}, bf16[80,32,256]{2,1,0:T(8,128)(2,1)}, u32[]{:S(2)}, u32[]{:S(2)}) collective-permute-start(bf16[80,32,256]{2,1,0:T(8,128)(2,1)} %get-tuple-element.27), channel_id=1, source_target_pairs={{1,2},{2,1},{5,6},{6,5},{9,10},{10,9},{13,14},{14,13},{17,18},{18,... | collective-permute-start | bytes 3932168 | tf_op jit(solution)/shard_map/ppermute | solution.py:291
  18.1 0.0 collective-permute-done.7.far_ref
  18.1 1.2 %edge_lat_sums.1 = bf16[19,128,128]{2,1,0:T(8,128)(2,1)} custom-call(bf16[10,128,128]{2,1,0:T(8,128)(2,1)S(1)} %get-tuple-element.23.b_first_ref.one_ref, bf16[9,128,128]{2,1,0:T(8,128)(2,1)S(1)} %get-tuple-element.32.two_ref, bf16[19,32,128]{2,1,0:T(8,128)(2,1)S(1)} %collective-permute-done.6.near_ref, ...), custom_call_target="tpu_custom_call" | custom-call | tf_op jit(solution)/shard_map/edge_lat_sums/pallas_call | solution.py:311
  19.3 4.7 %collective-permute-start.8 = (bf16[19,128,128]{2,1,0:T(8,128)(2,1)}, bf16[19,128,128]{2,1,0:T(8,128)(2,1)}, u32[]{:S(2)}, u32[]{:S(2)}) collective-permute-start(bf16[19,128,128]{2,1,0:T(8,128)(2,1)} %edge_lat_sums.1), channel_id=1, source_target_pairs={{0,28},{4,8},{8,4},{12,16},{16,12},{20,24},{24,20},{28,0},{1,29},{... | collective-permute-start | bytes 1867784 | tf_op jit(solution)/shard_map/ppermute | solution.py:291
  24.0 0.0 collective-permute-done.2.one_ref
  24.0 0.0 copy-start.2
  24.0 0.1 collective-permute-start.4
  24.1 3.5 %collective-permute-start.5 = (bf16[19,32,128]{2,1,0:T(8,128)(2,1)S(1)}, bf16[19,32,128]{2,1,0:T(8,128)(2,1)S(1)}, u32[]{:S(2)}, u32[]{:S(2)}) collective-permute-start(bf16[19,32,128]{2,1,0:T(8,128)(2,1)S(1)} %get-tuple-element.31), channel_id=1, source_target_pairs={{1,2},{2,1},{5,6},{6,5},{9,10},{10,9},{13,14},{14,13},{17,18},{18,... | collective-permute-start | bytes 466952 | tf_op jit(solution)/shard_map/ppermute | solution.py:291
  27.6 0.0 collective-permute-done.4.tnear_ref
  27.6 9.6 %collective-permute-done.5.tfar_ref = bf16[19,32,128]{2,1,0:T(8,128)(2,1)S(1)} collective-permute-done((bf16[19,32,128]{2,1,0:T(8,128)(2,1)S(1)}, bf16[19,32,128]{2,1,0:T(8,128)(2,1)S(1)}, u32[]{:S(2)}, u32[]{:S(2)}) %collective-permute-start.5) | collective-permute-done | bytes 155680 | tf_op jit(solution)/shard_map/ppermute | solution.py:291
  37.2 0.0 collective-permute-done.near_ref
  37.2 0.0 collective-permute-done.1.far_ref
  37.2 5.0 %all_but_second.1.acc_ref = f32[80,128,256]{2,1,0:T(8,128)S(1)} custom-call(bf16[80,128,256]{2,1,0:T(8,128)(2,1)S(1)} %get-tuple-element.25.own_ref, bf16[80,32,256]{2,1,0:T(8,128)(2,1)} %collective-permute-done.near_ref, bf16[80,32,256]{2,1,0:T(8,128)(2,1)} %collective-permute-done.1.far_ref, bf16[10,128,128]{2,1,0:T(8,128)(2,1)S(1)} %collective-permute-done.2.one_ref, ...), custom_call_target="tpu_custom_call" | custom-call | tf_op jit(solution)/shard_map/all_but_second/pallas_call | solution.py:311
  42.2 4.0 %add_second.1 = bf16[80,128,256]{2,1,0:T(8,128)(2,1)} custom-call(f32[80,128,256]{2,1,0:T(8,128)S(1)} %all_but_second.1.acc_ref, bf16[19,128,128]{2,1,0:T(8,128)(2,1)} %collective-permute-done.8.tiles_ref, bf16[8,256,256]{2,1,0:T(8,128)(2,1)S(1)} %copy-done), custom_call_target="tpu_custom_call" | custom-call | tf_op jit(solution)/shard_map/add_second/pallas_call | solution.py:311
  (9 shorter events, 0.1 us)
Async XLA Ops:
  3.0 21.0 %collective-permute-start.2 = (bf16[10,128,128]{2,1,0:T(8,128)(2,1)S(1)}, bf16[10,128,128]{2,1,0:T(8,128)(2,1)S(1)}, u32[]{:S(2)}, u32[]{:S(2)}) collective-permute-start(bf16[10,128,128]{2,1,0:T(8,128)(2,1)S(1)} %get-tuple-element.28), channel_id=1, source_target_pairs={{0,4},{4,0},{8,12},{12,8},{16,20},{20,16},{24,28},{28,24},{1,5},{5... | collective-permute-start | bytes 983048 | tf_op jit(solution)/shard_map/ppermute | solution.py:281
  5.1 7.4 %copy-start.3 = (bf16[256,256]{1,0:T(8,128)(2,1)S(1)}, bf16[256,256]{1,0:T(8,128)(2,1)}, u32[]{:S(2)}) copy-start(bf16[256,256]{1,0:T(8,128)(2,1)} %constant.6.clone.center_ref) | copy-start | bytes 393220
  7.9 10.2 %copy-start.1 = (bf16[2,128,192]{2,1,0:T(8,128)(2,1)S(1)}, bf16[2,128,192]{2,1,0:T(8,128)(2,1)}, u32[]{:S(2)}) copy-start(bf16[2,128,192]{2,1,0:T(8,128)(2,1)} %constant.8.clone.lat_ref) | copy-start | bytes 294916
  7.9 16.1 %collective-permute-start.3 = (bf16[9,128,128]{2,1,0:T(8,128)(2,1)S(1)}, bf16[9,128,128]{2,1,0:T(8,128)(2,1)S(1)}, u32[]{:S(2)}, u32[]{:S(2)}) collective-permute-start(bf16[9,128,128]{2,1,0:T(8,128)(2,1)S(1)} %get-tuple-element.29), channel_id=1, source_target_pairs={{0,4},{4,0},{8,12},{12,8},{16,20},{20,16},{24,28},{28,24},{1,5},{5... | collective-permute-start | bytes 884744 | tf_op jit(solution)/shard_map/ppermute | solution.py:281
  8.0 8.1 %collective-permute-start.6 = (bf16[19,32,128]{2,1,0:T(8,128)(2,1)S(1)}, bf16[19,32,128]{2,1,0:T(8,128)(2,1)S(1)}, u32[]{:S(2)}, u32[]{:S(2)}) collective-permute-start(bf16[19,32,128]{2,1,0:T(8,128)(2,1)S(1)} %get-tuple-element.33), channel_id=1, source_target_pairs={{0,1},{1,0},{2,3},{3,2},{4,5},{5,4},{6,7},{7,6},{8,9},{9,8},{10,11... | collective-permute-start | bytes 466952 | tf_op jit(solution)/shard_map/ppermute | solution.py:281
  9.0 9.1 %collective-permute-start.7 = (bf16[19,32,128]{2,1,0:T(8,128)(2,1)S(1)}, bf16[19,32,128]{2,1,0:T(8,128)(2,1)S(1)}, u32[]{:S(2)}, u32[]{:S(2)}) collective-permute-start(bf16[19,32,128]{2,1,0:T(8,128)(2,1)S(1)} %get-tuple-element.34), channel_id=1, source_target_pairs={{1,2},{2,1},{5,6},{6,5},{9,10},{10,9},{13,14},{14,13},{17,18},{18,... | collective-permute-start | bytes 466952 | tf_op jit(solution)/shard_map/ppermute | solution.py:291
  16.0 21.2 %collective-permute-start = (bf16[80,32,256]{2,1,0:T(8,128)(2,1)}, bf16[80,32,256]{2,1,0:T(8,128)(2,1)}, u32[]{:S(2)}, u32[]{:S(2)}) collective-permute-start(bf16[80,32,256]{2,1,0:T(8,128)(2,1)} %get-tuple-element.26), channel_id=1, source_target_pairs={{0,1},{1,0},{2,3},{3,2},{4,5},{5,4},{6,7},{7,6},{8,9},{9,8},{10,11... | collective-permute-start | bytes 3932168 | tf_op jit(solution)/shard_map/ppermute | solution.py:281
  16.0 21.2 %collective-permute-start.1 = (bf16[80,32,256]{2,1,0:T(8,128)(2,1)}, bf16[80,32,256]{2,1,0:T(8,128)(2,1)}, u32[]{:S(2)}, u32[]{:S(2)}) collective-permute-start(bf16[80,32,256]{2,1,0:T(8,128)(2,1)} %get-tuple-element.27), channel_id=1, source_target_pairs={{1,2},{2,1},{5,6},{6,5},{9,10},{10,9},{13,14},{14,13},{17,18},{18,... | collective-permute-start | bytes 3932168 | tf_op jit(solution)/shard_map/ppermute | solution.py:291
  19.3 22.9 %collective-permute-start.8 = (bf16[19,128,128]{2,1,0:T(8,128)(2,1)}, bf16[19,128,128]{2,1,0:T(8,128)(2,1)}, u32[]{:S(2)}, u32[]{:S(2)}) collective-permute-start(bf16[19,128,128]{2,1,0:T(8,128)(2,1)} %edge_lat_sums.1), channel_id=1, source_target_pairs={{0,28},{4,8},{8,4},{12,16},{16,12},{20,24},{24,20},{28,0},{1,29},{... | collective-permute-start | bytes 1867784 | tf_op jit(solution)/shard_map/ppermute | solution.py:291
  24.0 13.2 %copy-start = (bf16[8,256,256]{2,1,0:T(8,128)(2,1)S(1)}, bf16[8,256,256]{2,1,0:T(8,128)(2,1)}, u32[]{:S(2)}) copy-start(bf16[8,256,256]{2,1,0:T(8,128)(2,1)} %constant.7.clone.spread_ref) | copy-start | bytes 3145732
  24.0 13.2 %copy-start.2 = (bf16[2,128,192]{2,1,0:T(8,128)(2,1)S(1)}, bf16[2,128,192]{2,1,0:T(8,128)(2,1)}, u32[]{:S(2)}) copy-start(bf16[2,128,192]{2,1,0:T(8,128)(2,1)} %constant.8.clone.lat_ref) | copy-start | bytes 294916
  24.0 3.5 %collective-permute-start.4 = (bf16[19,32,128]{2,1,0:T(8,128)(2,1)S(1)}, bf16[19,32,128]{2,1,0:T(8,128)(2,1)S(1)}, u32[]{:S(2)}, u32[]{:S(2)}) collective-permute-start(bf16[19,32,128]{2,1,0:T(8,128)(2,1)S(1)} %get-tuple-element.30), channel_id=1, source_target_pairs={{0,1},{1,0},{2,3},{3,2},{4,5},{5,4},{6,7},{7,6},{8,9},{9,8},{10,11... | collective-permute-start | bytes 466952 | tf_op jit(solution)/shard_map/ppermute | solution.py:281
  24.1 13.1 %collective-permute-start.5 = (bf16[19,32,128]{2,1,0:T(8,128)(2,1)S(1)}, bf16[19,32,128]{2,1,0:T(8,128)(2,1)S(1)}, u32[]{:S(2)}, u32[]{:S(2)}) collective-permute-start(bf16[19,32,128]{2,1,0:T(8,128)(2,1)S(1)} %get-tuple-element.31), channel_id=1, source_target_pairs={{1,2},{2,1},{5,6},{6,5},{9,10},{10,9},{13,14},{14,13},{17,18},{18,... | collective-permute-start | bytes 466952 | tf_op jit(solution)/shard_map/ppermute | solution.py:291

commit v3 on v2

--- a/solution.py
+++ b/solution.py
@@ -14,7 +14,9 @@
 GROUP = 17
 VMEM_LIMIT = 16 * 1024 * 1024
 FIRST = 42
-HEAVY = 200_000_000_000
+LAST = 2
+BATCH = 8
+HEAVY = 10_000_000_000
 BF = jnp.bfloat16
 
 
@@ -129,139 +131,131 @@
         b_ref[at] = tiles[:, :, LANES:]
 
 
-def edge_rows(ref, rows):
-    side = odd("lat")
-    head, tail = 0, rows - EDGE
-    return (
-        pl.ds(pl.multiple_of((1 - side) * tail, EDGE), EDGE),
-        pl.ds(pl.multiple_of(side * tail, EDGE), EDGE),
-    )
+def emit_rows(v, near_ref, far_ref, at):
+    up = odd("lat") == 0
+    head, tail = v[:, :EDGE], v[:, v.shape[1] - EDGE :]
+    near_ref[at] = jnp.where(up, tail, head)
+    far_ref[at] = jnp.where(up, head, tail)
 
 
 def second_kernel(
     before, ens_ref, gvm_ref, select_ref, b_first_ref, prod_ref, a_ref, b_ref, near_ref, far_ref, buf, sem
 ):
-    count, rows = prod_ref.shape[:2]
+    count = prod_ref.shape[0]
     copy = pltpu.make_async_copy(ens_ref.at[pl.ds(before, count)], buf, sem)
     copy.start()
+    skip = b_first_ref.shape[0]
+    for t in range(skip):
+        emit_rows(b_first_ref[t : t + 1], near_ref, far_ref, pl.ds(t, 1))
     copy.wait()
     multiply(buf, before, gvm_ref, prod_ref)
     for at, tiles in packed_units(prod_ref, select_ref):
         a_ref[at] = tiles[:, :, :LANES]
         b_ref[at] = tiles[:, :, LANES:]
-    near, far = edge_rows(b_ref, rows)
+        emit_rows(tiles[:, :, LANES:], near_ref, far_ref, pl.ds(skip + at.start, at.size))
+
+
+def rows_kernel(one_ref, two_ref, near_ref, far_ref):
     start = 0
-    for ref in (b_first_ref, b_ref):
-        to = pl.ds(start, ref.shape[0])
-        near_ref[to] = ref[:, near]
-        far_ref[to] = ref[:, far]
+    for ref in (one_ref, two_ref):
+        for f in range(0, ref.shape[0], 4):
+            n = min(4, ref.shape[0] - f)
+            emit_rows(ref[f : f + n], near_ref, far_ref, pl.ds(start + f, n))
         start += ref.shape[0]
 
 
-def pair(ref, t):
-    if t + 1 < ref.shape[0]:
-        return jnp.concatenate([ref[t], ref[t + 1]], axis=1)
-    return ref[t]
-
-
-def lat_field(field, near, far, lat):
-    return dot(lat, jnp.concatenate([near, field, far], axis=0))
-
-
-def lat_tiles(refs, near_ref, far_ref, lat, emit):
+def lat_field(field, low, high, lat_ref):
+    return dot(lat_ref[...], jnp.concatenate([low, field, high], axis=0))
+
+
+def lat_tiles(refs, near_ref, far_ref, order, lat_ref, emit):
     start = 0
     for ref in refs:
         for t in range(0, ref.shape[0], 2):
             n = min(2, ref.shape[0] - t)
-            wide = [jnp.concatenate([r[start + t + i] for i in range(n)], axis=1) for r in (near_ref, far_ref)]
-            done = lat_field(pair(ref, t), *wide, lat).astype(BF)
+            wide = [
+                jnp.concatenate([r[i] for i in range(first, first + n)], axis=1)
+                for r, first in ((ref, t), (near_ref, start + t), (far_ref, start + t))
+            ]
+            done = lat_field(wide[0], *order(*wide[1:]), lat_ref).astype(BF)
             for i in range(n):
                 emit(start + t + i, done[:, i * LANES : (i + 1) * LANES])
         start += ref.shape[0]
 
 
-def edge_lat_kernel(one_ref, two_ref, near_ref, far_ref, lat_ref, out_ref):
+def edge_lat_kernel(one_ref, two_ref, near_ref, far_ref, lat_ref, *refs):
+    up = odd("lat") == 0
+    out_refs = [r for r in refs if r.shape[1:] == one_ref.shape[1:]]
+
+    def order(near, far):
+        return jnp.where(up, far, near), jnp.where(up, near, far)
+
     def emit(t, v):
-        out_ref[t] = v
-
-    lat_tiles((one_ref, two_ref), near_ref, far_ref, lat_ref[odd("lat")], emit)
-
-
-def own_kernel(one_ref, two_ref, center_ref, own_ref, near_ref, far_ref):
-    rows, width = own_ref.shape[1:]
-    start = 0
-    for prod_ref in (one_ref, two_ref):
-        count = prod_ref.shape[0]
-        for first in range(0, count, 4):
-            n = min(4, count - first)
-            v = dot(stack(prod_ref, first, n), center_ref[...]).astype(BF).reshape(n, rows, width)
-            own_ref[pl.ds(start + first, n)] = v
-        start += count
-    near, far = edge_rows(own_ref, rows)
-    near_ref[...] = own_ref[:, near]
-    far_ref[...] = own_ref[:, far]
-
-
-def tile_rows_kernel(one_ref, two_ref, near_ref, far_ref):
-    near, far = edge_rows(one_ref, one_ref.shape[1])
+        for ref in out_refs:
+            if t < ref.shape[0]:
+                ref[t] = v
+                return
+            t -= ref.shape[0]
+
+    lat_tiles((one_ref, two_ref), near_ref, far_ref, order, lat_ref, emit)
+
+
+def add_rows(acc_ref, rows_ref, start, near, center_ref, border_ref):
+    low = odd("lat") if near else 1 - odd("lat")
+    edge = acc_ref.shape[1] - EDGE
+    at = pl.ds(pl.multiple_of((1 - low) * edge, EDGE), EDGE)
+    for first in range(0, acc_ref.shape[0], BATCH):
+        count = min(BATCH, acc_ref.shape[0] - first)
+        own = dot(stack(rows_ref, start + first, count), center_ref[...]).astype(BF)
+        part = dot(border_ref[low, : count * EDGE, : count * EDGE], own)
+        for i in range(count):
+            acc_ref[first + i, at] += part[i * EDGE : (i + 1) * EDGE]
+
+
+def tile_rows_kernel(one_ref, two_ref, after_ref, near_ref, far_ref):
+    del after_ref
+    rows_kernel(one_ref, two_ref, near_ref, far_ref)
+
+
+def own_kernel(one_ref, two_ref, center_ref, lat_ref, acc_ref):
+    rows, width = acc_ref.shape[1:]
     start = 0
     for ref in (one_ref, two_ref):
-        to = pl.ds(start, ref.shape[0])
-        near_ref[to] = ref[:, near]
-        far_ref[to] = ref[:, far]
+        for f in range(0, ref.shape[0], 4):
+            n = min(4, ref.shape[0] - f)
+            own = dot(stack(ref, f, n), center_ref[...]).astype(BF)
+            for i in range(n):
+                acc_ref[start + f + i] = dot(lat_ref[:, EDGE : EDGE + rows], own[i * rows : (i + 1) * rows])
         start += ref.shape[0]
 
 
-def spread_rows(first):
-    side = odd("lon") if first else 1 - odd("lon")
-    return pl.ds(pl.multiple_of((1 - side) * LANES, LANES), LANES)
-
-
-def partial_kernel(
-    counts, own_ref, near_ref, far_ref, one_ref, two_ref, tnear_ref, tfar_ref, lat_ref, spread_ref, acc_ref, done
-):
-    lat = lat_ref[odd("lat")]
-    rows, width = own_ref.shape[1:]
-    at = spread_rows(True)
-
-    def emit(t, v):
-        done[t] = v
-
-    lat_tiles((one_ref, two_ref), tnear_ref, tfar_ref, lat, emit)
-
-    def own(first, n):
-        return jnp.concatenate(
-            [lat_field(own_ref[f], near_ref[f], far_ref[f], lat) for f in range(first, first + n)], axis=0
-        )
-
-    for first, n, extra, tile in all_units(counts):
-        edges = stack(done, tile, n)
+def halo_kernel(own_ref, near_ref, far_ref, center_ref, border_ref, acc_ref):
+    del own_ref
+    add_rows(acc_ref, near_ref, 0, True, center_ref, border_ref)
+    add_rows(acc_ref, far_ref, 0, False, center_ref, border_ref)
+
+
+def last_kernel(plan, acc_ref, done_ref, tiles_ref, spread_ref, *refs):
+    out_ref, buf, sems = refs[-3:]
+    rows, width = acc_ref.shape[1:]
+    up = odd("lon") == 0
+    start, skip = plan[0][0], plan[0][3]
+    copies = []
+    for first, n, extra, tile in plan:
+        a, b = stack(done_ref, tile, n), stack(tiles_ref, tile - skip, n)
+        edges = jnp.concatenate([jnp.where(up, b, a), jnp.where(up, a, b)], axis=1)
         for s in range(4):
-            v = own(first + s * n, n) + dot(edges, spread_ref[s, at])
-            acc_ref[pl.ds(first + s * n, n)] = v.reshape(n, rows, width)
-        if extra:
-            v = own(first + 4 * n, 1)
-            for t in range(n):
-                v += dot(done[tile + t], spread_ref[4 + t, at])
-            acc_ref[first + 4 * n] = v
-
-
-def last_kernel(counts, acc_ref, tiles_ref, spread_ref, out_ref, buf, sems):
-    rows, width = acc_ref.shape[1:]
-    at = spread_rows(False)
-    copies = []
-    for first, n, extra, tile in all_units(counts):
-        edges = stack(tiles_ref, tile, n)
-        for s in range(4):
-            to = pl.ds(first + s * n, n)
-            buf[to] = (acc_ref[to] + dot(edges, spread_ref[s, at]).reshape(n, rows, width)).astype(BF)
+            at = pl.ds(first + s * n, n)
+            v = acc_ref[at] + dot(edges, spread_ref[s]).reshape(n, rows, width)
+            buf[pl.ds(first - start + s * n, n)] = v.astype(BF)
         if extra:
             v = acc_ref[first + 4 * n]
             for t in range(n):
-                v += dot(tiles_ref[tile + t], spread_ref[4 + t, at])
-            buf[first + 4 * n] = v.astype(BF)
-        to = pl.ds(first, 4 * n + extra)
-        copies.append(pltpu.make_async_copy(buf.at[to], out_ref.at[to], sems.at[len(copies)]))
+                v += dot(edges[t * rows : (t + 1) * rows], spread_ref[4 + t])
+            buf[first - start + 4 * n] = v.astype(BF)
+        count = 4 * n + extra
+        from_, to = pl.ds(first - start, count), pl.ds(first, count)
+        copies.append(pltpu.make_async_copy(buf.at[from_], out_ref.at[to], sems.at[len(copies)]))
         copies[-1].start()
     for c in copies:
         c.wait()
@@ -329,8 +323,12 @@
     t_one, t_two = map(tiles_of, counts)
     n_tiles = t_one + t_two
     center, spread = map(jnp.asarray, lon_weights(width))
-    low, own, high = np.split(band(rows, EDGE).T, [EDGE, EDGE + rows], axis=1)
-    lat = jnp.asarray(np.stack([np.concatenate(v, axis=1) for v in ((high, own, low), (low, own, high))]))
+    lat = band(rows, EDGE).T
+    eye = np.eye(BATCH)
+    border = jnp.asarray(
+        np.stack([np.kron(eye, lat[rows - EDGE :, rows + EDGE :]), np.kron(eye, lat[:EDGE, :EDGE])]).astype(BF)
+    )
+    lat = jnp.asarray(lat.copy())
 
     def shape(n, r=rows, c=width):
         return pltpu.VMEM((n, r, c), BF)
@@ -358,33 +356,45 @@
         specs=[ANYWHERE, IN_VMEM, IN_VMEM, IN_VMEM],
     )
     a_two = first_partner(a_two, "lon")
+    tnear, tfar = lat_exchange(near, far)
+    near, far = call(rows_kernel, "edge_rows", (prod_one, prod_two), [shape(total, EDGE)] * 2)
     near, far = lat_exchange(near, far)
-    (b,) = call(edge_lat_kernel, "edge_lat_sums", (b_one, b_two, near, far, lat), [tiles(n_tiles)])
-    b = second_partner(b, "lon", True)
-
-    own, near, far = call(
-        own_kernel, "own_lon_sums", (prod_one, prod_two, center), [shape(total)] + [shape(total, EDGE)] * 2
-    )
-    near, far = lat_exchange(near, far)
+    sums = pltpu.VMEM((total, rows, width), jnp.float32)
+    (acc,) = call(own_kernel, "own_sums", (prod_one, prod_two, center, lat), [sums])
+    plan = all_units(counts)
+    t_last = sum(n for _, n, _, _ in plan[-LAST:])
+    payload, payload_last = call(
+        edge_lat_kernel,
+        "edge_lat_sums",
+        (b_one, b_two, tnear, tfar, lat, acc),
+        [tiles(n_tiles - t_last), tiles(t_last)],
+    )
+    b = second_partner(payload, "lon", True)
+
     tnear, tfar = call(
-        tile_rows_kernel, "tile_rows", (a_one, a_two), [tiles(n_tiles, EDGE)] * 2, weight=HEAVY
+        tile_rows_kernel, "tile_rows", (a_one, a_two, acc), [tiles(n_tiles, EDGE)] * 2, weight=HEAVY
     )
     tnear, tfar = lat_exchange(tnear, tfar)
-    (acc,) = call(
-        functools.partial(partial_kernel, counts),
-        "all_but_second",
-        (own, near, far, a_one, a_two, tnear, tfar, lat, spread),
-        [pltpu.VMEM((total, rows, width), jnp.float32)],
-        scratch=[tiles(n_tiles)],
-    )
-    (result,) = call(
-        functools.partial(last_kernel, counts),
-        "add_second",
-        (acc, b, spread),
-        [jax.ShapeDtypeStruct((total, rows, width), BF)],
-        scratch=[shape(total), dma((len(all_units(counts)),))],
-        out_specs=[ANYWHERE],
-    )
+    b_last = second_partner(payload_last, "lon", True)
+    (acc,) = call(halo_kernel, "halo_rows", (acc, near, far, center, border), [sums], aliases={0: 0})
+    (done,) = call(edge_lat_kernel, "first_lat_sums", (a_one, a_two, tnear, tfar, lat), [tiles(n_tiles)])
+
+    def finish(part, tiles_in, whole, name):
+        args = (acc, done, tiles_in, spread, *whole)
+        (result,) = call(
+            functools.partial(last_kernel, part),
+            name,
+            args,
+            [jax.ShapeDtypeStruct((total, rows, width), BF)],
+            scratch=[shape(sum(4 * n + x for _, n, x, _ in part)), dma((len(part),))],
+            specs=[IN_VMEM] * 4 + [ANYWHERE] * len(whole),
+            out_specs=[ANYWHERE],
+            aliases={4: 0} if whole else None,
+        )
+        return result
+
+    result = finish(plan[:-LAST], b, (), "edge_sums")
+    result = finish(plan[-LAST:], b_last, (result,), "edge_sums_last")
     return result.reshape(members, levels, rows, width)
 
 

time: 46.6 us -> 40.1 us (0.86)
  waiting for transfers between devices: 9.64 us -> 5.55 us
  Pallas kernels: 19.5 us -> 15.6 us
  starting transfers between devices: 17 us -> 18.4 us
    ppermute x4 -> x5, waiting for transfers between devices: 9.63 us -> 5.53 us  [second_partner(): return lax.ppermute(x, axis, pairs)]
    pallas_call x7 -> x10, Pallas kernels: 19.5 us -> 15.6 us  [call(): pl.pallas_call(kernel, in_specs=specs or [IN_VMEM] * len(args), out_specs...]
    ppermute x4 -> x5, starting transfers between devices: 13.7 us -> 15.1 us  [second_partner(): return lax.ppermute(x, axis, pairs)]
  transfers between devices with their start and end apart: 9 -> 10, of which waited for: 1 -> 1; matrix products, arithmetic and copies ran while one was open for 0% -> 0% of each run, Pallas kernels for 27% -> 28%
where the time goes in v3:
time: 40.1 us; the launch traced here: 39.9 us
  starting transfers between devices  18.4 us (46%)
  Pallas kernels  15.6 us (39%)
  waiting for transfers between devices  5.55 us (14%)
    pallas_call x10, Pallas kernels, call(): pl.pallas_call(kernel, in_specs=specs or [IN_VMEM] * len(args), out_specs...  15.6 us
    ppermute x5, starting transfers between devices, second_partner(): return lax.ppermute(x, axis, pairs)  15.1 us
    ppermute x5, waiting for transfers between devices, second_partner(): return lax.ppermute(x, axis, pairs)  5.53 us
    ppermute x5, starting transfers between devices, first_partner(): lax.ppermute(x, axis, [(i, i ^ 1) for i in range(lax.axis_size(axis))])  3.35 us
  transfers between devices with their start and end apart: 10, of which 1 were waited for; matrix products, arithmetic and copies ran while one was open for 0% of the time, Pallas kernels for 28%

profile of v3, /device:TPU:1, one launch (start us, length us, event | category | flops | bytes accessed | tf_op | source)
XLA Modules:
  0.0 39.9 jit_solution(2626489969261202938)
XLA Ops:
  0.0 2.9 %pack_first.1 = (bf16[10,128,128]{2,1,0:T(8,128)(2,1)S(1)}, bf16[10,128,128]{2,1,0:T(8,128)(2,1)S(1)}, bf16[42,128,256]{2,1,0:T(8,128)(2,1)S(1)}, bf16[8,256,256...) custom-call(bf16[80,128,256]{2,1,0:T(8,128)(2,1)} %bitcast.2, bf16[2,128,256]{2,1,0:T(8,128)(2,1)} %grad_ref.1), custom_call_target="tpu_custom_call" | custom-call | tf_op jit(solution)/shard_map/pack_first/pallas_call | solution.py:305
  3.0 2.1 %collective-permute-start.2 = (bf16[10,128,128]{2,1,0:T(8,128)(2,1)S(1)}, bf16[10,128,128]{2,1,0:T(8,128)(2,1)S(1)}, u32[]{:S(2)}, u32[]{:S(2)}) collective-permute-start(bf16[10,128,128]{2,1,0:T(8,128)(2,1)S(1)} %get-tuple-element.28), channel_id=1, source_target_pairs={{0,4},{4,0},{8,12},{12,8},{16,20},{20,16},{24,28},{28,24},{1,5},{5... | collective-permute-start | bytes 983048 | tf_op jit(solution)/shard_map/ppermute | solution.py:275
  5.1 2.7 %pack_second.1 = (bf16[38,128,256]{2,1,0:T(8,128)(2,1)S(1)}, bf16[9,128,128]{2,1,0:T(8,128)(2,1)S(1)}, bf16[9,128,128]{2,1,0:T(8,128)(2,1)S(1)}, bf16[19,32,128]...) custom-call(bf16[80,128,256]{2,1,0:T(8,128)(2,1)} %bitcast.3, bf16[2,128,256]{2,1,0:T(8,128)(2,1)S(1)} %get-tuple-element.22.gvm_ref, ...), custom_call_target="tpu_custom_call" | custom-call | tf_op jit(solution)/shard_map/pack_second/pallas_call | solution.py:305
  7.8 0.0 copy-start.1
  7.8 0.1 collective-permute-start.3
  7.9 1.0 %collective-permute-start.6 = (bf16[19,32,128]{2,1,0:T(8,128)(2,1)S(1)}, bf16[19,32,128]{2,1,0:T(8,128)(2,1)S(1)}, u32[]{:S(2)}, u32[]{:S(2)}) collective-permute-start(bf16[19,32,128]{2,1,0:T(8,128)(2,1)S(1)} %get-tuple-element.33), channel_id=1, source_target_pairs={{0,1},{1,0},{2,3},{3,2},{4,5},{5,4},{6,7},{7,6},{8,9},{9,8},{10,11... | collective-permute-start | bytes 466952 | tf_op jit(solution)/shard_map/ppermute | solution.py:275
  8.9 3.5 %collective-permute-start.7 = (bf16[19,32,128]{2,1,0:T(8,128)(2,1)S(1)}, bf16[19,32,128]{2,1,0:T(8,128)(2,1)S(1)}, u32[]{:S(2)}, u32[]{:S(2)}) collective-permute-start(bf16[19,32,128]{2,1,0:T(8,128)(2,1)S(1)} %get-tuple-element.34), channel_id=1, source_target_pairs={{1,2},{2,1},{5,6},{6,5},{9,10},{10,9},{13,14},{14,13},{17,18},{18,... | collective-permute-start | bytes 466952 | tf_op jit(solution)/shard_map/ppermute | solution.py:285
  12.4 0.2 edge_rows.1
  12.6 0.1 collective-permute-start
  12.7 2.1 %collective-permute-start.1 = (bf16[80,32,256]{2,1,0:T(8,128)(2,1)S(1)}, bf16[80,32,256]{2,1,0:T(8,128)(2,1)S(1)}, u32[]{:S(2)}, u32[]{:S(2)}) collective-permute-start(bf16[80,32,256]{2,1,0:T(8,128)(2,1)S(1)} %get-tuple-element.27), channel_id=1, source_target_pairs={{1,2},{2,1},{5,6},{6,5},{9,10},{10,9},{13,14},{14,13},{17,18},{18,... | collective-permute-start | bytes 3932168 | tf_op jit(solution)/shard_map/ppermute | solution.py:285
  14.8 3.2 %own_sums.1.own_ref.after_ref.refs_0_ = f32[80,128,256]{2,1,0:T(8,128)S(1)} custom-call(bf16[42,128,256]{2,1,0:T(8,128)(2,1)S(1)} %get-tuple-element.21.one_ref, bf16[38,128,256]{2,1,0:T(8,128)(2,1)S(1)} %get-tuple-element.25.two_ref, bf16[256,256]{1,0:T(8,128)(2,1)S(1)} %copy-done.2, bf16[128,192]{1,0:T(8,128)(2,1)S(1)} %copy-done.1), custom_call_target="tpu_custom_call" | custom-call | tf_op jit(solution)/shard_map/own_sums/pallas_call | solution.py:305
  18.0 0.4 edge_lat_sums.1
  18.3 0.0 copy-start.3
  18.4 4.8 %collective-permute-start.9 = (bf16[14,128,128]{2,1,0:T(8,128)(2,1)S(1)}, bf16[14,128,128]{2,1,0:T(8,128)(2,1)S(1)}, u32[]{:S(2)}, u32[]{:S(2)}) collective-permute-start(bf16[14,128,128]{2,1,0:T(8,128)(2,1)S(1)} %get-tuple-element.36), channel_id=1, source_target_pairs={{0,28},{4,8},{8,4},{12,16},{16,12},{20,24},{24,20},{28,0},{1,29},{... | collective-permute-start | bytes 1376264 | tf_op jit(solution)/shard_map/ppermute | solution.py:285
  23.1 0.1 tile_rows.1
  23.2 0.1 collective-permute-start.4
  23.3 1.4 %collective-permute-start.8 = (bf16[5,128,128]{2,1,0:T(8,128)(2,1)S(1)}, bf16[5,128,128]{2,1,0:T(8,128)(2,1)S(1)}, u32[]{:S(2)}, u32[]{:S(2)}) collective-permute-start(bf16[5,128,128]{2,1,0:T(8,128)(2,1)S(1)} %get-tuple-element.35), channel_id=1, source_target_pairs={{0,28},{4,8},{8,4},{12,16},{16,12},{20,24},{24,20},{28,0},{1,29},{... | collective-permute-start | bytes 491528 | tf_op jit(solution)/shard_map/ppermute | solution.py:285
  24.7 3.4 %collective-permute-start.5 = (bf16[19,32,128]{2,1,0:T(8,128)(2,1)S(1)}, bf16[19,32,128]{2,1,0:T(8,128)(2,1)S(1)}, u32[]{:S(2)}, u32[]{:S(2)}) collective-permute-start(bf16[19,32,128]{2,1,0:T(8,128)(2,1)S(1)} %get-tuple-element.31), channel_id=1, source_target_pairs={{1,2},{2,1},{5,6},{6,5},{9,10},{10,9},{13,14},{14,13},{17,18},{18,... | collective-permute-start | bytes 466952 | tf_op jit(solution)/shard_map/ppermute | solution.py:285
  28.1 5.5 %collective-permute-done.5.far_ref = bf16[19,32,128]{2,1,0:T(8,128)(2,1)S(1)} collective-permute-done((bf16[19,32,128]{2,1,0:T(8,128)(2,1)S(1)}, bf16[19,32,128]{2,1,0:T(8,128)(2,1)S(1)}, u32[]{:S(2)}, u32[]{:S(2)}) %collective-permute-start.5) | collective-permute-done | bytes 155680 | tf_op jit(solution)/shard_map/ppermute | solution.py:285
  33.6 0.3 first_lat_sums.1.done_ref
  33.9 0.0 copy-start
  34.0 1.7 %halo_rows.1.acc_ref = f32[80,128,256]{2,1,0:T(8,128)S(1)} custom-call(f32[80,128,256]{2,1,0:T(8,128)S(1)} %own_sums.1.own_ref.after_ref.refs_0_, bf16[80,32,256]{2,1,0:T(8,128)(2,1)S(1)} %collective-permute-done.near_ref, bf16[80,32,256]{2,1,0:T(8,128)(2,1)S(1)} %collective-permute-done.1.far_ref, ...), custom_call_target="tpu_custom_call", output_to_operand_aliasing={{}: (0, {})} | custom-call | tf_op jit(solution)/shard_map/halo_rows/pallas_call | solution.py:305
  35.7 2.5 %edge_sums.1.refs_0_ = bf16[80,128,256]{2,1,0:T(8,128)(2,1)} custom-call(f32[80,128,256]{2,1,0:T(8,128)S(1)} %halo_rows.1.acc_ref, bf16[19,128,128]{2,1,0:T(8,128)(2,1)S(1)} %first_lat_sums.1.done_ref, bf16[14,128,128]{2,1,0:T(8,128)(2,1)S(1)} %collective-permute-done.9.tiles_ref, bf16[8,256,256]{2,1,0:T(8,128)(2,1)S(1)} %copy-done), custom_call_target="tpu_custom_call" | custom-call | tf_op jit(solution)/shard_map/edge_sums/pallas_call | solution.py:305
  38.2 1.7 %edge_sums_last.1 = bf16[80,128,256]{2,1,0:T(8,128)(2,1)} custom-call(f32[80,128,256]{2,1,0:T(8,128)S(1)} %halo_rows.1.acc_ref, bf16[19,128,128]{2,1,0:T(8,128)(2,1)S(1)} %first_lat_sums.1.done_ref, bf16[5,128,128]{2,1,0:T(8,128)(2,1)S(1)} %collective-permute-done.8.tiles_ref, bf16[8,256,256]{2,1,0:T(8,128)(2,1)S(1)} %copy-done, ...), custom_call_target="tpu_custom_call", output_to_operand_aliasing={{}: (4, {})} | custom-call | tf_op jit(solution)/shard_map/edge_sums_last/pallas_call | solution.py:305
  (14 shorter events, 0.0 us)
Async XLA Ops:
  3.0 20.2 %collective-permute-start.2 = (bf16[10,128,128]{2,1,0:T(8,128)(2,1)S(1)}, bf16[10,128,128]{2,1,0:T(8,128)(2,1)S(1)}, u32[]{:S(2)}, u32[]{:S(2)}) collective-permute-start(bf16[10,128,128]{2,1,0:T(8,128)(2,1)S(1)} %get-tuple-element.28), channel_id=1, source_target_pairs={{0,4},{4,0},{8,12},{12,8},{16,20},{20,16},{24,28},{28,24},{1,5},{5... | collective-permute-start | bytes 983048 | tf_op jit(solution)/shard_map/ppermute | solution.py:275
  7.8 7.0 %copy-start.1 = (bf16[128,192]{1,0:T(8,128)(2,1)S(1)}, bf16[128,192]{1,0:T(8,128)(2,1)}, u32[]{:S(2)}) copy-start(bf16[128,192]{1,0:T(8,128)(2,1)} %constant.11.clone.lat_ref) | copy-start | bytes 147460
  7.8 7.0 %copy-start.2 = (bf16[256,256]{1,0:T(8,128)(2,1)S(1)}, bf16[256,256]{1,0:T(8,128)(2,1)}, u32[]{:S(2)}) copy-start(bf16[256,256]{1,0:T(8,128)(2,1)} %constant.8.clone.center_ref) | copy-start | bytes 393220
  7.8 15.3 %collective-permute-start.3 = (bf16[9,128,128]{2,1,0:T(8,128)(2,1)S(1)}, bf16[9,128,128]{2,1,0:T(8,128)(2,1)S(1)}, u32[]{:S(2)}, u32[]{:S(2)}) collective-permute-start(bf16[9,128,128]{2,1,0:T(8,128)(2,1)S(1)} %get-tuple-element.29), channel_id=1, source_target_pairs={{0,4},{4,0},{8,12},{12,8},{16,20},{20,16},{24,28},{28,24},{1,5},{5... | collective-permute-start | bytes 884744 | tf_op jit(solution)/shard_map/ppermute | solution.py:275
  7.9 4.8 %collective-permute-start.6 = (bf16[19,32,128]{2,1,0:T(8,128)(2,1)S(1)}, bf16[19,32,128]{2,1,0:T(8,128)(2,1)S(1)}, u32[]{:S(2)}, u32[]{:S(2)}) collective-permute-start(bf16[19,32,128]{2,1,0:T(8,128)(2,1)S(1)} %get-tuple-element.33), channel_id=1, source_target_pairs={{0,1},{1,0},{2,3},{3,2},{4,5},{5,4},{6,7},{7,6},{8,9},{9,8},{10,11... | collective-permute-start | bytes 466952 | tf_op jit(solution)/shard_map/ppermute | solution.py:275
  8.9 9.0 %collective-permute-start.7 = (bf16[19,32,128]{2,1,0:T(8,128)(2,1)S(1)}, bf16[19,32,128]{2,1,0:T(8,128)(2,1)S(1)}, u32[]{:S(2)}, u32[]{:S(2)}) collective-permute-start(bf16[19,32,128]{2,1,0:T(8,128)(2,1)S(1)} %get-tuple-element.34), channel_id=1, source_target_pairs={{1,2},{2,1},{5,6},{6,5},{9,10},{10,9},{13,14},{14,13},{17,18},{18,... | collective-permute-start | bytes 466952 | tf_op jit(solution)/shard_map/ppermute | solution.py:285
  12.6 21.3 %collective-permute-start = (bf16[80,32,256]{2,1,0:T(8,128)(2,1)S(1)}, bf16[80,32,256]{2,1,0:T(8,128)(2,1)S(1)}, u32[]{:S(2)}, u32[]{:S(2)}) collective-permute-start(bf16[80,32,256]{2,1,0:T(8,128)(2,1)S(1)} %get-tuple-element.26), channel_id=1, source_target_pairs={{0,1},{1,0},{2,3},{3,2},{4,5},{5,4},{6,7},{7,6},{8,9},{9,8},{10,11... | collective-permute-start | bytes 3932168 | tf_op jit(solution)/shard_map/ppermute | solution.py:275
  12.7 21.3 %collective-permute-start.1 = (bf16[80,32,256]{2,1,0:T(8,128)(2,1)S(1)}, bf16[80,32,256]{2,1,0:T(8,128)(2,1)S(1)}, u32[]{:S(2)}, u32[]{:S(2)}) collective-permute-start(bf16[80,32,256]{2,1,0:T(8,128)(2,1)S(1)} %get-tuple-element.27), channel_id=1, source_target_pairs={{1,2},{2,1},{5,6},{6,5},{9,10},{10,9},{13,14},{14,13},{17,18},{18,... | collective-permute-start | bytes 3932168 | tf_op jit(solution)/shard_map/ppermute | solution.py:285
  18.3 15.6 %copy-start.3 = (bf16[2,256,256]{2,1,0:T(8,128)(2,1)S(1)}, bf16[2,256,256]{2,1,0:T(8,128)(2,1)}, u32[]{:S(2)}) copy-start(bf16[2,256,256]{2,1,0:T(8,128)(2,1)} %constant.10.clone.border_ref) | copy-start | bytes 786436
  18.4 17.3 %collective-permute-start.9 = (bf16[14,128,128]{2,1,0:T(8,128)(2,1)S(1)}, bf16[14,128,128]{2,1,0:T(8,128)(2,1)S(1)}, u32[]{:S(2)}, u32[]{:S(2)}) collective-permute-start(bf16[14,128,128]{2,1,0:T(8,128)(2,1)S(1)} %get-tuple-element.36), channel_id=1, source_target_pairs={{0,28},{4,8},{8,4},{12,16},{16,12},{20,24},{24,20},{28,0},{1,29},{... | collective-permute-start | bytes 1376264 | tf_op jit(solution)/shard_map/ppermute | solution.py:285
  23.2 1.5 %collective-permute-start.4 = (bf16[19,32,128]{2,1,0:T(8,128)(2,1)S(1)}, bf16[19,32,128]{2,1,0:T(8,128)(2,1)S(1)}, u32[]{:S(2)}, u32[]{:S(2)}) collective-permute-start(bf16[19,32,128]{2,1,0:T(8,128)(2,1)S(1)} %get-tuple-element.30), channel_id=1, source_target_pairs={{0,1},{1,0},{2,3},{3,2},{4,5},{5,4},{6,7},{7,6},{8,9},{9,8},{10,11... | collective-permute-start | bytes 466952 | tf_op jit(solution)/shard_map/ppermute | solution.py:275
  23.3 14.9 %collective-permute-start.8 = (bf16[5,128,128]{2,1,0:T(8,128)(2,1)S(1)}, bf16[5,128,128]{2,1,0:T(8,128)(2,1)S(1)}, u32[]{:S(2)}, u32[]{:S(2)}) collective-permute-start(bf16[5,128,128]{2,1,0:T(8,128)(2,1)S(1)} %get-tuple-element.35), channel_id=1, source_target_pairs={{0,28},{4,8},{8,4},{12,16},{16,12},{20,24},{24,20},{28,0},{1,29},{... | collective-permute-start | bytes 491528 | tf_op jit(solution)/shard_map/ppermute | solution.py:285
  24.7 8.9 %collective-permute-start.5 = (bf16[19,32,128]{2,1,0:T(8,128)(2,1)S(1)}, bf16[19,32,128]{2,1,0:T(8,128)(2,1)S(1)}, u32[]{:S(2)}, u32[]{:S(2)}) collective-permute-start(bf16[19,32,128]{2,1,0:T(8,128)(2,1)S(1)} %get-tuple-element.31), channel_id=1, source_target_pairs={{1,2},{2,1},{5,6},{6,5},{9,10},{10,9},{13,14},{14,13},{17,18},{18,... | collective-permute-start | bytes 466952 | tf_op jit(solution)/shard_map/ppermute | solution.py:285
  33.9 1.8 %copy-start = (bf16[8,256,256]{2,1,0:T(8,128)(2,1)S(1)}, bf16[8,256,256]{2,1,0:T(8,128)(2,1)}, u32[]{:S(2)}) copy-start(bf16[8,256,256]{2,1,0:T(8,128)(2,1)} %constant.9.clone.spread_ref) | copy-start | bytes 3145732

commit v4 on v3

v4 whole, which is shorter than its diff:
```python
import functools

import jax
import jax.numpy as jnp
import numpy as np
from jax import lax
from jax.experimental import pallas as pl
from jax.experimental.pallas import tpu as pltpu
from jax.sharding import PartitionSpec as P

HALF = 30
LANES = 128
EDGE = 32
GROUP = 17
VMEM_LIMIT = 16 * 1024 * 1024
CHUNKS = (46, 34)
BATCH = 8
HEAVY = 25_000_000_000
BF = jnp.bfloat16


def taps():
    offsets = np.arange(-HALF, HALF + 1).astype(np.float32)
    spread = np.float32(HALF)
    norm = np.sqrt(np.sum(np.exp(-offsets * offsets / (spread * spread)), dtype=np.float32))
    return (np.exp(-offsets * offsets / (2 * spread * spread)) / norm).astype(BF)


def band(block_len, margin):
    k = taps()
    out = np.zeros((block_len + 2 * margin, block_len), BF)
    for q in range(block_len):
        out[q + margin - HALF : q + margin + HALF + 1, q] = k
    return out


def lon_weights(width):
    lon = band(width, HALF)
    spread = np.zeros((8, 2 * LANES, width), BF)
    for s in range(8):
        for j in range(HALF):
            lane = HALF * s + j if s < 4 else 120 + j - 8 * (s - 4)
            if s >= 4 and not 120 <= lane < 128:
                continue
            spread[s, lane] = lon[j]
            spread[s, LANES + lane] = lon[width + HALF + j]
    return lon[HALF : HALF + width].copy(), spread


def odd(axis):
    return lax.rem(lax.axis_index(axis), 2)


def fill_select(select_ref):
    width = select_ref.shape[1]
    side = odd("lon")
    row = lax.broadcasted_iota(jnp.int32, (width, 2 * LANES), 0)
    col = lax.broadcasted_iota(jnp.int32, (width, 2 * LANES), 1)
    diff = row - col
    end_tile, start_tile = side * LANES, (1 - side) * LANES
    for s in range(8):
        shift, lo, hi = (-HALF * s, HALF * s, HALF * s + HALF) if s < 4 else (8 * (s - 4) - 120, 120, 128)
        end = (diff == width - HALF + shift - end_tile) & (col >= end_tile + lo) & (col < end_tile + hi)
        start = (diff == shift - start_tile) & (col >= start_tile + lo) & (col < start_tile + hi) & (row < HALF)
        select_ref[s] = jnp.where(end | start, 1.0, 0.0).astype(BF)


def dot(a, b):
    return jnp.dot(a, b, preferred_element_type=jnp.float32)


def units(count):
    out, first = [], 0
    while count - first >= GROUP:
        out.append((first, 4, True))
        first += GROUP
    if count > first:
        out.append((first, (count - first) // 4, False))
    return out


def tiles_of(count):
    return sum(t for _, t, _ in units(count))


def stack(ref, first, count):
    return ref[first : first + count].reshape(count * ref.shape[1], ref.shape[2])


def pack(src_ref, unit, select_ref):
    first, n, extra = unit
    rows = src_ref.shape[1]
    acc = None
    for s in range(4):
        part = dot(stack(src_ref, first + s * n, n), select_ref[s])
        acc = part if acc is None else acc + part
    if extra:
        field = src_ref[first + 4 * n]
        acc += jnp.concatenate([dot(field, select_ref[4 + t]) for t in range(n)], axis=0)
    return acc.astype(BF).reshape(n, rows, 2 * LANES)


def multiply(raw_ref, start, gvm_ref, prod_ref, count):
    for f in range(start, start + count):
        grad = gvm_ref[f % gvm_ref.shape[0]].astype(jnp.float32)
        prod_ref[f] = (raw_ref[f].astype(jnp.float32) * grad).astype(BF)


def first_kernel(
    ens_ref, grad_ref, edge_ref, inner_ref, b_ref, near_ref, far_ref, prod_ref, gvm_ref, select_ref, buf, sems
):
    grad = pltpu.make_async_copy(grad_ref, gvm_ref, sems.at[0])
    grad.start()
    copies = []
    start = 0
    for i, count in enumerate(CHUNKS):
        at = pl.ds(start, count)
        copies.append(pltpu.make_async_copy(ens_ref.at[at], buf.at[at], sems.at[1 + i]))
        copies[-1].start()
        start += count
    fill_select(select_ref)
    grad.wait()
    start = 0
    rows = prod_ref.shape[1]
    plan = all_units(CHUNKS)
    for copy, count in zip(copies, CHUNKS):
        copy.wait()
        multiply(buf, start, gvm_ref, prod_ref, count)
        for first, n, extra, tile in plan:
            if start <= first < start + count:
                tiles = pack(prod_ref, (first, n, extra), select_ref)
                at = pl.ds(tile, n)
                edge_ref[at, :EDGE] = tiles[:, :EDGE, :LANES]
                edge_ref[at, EDGE:] = tiles[:, rows - EDGE :, :LANES]
                inner_ref[at] = tiles[:, EDGE : rows - EDGE, :LANES]
                b_ref[at] = tiles[:, :, LANES:]
                emit_rows(tiles[:, :, LANES:], near_ref, far_ref, at)
        start += count


def emit_rows(v, near_ref, far_ref, at):
    up = odd("lat") == 0
    head, tail = v[:, :EDGE], v[:, v.shape[1] - EDGE :]
    near_ref[at] = jnp.where(up, tail, head)
    far_ref[at] = jnp.where(up, head, tail)


def rows_kernel(ref, *refs):
    near_ref, far_ref = refs[-2:]
    for f in range(0, ref.shape[0], 4):
        n = min(4, ref.shape[0] - f)
        emit_rows(ref[f : f + n], near_ref, far_ref, pl.ds(f, n))


def lat_field(field, low, high, lat_ref):
    return dot(lat_ref[...], jnp.concatenate([low, field, high], axis=0))


def lat_tiles(count, tile, near_ref, far_ref, lat_ref, out_ref):
    up = odd("lat") == 0
    for t in range(0, count, 2):
        n = min(2, count - t)
        field = jnp.concatenate([tile(i) for i in range(t, t + n)], axis=1)
        near, far = (jnp.concatenate([r[i] for i in range(t, t + n)], axis=1) for r in (near_ref, far_ref))
        done = lat_field(field, jnp.where(up, far, near), jnp.where(up, near, far), lat_ref).astype(BF)
        for i in range(n):
            out_ref[t + i] = done[:, i * LANES : (i + 1) * LANES]


def edge_lat_kernel(tiles_ref, near_ref, far_ref, lat_ref, after_ref, out_ref):
    del after_ref
    lat_tiles(tiles_ref.shape[0], lambda t: tiles_ref[t], near_ref, far_ref, lat_ref, out_ref)


def split_lat_kernel(edge_ref, inner_ref, near_ref, far_ref, lat_ref, after_ref, out_ref):
    del after_ref

    def tile(t):
        return jnp.concatenate([edge_ref[t, :EDGE], inner_ref[t], edge_ref[t, EDGE:]], axis=0)

    lat_tiles(edge_ref.shape[0], tile, near_ref, far_ref, lat_ref, out_ref)


def add_rows(acc_ref, start, total, rows_ref, near, center_ref, border_ref):
    low = odd("lat") if near else 1 - odd("lat")
    edge = acc_ref.shape[1] - EDGE
    at = pl.ds(pl.multiple_of((1 - low) * edge, EDGE), EDGE)
    for first in range(start, start + total, BATCH):
        count = min(BATCH, start + total - first)
        own = dot(stack(rows_ref, first, count), center_ref[...]).astype(BF)
        part = dot(border_ref[low, : count * EDGE, : count * EDGE], own)
        for i in range(count):
            acc_ref[first + i, at] += part[i * EDGE : (i + 1) * EDGE]


def own_kernel(prod_ref, center_ref, lat_ref, after_ref, acc_ref):
    del after_ref
    rows = acc_ref.shape[1]
    for f in range(0, prod_ref.shape[0], 4):
        n = min(4, prod_ref.shape[0] - f)
        own = dot(stack(prod_ref, f, n), center_ref[...]).astype(BF)
        for i in range(n):
            acc_ref[f + i] = dot(lat_ref[:, EDGE : EDGE + rows], own[i * rows : (i + 1) * rows])


def partner_kernel(near, own_ref, rows_ref, center_ref, border_ref, acc_ref):
    del own_ref
    add_rows(acc_ref, 0, acc_ref.shape[0], rows_ref, near, center_ref, border_ref)


def last_kernel(plan, acc_ref, done_ref, tiles_ref, spread_ref, *refs):
    out_ref, buf, sems = refs[-3:]
    rows, width = acc_ref.shape[1:]
    up = odd("lon") == 0
    start, skip = plan[0][0], plan[0][3]
    copies = []
    for first, n, extra, tile in plan:
        a, b = stack(done_ref, tile, n), stack(tiles_ref, tile - skip, n)
        edges = jnp.concatenate([jnp.where(up, b, a), jnp.where(up, a, b)], axis=1)
        for s in range(4):
            at = pl.ds(first + s * n, n)
            v = acc_ref[at] + dot(edges, spread_ref[s]).reshape(n, rows, width)
            buf[pl.ds(first - start + s * n, n)] = v.astype(BF)
        if extra:
            v = acc_ref[first + 4 * n]
            for t in range(n):
                v += dot(edges[t * rows : (t + 1) * rows], spread_ref[4 + t])
            buf[first - start + 4 * n] = v.astype(BF)
        count = 4 * n + extra
        from_, to = pl.ds(first - start, count), pl.ds(first, count)
        copies.append(pltpu.make_async_copy(buf.at[from_], out_ref.at[to], sems.at[len(copies)]))
        copies[-1].start()
    for c in copies:
        c.wait()


def all_units(counts):
    out, start, tile = [], 0, 0
    for count in counts:
        for first, n, extra in units(count):
            out.append((start + first, n, extra, tile))
            tile += n
        start += count
    return out


def first_partner(x, axis):
    return lax.ppermute(x, axis, [(i, i ^ 1) for i in range(lax.axis_size(axis))])


def second_partner(x, axis, periodic):
    count = lax.axis_size(axis)
    pairs = []
    for i in range(count):
        j = i + 1 if i % 2 else i - 1
        if periodic or 0 <= j < count:
            pairs.append((i, j % count))
    return lax.ppermute(x, axis, pairs)


def lat_exchange(near, far):
    return first_partner(near, "lat"), second_partner(far, "lat", False)


IN_VMEM = pl.BlockSpec(memory_space=pltpu.VMEM)
ANYWHERE = pl.BlockSpec(memory_space=pl.ANY)


def vm(x):
    return pltpu.with_memory_space_constraint(x, pltpu.VMEM)


def hbm(x):
    return pltpu.with_memory_space_constraint(x, pltpu.HBM)


def call(kernel, name, args, outs, scratch=(), specs=None, out_specs=None, aliases=None, weight=0):
    return pl.pallas_call(
        kernel,
        in_specs=specs or [IN_VMEM] * len(args),
        out_specs=out_specs or [IN_VMEM] * len(outs),
        out_shape=outs,
        scratch_shapes=list(scratch),
        input_output_aliases=aliases or {},
        compiler_params=pltpu.CompilerParams(vmem_limit_bytes=VMEM_LIMIT),
        cost_estimate=pl.CostEstimate(flops=weight, bytes_accessed=weight, transcendentals=0),
        name=name,
    )(*[vm(a) if specs is None or specs[i] is IN_VMEM else a for i, a in enumerate(args)])


def shards(ensemble, gradient):
    members, levels, rows, width = ensemble.shape
    total = members * levels
    ens = hbm(ensemble.reshape(total, rows, width))
    plan = all_units(CHUNKS)
    n_tiles = sum(n for _, n, _, _ in plan)
    center, spread = map(jnp.asarray, lon_weights(width))
    lat = band(rows, EDGE).T
    eye = np.eye(BATCH)
    border = jnp.asarray(
        np.stack([np.kron(eye, lat[rows - EDGE :, rows + EDGE :]), np.kron(eye, lat[:EDGE, :EDGE])]).astype(BF)
    )
    lat = jnp.asarray(lat.copy())

    def shape(n, r=rows, c=width):
        return pltpu.VMEM((n, r, c), BF)

    def tiles(n, r=rows):
        return shape(n, r, LANES)

    dma = pltpu.SemaphoreType.DMA
    edge, inner, second, near, far, prod = call(
        first_kernel,
        "pack_edges",
        (ens, hbm(gradient)),
        [tiles(n_tiles, 2 * EDGE), tiles(n_tiles, rows - 2 * EDGE), tiles(n_tiles)]
        + [tiles(n_tiles, EDGE)] * 2
        + [shape(total)],
        scratch=[shape(levels), shape(8, width, 2 * LANES), shape(total), dma((1 + len(CHUNKS),))],
        specs=[ANYWHERE] * 2,
    )
    edge = first_partner(edge, "lon")
    inner = first_partner(inner, "lon")
    tnear, tfar = lat_exchange(near, far)
    near, far = call(rows_kernel, "edge_rows", (prod,), [shape(total, EDGE)] * 2)
    near, far = lat_exchange(near, far)
    sums = pltpu.VMEM((total, rows, width), jnp.float32)
    (acc,) = call(own_kernel, "own_sums", (prod, center, lat, tnear), [sums])
    (second,) = call(edge_lat_kernel, "edge_lat_sums", (second, tnear, tfar, lat, acc), [tiles(n_tiles)])
    second = second_partner(second, "lon", True)

    tnear, tfar = call(rows_kernel, "tile_rows", (edge, acc), [tiles(n_tiles, EDGE)] * 2, weight=HEAVY)
    tnear, tfar = lat_exchange(tnear, tfar)
    for is_near, rows_in in ((True, near), (False, far)):
        (acc,) = call(
            functools.partial(partner_kernel, is_near),
            "near_rows" if is_near else "far_rows",
            (acc, rows_in, center, border),
            [sums],
            aliases={0: 0},
        )
    (first,) = call(split_lat_kernel, "first_lat_sums", (edge, inner, tnear, tfar, lat, acc), [tiles(n_tiles)])
    (result,) = call(
        functools.partial(last_kernel, plan),
        "edge_sums",
        (acc, first, second, spread),
        [jax.ShapeDtypeStruct((total, rows, width), BF)],
        scratch=[shape(total), dma((len(plan),))],
        out_specs=[ANYWHERE],
    )
    return result.reshape(members, levels, rows, width)


def solution(mesh):
    placed = (P(None, None, "lat", "lon"), P(None, "lat", "lon"))
    return jax.shard_map(
        shards, mesh=mesh, in_specs=placed, out_specs=P(None, None, "lat", "lon"), check_vma=False
    )
```

time: 40.1 us -> 37.7 us (0.940)
  Pallas kernels: 15.6 us -> 13.2 us
  waiting for transfers between devices: 5.55 us -> 7.43 us
  starting transfers between devices: 18.4 us -> 16.7 us
    pallas_call x10 -> x9, Pallas kernels: 15.6 us -> 13.2 us  [call(): pl.pallas_call(kernel, in_specs=specs or [IN_VMEM] * len(args), out_specs...]
    ppermute x5 -> x4, starting transfers between devices: 15.1 us -> 13.2 us  [second_partner(): return lax.ppermute(x, axis, pairs)]
    ppermute x5 -> x4, waiting for transfers between devices: 5.53 us -> 7.42 us  [second_partner(): return lax.ppermute(x, axis, pairs)]
  transfers between devices with their start and end apart: 10 -> 9, of which waited for: 1 -> 3; matrix products, arithmetic and copies ran while one was open for 0% -> 0% of each run, Pallas kernels for 28% -> 16%
where the time goes in v4:
time: 37.7 us; the launch traced here: 37.6 us
  starting transfers between devices  16.7 us (44%)
  Pallas kernels  13.2 us (35%)
  waiting for transfers between devices  7.43 us (20%)
    pallas_call x9, Pallas kernels, call(): pl.pallas_call(kernel, in_specs=specs or [IN_VMEM] * len(args), out_specs...  13.2 us
    ppermute x4, starting transfers between devices, second_partner(): return lax.ppermute(x, axis, pairs)  13.2 us
    ppermute x4, waiting for transfers between devices, second_partner(): return lax.ppermute(x, axis, pairs)  7.42 us
    ppermute x5, starting transfers between devices, first_partner(): lax.ppermute(x, axis, [(i, i ^ 1) for i in range(lax.axis_size(axis))])  3.52 us
  transfers between devices with their start and end apart: 9, of which 3 were waited for; matrix products, arithmetic and copies ran while one was open for 0% of the time, Pallas kernels for 16%

profile of v4, /device:TPU:1, one launch (start us, length us, event | category | flops | bytes accessed | tf_op | source)
XLA Modules:
  0.0 37.6 jit_solution(11560300782078767219)
XLA Ops:
  0.0 4.1 %pack_edges.1 = (bf16[19,64,128]{2,1,0:T(8,128)(2,1)S(1)}, bf16[19,64,128]{2,1,0:T(8,128)(2,1)S(1)}, bf16[19,128,128]{2,1,0:T(8,128)(2,1)S(1)}, bf16[19,32,128]{...) custom-call(bf16[80,128,256]{2,1,0:T(8,128)(2,1)} %bitcast.2, ...), custom_call_target="tpu_custom_call" | custom-call | tf_op jit(solution)/shard_map/pack_edges/pallas_call | solution.py:278
  4.1 2.1 %collective-permute-start.3 = (bf16[19,64,128]{2,1,0:T(8,128)(2,1)S(1)}, bf16[19,64,128]{2,1,0:T(8,128)(2,1)S(1)}, u32[]{:S(2)}, u32[]{:S(2)}) collective-permute-start(bf16[19,64,128]{2,1,0:T(8,128)(2,1)S(1)} %get-tuple-element.19), channel_id=1, source_target_pairs={{0,4},{4,0},{8,12},{12,8},{16,20},{20,16},{24,28},{28,24},{1,5},{5... | collective-permute-start | bytes 933896 | tf_op jit(solution)/shard_map/ppermute | solution.py:248
  6.2 1.0 %collective-permute-start = (bf16[19,32,128]{2,1,0:T(8,128)(2,1)S(1)}, bf16[19,32,128]{2,1,0:T(8,128)(2,1)S(1)}, u32[]{:S(2)}, u32[]{:S(2)}) collective-permute-start(bf16[19,32,128]{2,1,0:T(8,128)(2,1)S(1)} %get-tuple-element.16), channel_id=1, source_target_pairs={{0,1},{1,0},{2,3},{3,2},{4,5},{5,4},{6,7},{7,6},{8,9},{9,8},{10,11... | collective-permute-start | bytes 466952 | tf_op jit(solution)/shard_map/ppermute | solution.py:248
  7.2 3.0 %collective-permute-start.7 = (bf16[19,32,128]{2,1,0:T(8,128)(2,1)S(1)}, bf16[19,32,128]{2,1,0:T(8,128)(2,1)S(1)}, u32[]{:S(2)}, u32[]{:S(2)}) collective-permute-start(bf16[19,32,128]{2,1,0:T(8,128)(2,1)S(1)} %get-tuple-element.24), channel_id=1, source_target_pairs={{1,2},{2,1},{5,6},{6,5},{9,10},{10,9},{13,14},{14,13},{17,18},{18,... | collective-permute-start | bytes 466952 | tf_op jit(solution)/shard_map/ppermute | solution.py:258
  10.2 0.3 collective-permute-start.4
  10.5 0.2 edge_rows.1
  10.7 0.1 collective-permute-start.1
  10.8 0.0 collective-permute-done.after_ref.near_ref
  10.8 2.3 %collective-permute-start.2 = (bf16[80,32,256]{2,1,0:T(8,128)(2,1)S(1)}, bf16[80,32,256]{2,1,0:T(8,128)(2,1)S(1)}, u32[]{:S(2)}, u32[]{:S(2)}) collective-permute-start(bf16[80,32,256]{2,1,0:T(8,128)(2,1)S(1)} %get-tuple-element.18), channel_id=1, source_target_pairs={{1,2},{2,1},{5,6},{6,5},{9,10},{10,9},{13,14},{14,13},{17,18},{18,... | collective-permute-start | bytes 3932168 | tf_op jit(solution)/shard_map/ppermute | solution.py:258
  13.2 3.2 %own_sums.1.own_ref.refs_0_.after_ref = f32[80,128,256]{2,1,0:T(8,128)S(1)} custom-call(bf16[80,128,256]{2,1,0:T(8,128)(2,1)S(1)} %get-tuple-element.15.prod_ref.ref, bf16[256,256]{1,0:T(8,128)(2,1)S(1)} %copy-done, bf16[128,192]{1,0:T(8,128)(2,1)S(1)} %copy-done.3, bf16[19,32,128]{2,1,0:T(8,128)(2,1)S(1)} %collective-permute-done.after_ref.near_ref), custom_call_target="tpu_custom_call" | custom-call | tf_op jit(solution)/shard_map/own_sums/pallas_call | solution.py:278
  16.4 0.3 edge_lat_sums.1
  16.7 0.0 copy-start.1
  16.7 4.8 %collective-permute-start.8 = (bf16[19,128,128]{2,1,0:T(8,128)(2,1)S(1)}, bf16[19,128,128]{2,1,0:T(8,128)(2,1)S(1)}, u32[]{:S(2)}, u32[]{:S(2)}) collective-permute-start(bf16[19,128,128]{2,1,0:T(8,128)(2,1)S(1)} %edge_lat_sums.1), channel_id=1, source_target_pairs={{0,28},{4,8},{8,4},{12,16},{16,12},{20,24},{24,20},{28,0},{1,29},{... | collective-permute-start | bytes 1867784 | tf_op jit(solution)/shard_map/ppermute | solution.py:258
  21.5 0.1 tile_rows.1
  21.6 0.1 collective-permute-start.5
  21.7 3.0 %collective-permute-start.6 = (bf16[19,32,128]{2,1,0:T(8,128)(2,1)S(1)}, bf16[19,32,128]{2,1,0:T(8,128)(2,1)S(1)}, u32[]{:S(2)}, u32[]{:S(2)}) collective-permute-start(bf16[19,32,128]{2,1,0:T(8,128)(2,1)S(1)} %get-tuple-element.22), channel_id=1, source_target_pairs={{1,2},{2,1},{5,6},{6,5},{9,10},{10,9},{13,14},{14,13},{17,18},{18,... | collective-permute-start | bytes 466952 | tf_op jit(solution)/shard_map/ppermute | solution.py:258
  24.7 1.0 %near_rows.1.own_ref = f32[80,128,256]{2,1,0:T(8,128)S(1)} custom-call(f32[80,128,256]{2,1,0:T(8,128)S(1)} %own_sums.1.own_ref.refs_0_.after_ref, bf16[80,32,256]{2,1,0:T(8,128)(2,1)S(1)} %collective-permute-done.1.rows_ref, bf16[256,256]{1,0:T(8,128)(2,1)S(1)} %copy-done, bf16[2,256,256]{2,1,0:T(8,128)(2,1)S(1)} %copy-done.1), custom_call_target="tpu_custom_call", output_to_operand_aliasing={{}: (0, {})} | custom-call | tf_op jit(solution)/shard_map/near_rows/pallas_call | solution.py:278
  25.7 4.3 %collective-permute-done.2.rows_ref = bf16[80,32,256]{2,1,0:T(8,128)(2,1)S(1)} collective-permute-done((bf16[80,32,256]{2,1,0:T(8,128)(2,1)S(1)}, bf16[80,32,256]{2,1,0:T(8,128)(2,1)S(1)}, u32[]{:S(2)}, u32[]{:S(2)}) %collective-permute-start.2) | collective-permute-done | bytes 1310752 | tf_op jit(solution)/shard_map/ppermute | solution.py:258
  30.0 1.0 %far_rows.1.after_ref.acc_ref = f32[80,128,256]{2,1,0:T(8,128)S(1)} custom-call(f32[80,128,256]{2,1,0:T(8,128)S(1)} %near_rows.1.own_ref, bf16[80,32,256]{2,1,0:T(8,128)(2,1)S(1)} %collective-permute-done.2.rows_ref, bf16[256,256]{1,0:T(8,128)(2,1)S(1)} %copy-done, bf16[2,256,256]{2,1,0:T(8,128)(2,1)S(1)} %copy-done.1), custom_call_target="tpu_custom_call", output_to_operand_aliasing={{}: (0, {})} | custom-call | tf_op jit(solution)/shard_map/far_rows/pallas_call | solution.py:278
  31.1 0.0 copy-start.2
  31.1 0.6 %collective-permute-done.6.far_ref = bf16[19,32,128]{2,1,0:T(8,128)(2,1)S(1)} collective-permute-done((bf16[19,32,128]{2,1,0:T(8,128)(2,1)S(1)}, bf16[19,32,128]{2,1,0:T(8,128)(2,1)S(1)}, u32[]{:S(2)}, u32[]{:S(2)}) %collective-permute-start.6) | collective-permute-done | bytes 155680 | tf_op jit(solution)/shard_map/ppermute | solution.py:258
  31.7 0.3 first_lat_sums.1.done_ref
  32.0 2.6 %collective-permute-done.8.tiles_ref = bf16[19,128,128]{2,1,0:T(8,128)(2,1)S(1)} collective-permute-done((bf16[19,128,128]{2,1,0:T(8,128)(2,1)S(1)}, bf16[19,128,128]{2,1,0:T(8,128)(2,1)S(1)}, u32[]{:S(2)}, u32[]{:S(2)}) %collective-permute-start.8) | collective-permute-done | bytes 622624 | tf_op jit(solution)/shard_map/ppermute | solution.py:258
  34.6 3.0 %edge_sums.1 = bf16[80,128,256]{2,1,0:T(8,128)(2,1)} custom-call(f32[80,128,256]{2,1,0:T(8,128)S(1)} %far_rows.1.after_ref.acc_ref, bf16[19,128,128]{2,1,0:T(8,128)(2,1)S(1)} %first_lat_sums.1.done_ref, bf16[19,128,128]{2,1,0:T(8,128)(2,1)S(1)} %collective-permute-done.8.tiles_ref, bf16[8,256,256]{2,1,0:T(8,128)(2,1)S(1)} %copy-done.2), custom_call_target="tpu_custom_call" | custom-call | tf_op jit(solution)/shard_map/edge_sums/pallas_call | solution.py:278
  (11 shorter events, 0.0 us)
Async XLA Ops:
  0.0 13.1 %copy-start = (bf16[256,256]{1,0:T(8,128)(2,1)S(1)}, bf16[256,256]{1,0:T(8,128)(2,1)}, u32[]{:S(2)}) copy-start(bf16[256,256]{1,0:T(8,128)(2,1)} %constant.8.clone.center_ref) | copy-start | bytes 393220
  0.0 13.2 %copy-start.3 = (bf16[128,192]{1,0:T(8,128)(2,1)S(1)}, bf16[128,192]{1,0:T(8,128)(2,1)}, u32[]{:S(2)}) copy-start(bf16[128,192]{1,0:T(8,128)(2,1)} %constant.11.clone.lat_ref) | copy-start | bytes 147460
  4.1 17.4 %collective-permute-start.3 = (bf16[19,64,128]{2,1,0:T(8,128)(2,1)S(1)}, bf16[19,64,128]{2,1,0:T(8,128)(2,1)S(1)}, u32[]{:S(2)}, u32[]{:S(2)}) collective-permute-start(bf16[19,64,128]{2,1,0:T(8,128)(2,1)S(1)} %get-tuple-element.19), channel_id=1, source_target_pairs={{0,4},{4,0},{8,12},{12,8},{16,20},{20,16},{24,28},{28,24},{1,5},{5... | collective-permute-start | bytes 933896 | tf_op jit(solution)/shard_map/ppermute | solution.py:248
  6.2 4.6 %collective-permute-start = (bf16[19,32,128]{2,1,0:T(8,128)(2,1)S(1)}, bf16[19,32,128]{2,1,0:T(8,128)(2,1)S(1)}, u32[]{:S(2)}, u32[]{:S(2)}) collective-permute-start(bf16[19,32,128]{2,1,0:T(8,128)(2,1)S(1)} %get-tuple-element.16), channel_id=1, source_target_pairs={{0,1},{1,0},{2,3},{3,2},{4,5},{5,4},{6,7},{7,6},{8,9},{9,8},{10,11... | collective-permute-start | bytes 466952 | tf_op jit(solution)/shard_map/ppermute | solution.py:248
  7.2 9.2 %collective-permute-start.7 = (bf16[19,32,128]{2,1,0:T(8,128)(2,1)S(1)}, bf16[19,32,128]{2,1,0:T(8,128)(2,1)S(1)}, u32[]{:S(2)}, u32[]{:S(2)}) collective-permute-start(bf16[19,32,128]{2,1,0:T(8,128)(2,1)S(1)} %get-tuple-element.24), channel_id=1, source_target_pairs={{1,2},{2,1},{5,6},{6,5},{9,10},{10,9},{13,14},{14,13},{17,18},{18,... | collective-permute-start | bytes 466952 | tf_op jit(solution)/shard_map/ppermute | solution.py:258
  10.2 20.9 %collective-permute-start.4 = (bf16[19,64,128]{2,1,0:T(8,128)(2,1)S(1)}, bf16[19,64,128]{2,1,0:T(8,128)(2,1)S(1)}, u32[]{:S(2)}, u32[]{:S(2)}) collective-permute-start(bf16[19,64,128]{2,1,0:T(8,128)(2,1)S(1)} %get-tuple-element.20), channel_id=1, source_target_pairs={{0,4},{4,0},{8,12},{12,8},{16,20},{20,16},{24,28},{28,24},{1,5},{5... | collective-permute-start | bytes 933896 | tf_op jit(solution)/shard_map/ppermute | solution.py:248
  10.7 10.9 %collective-permute-start.1 = (bf16[80,32,256]{2,1,0:T(8,128)(2,1)S(1)}, bf16[80,32,256]{2,1,0:T(8,128)(2,1)S(1)}, u32[]{:S(2)}, u32[]{:S(2)}) collective-permute-start(bf16[80,32,256]{2,1,0:T(8,128)(2,1)S(1)} %get-tuple-element.17), channel_id=1, source_target_pairs={{0,1},{1,0},{2,3},{3,2},{4,5},{5,4},{6,7},{7,6},{8,9},{9,8},{10,11... | collective-permute-start | bytes 3932168 | tf_op jit(solution)/shard_map/ppermute | solution.py:248
  10.8 19.2 %collective-permute-start.2 = (bf16[80,32,256]{2,1,0:T(8,128)(2,1)S(1)}, bf16[80,32,256]{2,1,0:T(8,128)(2,1)S(1)}, u32[]{:S(2)}, u32[]{:S(2)}) collective-permute-start(bf16[80,32,256]{2,1,0:T(8,128)(2,1)S(1)} %get-tuple-element.18), channel_id=1, source_target_pairs={{1,2},{2,1},{5,6},{6,5},{9,10},{10,9},{13,14},{14,13},{17,18},{18,... | collective-permute-start | bytes 3932168 | tf_op jit(solution)/shard_map/ppermute | solution.py:258
  16.7 8.0 %copy-start.1 = (bf16[2,256,256]{2,1,0:T(8,128)(2,1)S(1)}, bf16[2,256,256]{2,1,0:T(8,128)(2,1)}, u32[]{:S(2)}) copy-start(bf16[2,256,256]{2,1,0:T(8,128)(2,1)} %constant.10.clone.border_ref) | copy-start | bytes 786436
  16.7 17.9 %collective-permute-start.8 = (bf16[19,128,128]{2,1,0:T(8,128)(2,1)S(1)}, bf16[19,128,128]{2,1,0:T(8,128)(2,1)S(1)}, u32[]{:S(2)}, u32[]{:S(2)}) collective-permute-start(bf16[19,128,128]{2,1,0:T(8,128)(2,1)S(1)} %edge_lat_sums.1), channel_id=1, source_target_pairs={{0,28},{4,8},{8,4},{12,16},{16,12},{20,24},{24,20},{28,0},{1,29},{... | collective-permute-start | bytes 1867784 | tf_op jit(solution)/shard_map/ppermute | solution.py:258
  21.6 9.5 %collective-permute-start.5 = (bf16[19,32,128]{2,1,0:T(8,128)(2,1)S(1)}, bf16[19,32,128]{2,1,0:T(8,128)(2,1)S(1)}, u32[]{:S(2)}, u32[]{:S(2)}) collective-permute-start(bf16[19,32,128]{2,1,0:T(8,128)(2,1)S(1)} %get-tuple-element.21), channel_id=1, source_target_pairs={{0,1},{1,0},{2,3},{3,2},{4,5},{5,4},{6,7},{7,6},{8,9},{9,8},{10,11... | collective-permute-start | bytes 466952 | tf_op jit(solution)/shard_map/ppermute | solution.py:248
  21.7 10.0 %collective-permute-start.6 = (bf16[19,32,128]{2,1,0:T(8,128)(2,1)S(1)}, bf16[19,32,128]{2,1,0:T(8,128)(2,1)S(1)}, u32[]{:S(2)}, u32[]{:S(2)}) collective-permute-start(bf16[19,32,128]{2,1,0:T(8,128)(2,1)S(1)} %get-tuple-element.22), channel_id=1, source_target_pairs={{1,2},{2,1},{5,6},{6,5},{9,10},{10,9},{13,14},{14,13},{17,18},{18,... | collective-permute-start | bytes 466952 | tf_op jit(solution)/shard_map/ppermute | solution.py:258
  31.1 3.5 %copy-start.2 = (bf16[8,256,256]{2,1,0:T(8,128)(2,1)S(1)}, bf16[8,256,256]{2,1,0:T(8,128)(2,1)}, u32[]{:S(2)}) copy-start(bf16[8,256,256]{2,1,0:T(8,128)(2,1)} %constant.9.clone.spread_ref) | copy-start | bytes 3145732

commit v5 on v4

--- a/solution.py
+++ b/solution.py
@@ -100,42 +100,48 @@
     return acc.astype(BF).reshape(n, rows, 2 * LANES)
 
 
-def multiply(raw_ref, start, gvm_ref, prod_ref, count):
-    for f in range(start, start + count):
-        grad = gvm_ref[f % gvm_ref.shape[0]].astype(jnp.float32)
-        prod_ref[f] = (raw_ref[f].astype(jnp.float32) * grad).astype(BF)
-
-
-def first_kernel(
-    ens_ref, grad_ref, edge_ref, inner_ref, b_ref, near_ref, far_ref, prod_ref, gvm_ref, select_ref, buf, sems
-):
+def product_and_pack(pieces, first, count, raw_ref, gvm_ref, select_ref, prod_ref, a_ref, b_ref):
+    for f in range(first, first + count):
+        level = f % gvm_ref.shape[0]
+        grad = jnp.concatenate([gvm_ref[level, row : row + n] for row, n in pieces], axis=0)
+        prod_ref[f] = (raw_ref[f].astype(jnp.float32) * grad.astype(jnp.float32)).astype(BF)
+    for start, n, extra, tile in all_units(CHUNKS):
+        if first <= start < first + count:
+            tiles = pack(prod_ref, (start, n, extra), select_ref)
+            a_ref[pl.ds(tile, n)] = tiles[:, :, :LANES]
+            b_ref[pl.ds(tile, n)] = tiles[:, :, LANES:]
+
+
+def edge_kernel(ens_ref, grad_ref, a_ref, b_ref, prod_ref, select_ref, gvm_ref, raw_ref, buf, sems):
+    rows = ens_ref.shape[1]
+    pieces = ((0, EDGE), (rows - EDGE, EDGE))
     grad = pltpu.make_async_copy(grad_ref, gvm_ref, sems.at[0])
+    inner = pltpu.make_async_copy(ens_ref.at[:, pl.ds(EDGE, rows - 2 * EDGE)], raw_ref, sems.at[1])
     grad.start()
     copies = []
     start = 0
-    for i, count in enumerate(CHUNKS):
+    for count in CHUNKS:
         at = pl.ds(start, count)
-        copies.append(pltpu.make_async_copy(ens_ref.at[at], buf.at[at], sems.at[1 + i]))
-        copies[-1].start()
+        for i, (row, n) in enumerate(pieces):
+            from_ref, to_ref = ens_ref.at[at, pl.ds(row, n)], buf.at[at, pl.ds(i * EDGE, n)]
+            copies.append(pltpu.make_async_copy(from_ref, to_ref, sems.at[2 + len(copies)]))
+            copies[-1].start()
         start += count
     fill_select(select_ref)
+    inner.start()
     grad.wait()
     start = 0
-    rows = prod_ref.shape[1]
-    plan = all_units(CHUNKS)
-    for copy, count in zip(copies, CHUNKS):
-        copy.wait()
-        multiply(buf, start, gvm_ref, prod_ref, count)
-        for first, n, extra, tile in plan:
-            if start <= first < start + count:
-                tiles = pack(prod_ref, (first, n, extra), select_ref)
-                at = pl.ds(tile, n)
-                edge_ref[at, :EDGE] = tiles[:, :EDGE, :LANES]
-                edge_ref[at, EDGE:] = tiles[:, rows - EDGE :, :LANES]
-                inner_ref[at] = tiles[:, EDGE : rows - EDGE, :LANES]
-                b_ref[at] = tiles[:, :, LANES:]
-                emit_rows(tiles[:, :, LANES:], near_ref, far_ref, at)
+    for i, count in enumerate(CHUNKS):
+        for copy in copies[2 * i : 2 * i + 2]:
+            copy.wait()
+        product_and_pack(pieces, start, count, buf, gvm_ref, select_ref, prod_ref, a_ref, b_ref)
         start += count
+    inner.wait()
+
+
+def inner_kernel(raw_ref, gvm_ref, select_ref, a_ref, b_ref, prod_ref):
+    pieces = ((EDGE, raw_ref.shape[1]),)
+    product_and_pack(pieces, 0, raw_ref.shape[0], raw_ref, gvm_ref, select_ref, prod_ref, a_ref, b_ref)
 
 
 def emit_rows(v, near_ref, far_ref, at):
@@ -167,12 +173,7 @@
             out_ref[t + i] = done[:, i * LANES : (i + 1) * LANES]
 
 
-def edge_lat_kernel(tiles_ref, near_ref, far_ref, lat_ref, after_ref, out_ref):
-    del after_ref
-    lat_tiles(tiles_ref.shape[0], lambda t: tiles_ref[t], near_ref, far_ref, lat_ref, out_ref)
-
-
-def split_lat_kernel(edge_ref, inner_ref, near_ref, far_ref, lat_ref, after_ref, out_ref):
+def edge_lat_kernel(edge_ref, inner_ref, near_ref, far_ref, lat_ref, after_ref, out_ref):
     del after_ref
 
     def tile(t):
@@ -193,14 +194,17 @@
             acc_ref[first + i, at] += part[i * EDGE : (i + 1) * EDGE]
 
 
-def own_kernel(prod_ref, center_ref, lat_ref, after_ref, acc_ref):
+def own_kernel(edge_ref, inner_ref, center_ref, lat_ref, after_ref, acc_ref):
     del after_ref
     rows = acc_ref.shape[1]
-    for f in range(0, prod_ref.shape[0], 4):
-        n = min(4, prod_ref.shape[0] - f)
-        own = dot(stack(prod_ref, f, n), center_ref[...]).astype(BF)
+    for f in range(0, acc_ref.shape[0], 4):
+        n = min(4, acc_ref.shape[0] - f)
+        edge, inner = (
+            dot(stack(ref, f, n), center_ref[...]).astype(BF).reshape(n, *ref.shape[1:]) for ref in (edge_ref, inner_ref)
+        )
         for i in range(n):
-            acc_ref[f + i] = dot(lat_ref[:, EDGE : EDGE + rows], own[i * rows : (i + 1) * rows])
+            own = jnp.concatenate([edge[i, :EDGE], inner[i], edge[i, EDGE:]], axis=0)
+            acc_ref[f + i] = dot(lat_ref[:, EDGE : EDGE + rows], own)
 
 
 def partner_kernel(near, own_ref, rows_ref, center_ref, border_ref, acc_ref):
@@ -208,30 +212,24 @@
     add_rows(acc_ref, 0, acc_ref.shape[0], rows_ref, near, center_ref, border_ref)
 
 
-def last_kernel(plan, acc_ref, done_ref, tiles_ref, spread_ref, *refs):
-    out_ref, buf, sems = refs[-3:]
+def last_kernel(plan, acc_ref, done_ref, tiles_ref, spread_ref, out_ref, buf, sem):
     rows, width = acc_ref.shape[1:]
     up = odd("lon") == 0
-    start, skip = plan[0][0], plan[0][3]
-    copies = []
+
+    def emit(first, n, v):
+        at = pl.ds(first, n)
+        buf[at] = (acc_ref[at].astype(jnp.float32) + v.reshape(n, rows, width)).astype(BF)
+        pltpu.make_async_copy(buf.at[at], out_ref.at[at], sem).start()
+
     for first, n, extra, tile in plan:
-        a, b = stack(done_ref, tile, n), stack(tiles_ref, tile - skip, n)
+        a, b = stack(done_ref, tile, n), stack(tiles_ref, tile, n)
         edges = jnp.concatenate([jnp.where(up, b, a), jnp.where(up, a, b)], axis=1)
         for s in range(4):
-            at = pl.ds(first + s * n, n)
-            v = acc_ref[at] + dot(edges, spread_ref[s]).reshape(n, rows, width)
-            buf[pl.ds(first - start + s * n, n)] = v.astype(BF)
+            emit(first + s * n, n, dot(edges, spread_ref[s]))
         if extra:
-            v = acc_ref[first + 4 * n]
-            for t in range(n):
-                v += dot(edges[t * rows : (t + 1) * rows], spread_ref[4 + t])
-            buf[first - start + 4 * n] = v.astype(BF)
-        count = 4 * n + extra
-        from_, to = pl.ds(first - start, count), pl.ds(first, count)
-        copies.append(pltpu.make_async_copy(buf.at[from_], out_ref.at[to], sems.at[len(copies)]))
-        copies[-1].start()
-    for c in copies:
-        c.wait()
+            parts = [dot(edges[t * rows : (t + 1) * rows], spread_ref[4 + t]) for t in range(n)]
+            emit(first + 4 * n, 1, sum(parts[1:], parts[0]))
+    pltpu.make_async_copy(buf, out_ref, sem).wait()
 
 
 def all_units(counts):
@@ -309,25 +307,38 @@
         return shape(n, r, LANES)
 
     dma = pltpu.SemaphoreType.DMA
-    edge, inner, second, near, far, prod = call(
-        first_kernel,
-        "pack_edges",
+    between = rows - 2 * EDGE
+    edge, b_edge, prod_edge, select, grad, raw = call(
+        edge_kernel,
+        "pack_edge_rows",
         (ens, hbm(gradient)),
-        [tiles(n_tiles, 2 * EDGE), tiles(n_tiles, rows - 2 * EDGE), tiles(n_tiles)]
-        + [tiles(n_tiles, EDGE)] * 2
-        + [shape(total)],
-        scratch=[shape(levels), shape(8, width, 2 * LANES), shape(total), dma((1 + len(CHUNKS),))],
+        [
+            tiles(n_tiles, 2 * EDGE),
+            tiles(n_tiles, 2 * EDGE),
+            shape(total, 2 * EDGE),
+            shape(8, width, 2 * LANES),
+            shape(levels),
+            shape(total, between),
+        ],
+        scratch=[shape(total, 2 * EDGE), dma((2 + 2 * len(CHUNKS),))],
         specs=[ANYWHERE] * 2,
     )
     edge = first_partner(edge, "lon")
+    near, far = call(rows_kernel, "packed_rows", (b_edge,), [tiles(n_tiles, EDGE)] * 2)
+    tnear, tfar = lat_exchange(near, far)
+    inner, b_inner, prod_inner = call(
+        inner_kernel,
+        "pack_inner_rows",
+        (raw, grad, select),
+        [tiles(n_tiles, between), tiles(n_tiles, between), shape(total, between)],
+    )
     inner = first_partner(inner, "lon")
-    tnear, tfar = lat_exchange(near, far)
-    near, far = call(rows_kernel, "edge_rows", (prod,), [shape(total, EDGE)] * 2)
+    near, far = call(rows_kernel, "edge_rows", (prod_edge, b_inner), [shape(total, EDGE)] * 2)
     near, far = lat_exchange(near, far)
     sums = pltpu.VMEM((total, rows, width), jnp.float32)
-    (acc,) = call(own_kernel, "own_sums", (prod, center, lat, tnear), [sums])
-    (second,) = call(edge_lat_kernel, "edge_lat_sums", (second, tnear, tfar, lat, acc), [tiles(n_tiles)])
-    second = second_partner(second, "lon", True)
+    (payload,) = call(edge_lat_kernel, "edge_lat_sums", (b_edge, b_inner, tnear, tfar, lat, tnear), [tiles(n_tiles)])
+    (acc,) = call(own_kernel, "own_sums", (prod_edge, prod_inner, center, lat, edge), [sums])
+    second = second_partner(payload, "lon", True)
 
     tnear, tfar = call(rows_kernel, "tile_rows", (edge, acc), [tiles(n_tiles, EDGE)] * 2, weight=HEAVY)
     tnear, tfar = lat_exchange(tnear, tfar)
@@ -339,13 +350,13 @@
             [sums],
             aliases={0: 0},
         )
-    (first,) = call(split_lat_kernel, "first_lat_sums", (edge, inner, tnear, tfar, lat, acc), [tiles(n_tiles)])
+    (first,) = call(edge_lat_kernel, "first_lat_sums", (edge, inner, tnear, tfar, lat, acc), [tiles(n_tiles)])
     (result,) = call(
         functools.partial(last_kernel, plan),
         "edge_sums",
         (acc, first, second, spread),
         [jax.ShapeDtypeStruct((total, rows, width), BF)],
-        scratch=[shape(total), dma((len(plan),))],
+        scratch=[shape(total), dma],
         out_specs=[ANYWHERE],
     )
     return result.reshape(members, levels, rows, width)

time: 37.7 us -> 36.5 us (0.968); the launches traced: 37.6 us -> 36 us
  waiting for transfers between devices: 7.43 us -> 3.7 us
  Pallas kernels: 13.2 us -> 14.9 us
    ppermute x4, waiting for transfers between devices: 7.42 us -> 2.25 us  [second_partner(): return lax.ppermute(x, axis, pairs)]
    pallas_call x9 -> x11, Pallas kernels: 13.2 us -> 14.9 us  [call(): pl.pallas_call(kernel, in_specs=specs or [IN_VMEM] * len(args), out_specs...]
    ppermute x5, waiting for transfers between devices: 0.01 us -> 1.45 us  [first_partner(): lax.ppermute(x, axis, [(i, i ^ 1) for i in range(lax.axis_size(axis))])]
  transfers between devices with their start and end apart: 9 -> 9, of which waited for: 3 -> 2; matrix products, arithmetic and copies ran while one was open for 0% -> 0% of each run, Pallas kernels for 16% -> 26%
where the time goes in v5:
time: 36.5 us; the launch traced here: 36 us
  starting transfers between devices  17 us (47%)
  Pallas kernels  14.9 us (41%)
  waiting for transfers between devices  3.7 us (10%)
    pallas_call x11, Pallas kernels, call(): pl.pallas_call(kernel, in_specs=specs or [IN_VMEM] * len(args), out_specs...  14.9 us
    ppermute x4, starting transfers between devices, second_partner(): return lax.ppermute(x, axis, pairs)  13.4 us
    ppermute x5, starting transfers between devices, first_partner(): lax.ppermute(x, axis, [(i, i ^ 1) for i in range(lax.axis_size(axis))])  3.6 us
    ppermute x4, waiting for transfers between devices, second_partner(): return lax.ppermute(x, axis, pairs)  2.25 us
    ppermute x5, waiting for transfers between devices, first_partner(): lax.ppermute(x, axis, [(i, i ^ 1) for i in range(lax.axis_size(axis))])  1.45 us
  transfers between devices with their start and end apart: 9, of which 2 were waited for; matrix products, arithmetic and copies ran while one was open for 0% of the time, Pallas kernels for 26%

profile of v5, /device:TPU:1, one launch (start us, length us, event | category | flops | bytes accessed | tf_op | source)
XLA Modules:
  0.0 36.0 jit_solution(6297372530321220014)
XLA Ops:
  0.0 2.9 %pack_edge_rows.1 = (bf16[19,64,128]{2,1,0:T(8,128)(2,1)S(1)}, bf16[19,64,128]{2,1,0:T(8,128)(2,1)S(1)}, bf16[80,64,256]{2,1,0:T(8,128)(2,1)S(1)}, bf16[8,256,25...) custom-call(bf16[80,128,256]{2,1,0:T(8,128)(2,1)} %bitcast.2, ...), custom_call_target="tpu_custom_call" | custom-call | tf_op jit(solution)/shard_map/pack_edge_rows/pallas_call | solution.py:276
  2.9 2.1 %collective-permute-start = (bf16[19,64,128]{2,1,0:T(8,128)(2,1)S(1)}, bf16[19,64,128]{2,1,0:T(8,128)(2,1)S(1)}, u32[]{:S(2)}, u32[]{:S(2)}) collective-permute-start(bf16[19,64,128]{2,1,0:T(8,128)(2,1)S(1)} %get-tuple-element.25), channel_id=1, source_target_pairs={{0,4},{4,0},{8,12},{12,8},{16,20},{20,16},{24,28},{28,24},{1,5},{5... | collective-permute-start | bytes 933896 | tf_op jit(solution)/shard_map/ppermute | solution.py:246
  5.0 0.1 packed_rows.1
  5.0 1.0 %collective-permute-start.6 = (bf16[19,32,128]{2,1,0:T(8,128)(2,1)S(1)}, bf16[19,32,128]{2,1,0:T(8,128)(2,1)S(1)}, u32[]{:S(2)}, u32[]{:S(2)}) collective-permute-start(bf16[19,32,128]{2,1,0:T(8,128)(2,1)S(1)} %get-tuple-element.33), channel_id=1, source_target_pairs={{0,1},{1,0},{2,3},{3,2},{4,5},{5,4},{6,7},{7,6},{8,9},{9,8},{10,11... | collective-permute-start | bytes 466952 | tf_op jit(solution)/shard_map/ppermute | solution.py:246
  6.1 3.0 %collective-permute-start.7 = (bf16[19,32,128]{2,1,0:T(8,128)(2,1)S(1)}, bf16[19,32,128]{2,1,0:T(8,128)(2,1)S(1)}, u32[]{:S(2)}, u32[]{:S(2)}) collective-permute-start(bf16[19,32,128]{2,1,0:T(8,128)(2,1)S(1)} %get-tuple-element.34), channel_id=1, source_target_pairs={{1,2},{2,1},{5,6},{6,5},{9,10},{10,9},{13,14},{14,13},{17,18},{18,... | collective-permute-start | bytes 466952 | tf_op jit(solution)/shard_map/ppermute | solution.py:256
  9.1 0.0 copy-start.3
  9.1 1.2 %pack_inner_rows.1 = (bf16[19,64,128]{2,1,0:T(8,128)(2,1)S(1)}, bf16[19,64,128]{2,1,0:T(8,128)(2,1)S(1)}, bf16[80,64,256]{2,1,0:T(8,128)(2,1)S(1)}) custom-call(bf16[80,64,256]{2,1,0:T(8,128)(2,1)S(1)} %get-tuple-element.21.raw_ref, bf16[2,128,256]{2,1,0:T(8,128)(2,1)S(1)} %get-tuple-element.22.gvm_ref, bf16[8,256,256]{2,1,0:T(8,128)(2,1)S(1)} %get-tuple-element.23.select_ref), custom_call_target="tpu_custom_call" | custom-call | tf_op jit(solution)/shard_map/pack_inner_rows/pallas_call | solution.py:276
  10.3 0.0 copy-start
  10.3 0.3 collective-permute-start.3
  10.7 0.2 edge_rows.1
  10.8 0.1 collective-permute-start.1
  10.9 2.3 %collective-permute-start.2 = (bf16[80,32,256]{2,1,0:T(8,128)(2,1)S(1)}, bf16[80,32,256]{2,1,0:T(8,128)(2,1)S(1)}, u32[]{:S(2)}, u32[]{:S(2)}) collective-permute-start(bf16[80,32,256]{2,1,0:T(8,128)(2,1)S(1)} %get-tuple-element.28), channel_id=1, source_target_pairs={{1,2},{2,1},{5,6},{6,5},{9,10},{10,9},{13,14},{14,13},{17,18},{18,... | collective-permute-start | bytes 3932168 | tf_op jit(solution)/shard_map/ppermute | solution.py:256
  13.2 0.3 edge_lat_sums.1
  13.6 4.8 %collective-permute-start.8 = (bf16[19,128,128]{2,1,0:T(8,128)(2,1)S(1)}, bf16[19,128,128]{2,1,0:T(8,128)(2,1)S(1)}, u32[]{:S(2)}, u32[]{:S(2)}) collective-permute-start(bf16[19,128,128]{2,1,0:T(8,128)(2,1)S(1)} %edge_lat_sums.1), channel_id=1, source_target_pairs={{0,28},{4,8},{8,4},{12,16},{16,12},{20,24},{24,20},{28,0},{1,29},{... | collective-permute-start | bytes 1867784 | tf_op jit(solution)/shard_map/ppermute | solution.py:256
  18.4 5.1 %own_sums.1.own_ref.refs_0_ = f32[80,128,256]{2,1,0:T(8,128)S(1)} custom-call(bf16[80,64,256]{2,1,0:T(8,128)(2,1)S(1)} %get-tuple-element.20.edge_ref.ref, bf16[80,64,256]{2,1,0:T(8,128)(2,1)S(1)} %get-tuple-element.24.inner_ref, bf16[256,256]{1,0:T(8,128)(2,1)S(1)} %copy-done, bf16[128,192]{1,0:T(8,128)(2,1)S(1)} %copy-done.3, ...), custom_call_target="tpu_custom_call" | custom-call | tf_op jit(solution)/shard_map/own_sums/pallas_call | solution.py:276
  23.5 0.1 tile_rows.1
  23.6 0.1 collective-permute-start.4
  23.6 3.2 %collective-permute-start.5 = (bf16[19,32,128]{2,1,0:T(8,128)(2,1)S(1)}, bf16[19,32,128]{2,1,0:T(8,128)(2,1)S(1)}, u32[]{:S(2)}, u32[]{:S(2)}) collective-permute-start(bf16[19,32,128]{2,1,0:T(8,128)(2,1)S(1)} %get-tuple-element.31), channel_id=1, source_target_pairs={{1,2},{2,1},{5,6},{6,5},{9,10},{10,9},{13,14},{14,13},{17,18},{18,... | collective-permute-start | bytes 466952 | tf_op jit(solution)/shard_map/ppermute | solution.py:256
  26.9 1.0 %near_rows.1.own_ref = f32[80,128,256]{2,1,0:T(8,128)S(1)} custom-call(f32[80,128,256]{2,1,0:T(8,128)S(1)} %own_sums.1.own_ref.refs_0_, bf16[80,32,256]{2,1,0:T(8,128)(2,1)S(1)} %collective-permute-done.1.rows_ref, bf16[256,256]{1,0:T(8,128)(2,1)S(1)} %copy-done, bf16[2,256,256]{2,1,0:T(8,128)(2,1)S(1)} %copy-done.1), custom_call_target="tpu_custom_call", output_to_operand_aliasing={{}: (0, {})} | custom-call | tf_op jit(solution)/shard_map/near_rows/pallas_call | solution.py:276
  27.9 2.2 %collective-permute-done.2.rows_ref = bf16[80,32,256]{2,1,0:T(8,128)(2,1)S(1)} collective-permute-done((bf16[80,32,256]{2,1,0:T(8,128)(2,1)S(1)}, bf16[80,32,256]{2,1,0:T(8,128)(2,1)S(1)}, u32[]{:S(2)}, u32[]{:S(2)}) %collective-permute-start.2) | collective-permute-done | bytes 1310752 | tf_op jit(solution)/shard_map/ppermute | solution.py:256
  30.2 1.0 %far_rows.1.after_ref.acc_ref = f32[80,128,256]{2,1,0:T(8,128)S(1)} custom-call(f32[80,128,256]{2,1,0:T(8,128)S(1)} %near_rows.1.own_ref, bf16[80,32,256]{2,1,0:T(8,128)(2,1)S(1)} %collective-permute-done.2.rows_ref, bf16[256,256]{1,0:T(8,128)(2,1)S(1)} %copy-done, bf16[2,256,256]{2,1,0:T(8,128)(2,1)S(1)} %copy-done.1), custom_call_target="tpu_custom_call", output_to_operand_aliasing={{}: (0, {})} | custom-call | tf_op jit(solution)/shard_map/far_rows/pallas_call | solution.py:276
  31.2 1.4 %collective-permute-done.3.inner_ref = bf16[19,64,128]{2,1,0:T(8,128)(2,1)S(1)} collective-permute-done((bf16[19,64,128]{2,1,0:T(8,128)(2,1)S(1)}, bf16[19,64,128]{2,1,0:T(8,128)(2,1)S(1)}, u32[]{:S(2)}, u32[]{:S(2)}) %collective-permute-start.3) | collective-permute-done | bytes 311328 | tf_op jit(solution)/shard_map/ppermute | solution.py:246
  32.6 0.3 first_lat_sums.1.done_ref
  33.0 2.8 %edge_sums.1 = bf16[80,128,256]{2,1,0:T(8,128)(2,1)} custom-call(f32[80,128,256]{2,1,0:T(8,128)S(1)} %far_rows.1.after_ref.acc_ref, bf16[19,128,128]{2,1,0:T(8,128)(2,1)S(1)} %first_lat_sums.1.done_ref, bf16[19,128,128]{2,1,0:T(8,128)(2,1)S(1)} %collective-permute-done.8.tiles_ref, bf16[8,256,256]{2,1,0:T(8,128)(2,1)S(1)} %copy-done.2), custom_call_target="tpu_custom_call" | custom-call | tf_op jit(solution)/shard_map/edge_sums/pallas_call | solution.py:276
  (13 shorter events, 0.0 us)
Async XLA Ops:
  2.9 15.5 %collective-permute-start = (bf16[19,64,128]{2,1,0:T(8,128)(2,1)S(1)}, bf16[19,64,128]{2,1,0:T(8,128)(2,1)S(1)}, u32[]{:S(2)}, u32[]{:S(2)}) collective-permute-start(bf16[19,64,128]{2,1,0:T(8,128)(2,1)S(1)} %get-tuple-element.25), channel_id=1, source_target_pairs={{0,4},{4,0},{8,12},{12,8},{16,20},{20,16},{24,28},{28,24},{1,5},{5... | collective-permute-start | bytes 933896 | tf_op jit(solution)/shard_map/ppermute | solution.py:246
  5.0 5.9 %collective-permute-start.6 = (bf16[19,32,128]{2,1,0:T(8,128)(2,1)S(1)}, bf16[19,32,128]{2,1,0:T(8,128)(2,1)S(1)}, u32[]{:S(2)}, u32[]{:S(2)}) collective-permute-start(bf16[19,32,128]{2,1,0:T(8,128)(2,1)S(1)} %get-tuple-element.33), channel_id=1, source_target_pairs={{0,1},{1,0},{2,3},{3,2},{4,5},{5,4},{6,7},{7,6},{8,9},{9,8},{10,11... | collective-permute-start | bytes 466952 | tf_op jit(solution)/shard_map/ppermute | solution.py:246
  6.1 7.2 %collective-permute-start.7 = (bf16[19,32,128]{2,1,0:T(8,128)(2,1)S(1)}, bf16[19,32,128]{2,1,0:T(8,128)(2,1)S(1)}, u32[]{:S(2)}, u32[]{:S(2)}) collective-permute-start(bf16[19,32,128]{2,1,0:T(8,128)(2,1)S(1)} %get-tuple-element.34), channel_id=1, source_target_pairs={{1,2},{2,1},{5,6},{6,5},{9,10},{10,9},{13,14},{14,13},{17,18},{18,... | collective-permute-start | bytes 466952 | tf_op jit(solution)/shard_map/ppermute | solution.py:256
  9.1 4.1 %copy-start.3 = (bf16[128,192]{1,0:T(8,128)(2,1)S(1)}, bf16[128,192]{1,0:T(8,128)(2,1)}, u32[]{:S(2)}) copy-start(bf16[128,192]{1,0:T(8,128)(2,1)} %constant.11.clone.lat_ref) | copy-start | bytes 147460
  10.3 8.1 %copy-start = (bf16[256,256]{1,0:T(8,128)(2,1)S(1)}, bf16[256,256]{1,0:T(8,128)(2,1)}, u32[]{:S(2)}) copy-start(bf16[256,256]{1,0:T(8,128)(2,1)} %constant.8.clone.center_ref) | copy-start | bytes 393220
  10.3 22.3 %collective-permute-start.3 = (bf16[19,64,128]{2,1,0:T(8,128)(2,1)S(1)}, bf16[19,64,128]{2,1,0:T(8,128)(2,1)S(1)}, u32[]{:S(2)}, u32[]{:S(2)}) collective-permute-start(bf16[19,64,128]{2,1,0:T(8,128)(2,1)S(1)} %get-tuple-element.29), channel_id=1, source_target_pairs={{0,4},{4,0},{8,12},{12,8},{16,20},{20,16},{24,28},{28,24},{1,5},{5... | collective-permute-start | bytes 933896 | tf_op jit(solution)/shard_map/ppermute | solution.py:246
  10.8 12.8 %collective-permute-start.1 = (bf16[80,32,256]{2,1,0:T(8,128)(2,1)S(1)}, bf16[80,32,256]{2,1,0:T(8,128)(2,1)S(1)}, u32[]{:S(2)}, u32[]{:S(2)}) collective-permute-start(bf16[80,32,256]{2,1,0:T(8,128)(2,1)S(1)} %get-tuple-element.27), channel_id=1, source_target_pairs={{0,1},{1,0},{2,3},{3,2},{4,5},{5,4},{6,7},{7,6},{8,9},{9,8},{10,11... | collective-permute-start | bytes 3932168 | tf_op jit(solution)/shard_map/ppermute | solution.py:246
  10.9 19.2 %collective-permute-start.2 = (bf16[80,32,256]{2,1,0:T(8,128)(2,1)S(1)}, bf16[80,32,256]{2,1,0:T(8,128)(2,1)S(1)}, u32[]{:S(2)}, u32[]{:S(2)}) collective-permute-start(bf16[80,32,256]{2,1,0:T(8,128)(2,1)S(1)} %get-tuple-element.28), channel_id=1, source_target_pairs={{1,2},{2,1},{5,6},{6,5},{9,10},{10,9},{13,14},{14,13},{17,18},{18,... | collective-permute-start | bytes 3932168 | tf_op jit(solution)/shard_map/ppermute | solution.py:256
  13.6 19.4 %collective-permute-start.8 = (bf16[19,128,128]{2,1,0:T(8,128)(2,1)S(1)}, bf16[19,128,128]{2,1,0:T(8,128)(2,1)S(1)}, u32[]{:S(2)}, u32[]{:S(2)}) collective-permute-start(bf16[19,128,128]{2,1,0:T(8,128)(2,1)S(1)} %edge_lat_sums.1), channel_id=1, source_target_pairs={{0,28},{4,8},{8,4},{12,16},{16,12},{20,24},{24,20},{28,0},{1,29},{... | collective-permute-start | bytes 1867784 | tf_op jit(solution)/shard_map/ppermute | solution.py:256
  23.5 3.4 %copy-start.1 = (bf16[2,256,256]{2,1,0:T(8,128)(2,1)S(1)}, bf16[2,256,256]{2,1,0:T(8,128)(2,1)}, u32[]{:S(2)}) copy-start(bf16[2,256,256]{2,1,0:T(8,128)(2,1)} %constant.10.clone.border_ref) | copy-start | bytes 786436
  23.6 9.1 %collective-permute-start.4 = (bf16[19,32,128]{2,1,0:T(8,128)(2,1)S(1)}, bf16[19,32,128]{2,1,0:T(8,128)(2,1)S(1)}, u32[]{:S(2)}, u32[]{:S(2)}) collective-permute-start(bf16[19,32,128]{2,1,0:T(8,128)(2,1)S(1)} %get-tuple-element.30), channel_id=1, source_target_pairs={{0,1},{1,0},{2,3},{3,2},{4,5},{5,4},{6,7},{7,6},{8,9},{9,8},{10,11... | collective-permute-start | bytes 466952 | tf_op jit(solution)/shard_map/ppermute | solution.py:246
  23.6 9.0 %collective-permute-start.5 = (bf16[19,32,128]{2,1,0:T(8,128)(2,1)S(1)}, bf16[19,32,128]{2,1,0:T(8,128)(2,1)S(1)}, u32[]{:S(2)}, u32[]{:S(2)}) collective-permute-start(bf16[19,32,128]{2,1,0:T(8,128)(2,1)S(1)} %get-tuple-element.31), channel_id=1, source_target_pairs={{1,2},{2,1},{5,6},{6,5},{9,10},{10,9},{13,14},{14,13},{17,18},{18,... | collective-permute-start | bytes 466952 | tf_op jit(solution)/shard_map/ppermute | solution.py:256
  31.2 1.8 %copy-start.2 = (bf16[8,256,256]{2,1,0:T(8,128)(2,1)S(1)}, bf16[8,256,256]{2,1,0:T(8,128)(2,1)}, u32[]{:S(2)}) copy-start(bf16[8,256,256]{2,1,0:T(8,128)(2,1)} %constant.9.clone.spread_ref) | copy-start | bytes 3145732

commit v6 on v5

--- a/solution.py
+++ b/solution.py
@@ -352,7 +352,7 @@
         )
     (first,) = call(edge_lat_kernel, "first_lat_sums", (edge, inner, tnear, tfar, lat, acc), [tiles(n_tiles)])
     (result,) = call(
-        functools.partial(last_kernel, plan),
+        functools.partial(last_kernel, sorted(plan, key=lambda unit: unit[1])),
         "edge_sums",
         (acc, first, second, spread),
         [jax.ShapeDtypeStruct((total, rows, width), BF)],

time: 36.5 us -> 36.5 us (level)
  no operation moved by 1% of the time
where the time goes in v6:
time: 36.5 us; the launch traced here: 36 us
  starting transfers between devices  17 us (47%)
  Pallas kernels  14.9 us (41%)
  waiting for transfers between devices  3.7 us (10%)
    pallas_call x11, Pallas kernels, call(): pl.pallas_call(kernel, in_specs=specs or [IN_VMEM] * len(args), out_specs...  14.9 us
    ppermute x4, starting transfers between devices, second_partner(): return lax.ppermute(x, axis, pairs)  13.4 us
    ppermute x5, starting transfers between devices, first_partner(): lax.ppermute(x, axis, [(i, i ^ 1) for i in range(lax.axis_size(axis))])  3.6 us
    ppermute x4, waiting for transfers between devices, second_partner(): return lax.ppermute(x, axis, pairs)  2.25 us
    ppermute x5, waiting for transfers between devices, first_partner(): lax.ppermute(x, axis, [(i, i ^ 1) for i in range(lax.axis_size(axis))])  1.45 us
  transfers between devices with their start and end apart: 9, of which 2 were waited for; matrix products, arithmetic and copies ran while one was open for 0% of the time, Pallas kernels for 26%

profile of v6, /device:TPU:1, one launch (start us, length us, event | category | flops | bytes accessed | tf_op | source)
XLA Modules:
  0.0 36.0 jit_solution(11187961019823346288)
XLA Ops:
  0.0 2.9 %pack_edge_rows.1 = (bf16[19,64,128]{2,1,0:T(8,128)(2,1)S(1)}, bf16[19,64,128]{2,1,0:T(8,128)(2,1)S(1)}, bf16[80,64,256]{2,1,0:T(8,128)(2,1)S(1)}, bf16[8,256,25...) custom-call(bf16[80,128,256]{2,1,0:T(8,128)(2,1)} %bitcast.2, ...), custom_call_target="tpu_custom_call" | custom-call | tf_op jit(solution)/shard_map/pack_edge_rows/pallas_call | solution.py:276
  2.9 2.1 %collective-permute-start = (bf16[19,64,128]{2,1,0:T(8,128)(2,1)S(1)}, bf16[19,64,128]{2,1,0:T(8,128)(2,1)S(1)}, u32[]{:S(2)}, u32[]{:S(2)}) collective-permute-start(bf16[19,64,128]{2,1,0:T(8,128)(2,1)S(1)} %get-tuple-element.25), channel_id=1, source_target_pairs={{0,4},{4,0},{8,12},{12,8},{16,20},{20,16},{24,28},{28,24},{1,5},{5... | collective-permute-start | bytes 933896 | tf_op jit(solution)/shard_map/ppermute | solution.py:246
  5.0 0.1 packed_rows.1
  5.0 1.0 %collective-permute-start.6 = (bf16[19,32,128]{2,1,0:T(8,128)(2,1)S(1)}, bf16[19,32,128]{2,1,0:T(8,128)(2,1)S(1)}, u32[]{:S(2)}, u32[]{:S(2)}) collective-permute-start(bf16[19,32,128]{2,1,0:T(8,128)(2,1)S(1)} %get-tuple-element.33), channel_id=1, source_target_pairs={{0,1},{1,0},{2,3},{3,2},{4,5},{5,4},{6,7},{7,6},{8,9},{9,8},{10,11... | collective-permute-start | bytes 466952 | tf_op jit(solution)/shard_map/ppermute | solution.py:246
  6.1 3.0 %collective-permute-start.7 = (bf16[19,32,128]{2,1,0:T(8,128)(2,1)S(1)}, bf16[19,32,128]{2,1,0:T(8,128)(2,1)S(1)}, u32[]{:S(2)}, u32[]{:S(2)}) collective-permute-start(bf16[19,32,128]{2,1,0:T(8,128)(2,1)S(1)} %get-tuple-element.34), channel_id=1, source_target_pairs={{1,2},{2,1},{5,6},{6,5},{9,10},{10,9},{13,14},{14,13},{17,18},{18,... | collective-permute-start | bytes 466952 | tf_op jit(solution)/shard_map/ppermute | solution.py:256
  9.1 0.0 copy-start.3
  9.1 1.2 %pack_inner_rows.1 = (bf16[19,64,128]{2,1,0:T(8,128)(2,1)S(1)}, bf16[19,64,128]{2,1,0:T(8,128)(2,1)S(1)}, bf16[80,64,256]{2,1,0:T(8,128)(2,1)S(1)}) custom-call(bf16[80,64,256]{2,1,0:T(8,128)(2,1)S(1)} %get-tuple-element.21.raw_ref, bf16[2,128,256]{2,1,0:T(8,128)(2,1)S(1)} %get-tuple-element.22.gvm_ref, bf16[8,256,256]{2,1,0:T(8,128)(2,1)S(1)} %get-tuple-element.23.select_ref), custom_call_target="tpu_custom_call" | custom-call | tf_op jit(solution)/shard_map/pack_inner_rows/pallas_call | solution.py:276
  10.3 0.0 copy-start
  10.3 0.3 collective-permute-start.3
  10.7 0.2 edge_rows.1
  10.8 0.1 collective-permute-start.1
  10.9 2.3 %collective-permute-start.2 = (bf16[80,32,256]{2,1,0:T(8,128)(2,1)S(1)}, bf16[80,32,256]{2,1,0:T(8,128)(2,1)S(1)}, u32[]{:S(2)}, u32[]{:S(2)}) collective-permute-start(bf16[80,32,256]{2,1,0:T(8,128)(2,1)S(1)} %get-tuple-element.28), channel_id=1, source_target_pairs={{1,2},{2,1},{5,6},{6,5},{9,10},{10,9},{13,14},{14,13},{17,18},{18,... | collective-permute-start | bytes 3932168 | tf_op jit(solution)/shard_map/ppermute | solution.py:256
  13.2 0.3 edge_lat_sums.1
  13.6 4.8 %collective-permute-start.8 = (bf16[19,128,128]{2,1,0:T(8,128)(2,1)S(1)}, bf16[19,128,128]{2,1,0:T(8,128)(2,1)S(1)}, u32[]{:S(2)}, u32[]{:S(2)}) collective-permute-start(bf16[19,128,128]{2,1,0:T(8,128)(2,1)S(1)} %edge_lat_sums.1), channel_id=1, source_target_pairs={{0,28},{4,8},{8,4},{12,16},{16,12},{20,24},{24,20},{28,0},{1,29},{... | collective-permute-start | bytes 1867784 | tf_op jit(solution)/shard_map/ppermute | solution.py:256
  18.4 5.1 %own_sums.1.own_ref.refs_0_ = f32[80,128,256]{2,1,0:T(8,128)S(1)} custom-call(bf16[80,64,256]{2,1,0:T(8,128)(2,1)S(1)} %get-tuple-element.20.edge_ref.ref, bf16[80,64,256]{2,1,0:T(8,128)(2,1)S(1)} %get-tuple-element.24.inner_ref, bf16[256,256]{1,0:T(8,128)(2,1)S(1)} %copy-done, bf16[128,192]{1,0:T(8,128)(2,1)S(1)} %copy-done.3, ...), custom_call_target="tpu_custom_call" | custom-call | tf_op jit(solution)/shard_map/own_sums/pallas_call | solution.py:276
  23.5 0.1 tile_rows.1
  23.6 0.1 collective-permute-start.4
  23.6 3.2 %collective-permute-start.5 = (bf16[19,32,128]{2,1,0:T(8,128)(2,1)S(1)}, bf16[19,32,128]{2,1,0:T(8,128)(2,1)S(1)}, u32[]{:S(2)}, u32[]{:S(2)}) collective-permute-start(bf16[19,32,128]{2,1,0:T(8,128)(2,1)S(1)} %get-tuple-element.31), channel_id=1, source_target_pairs={{1,2},{2,1},{5,6},{6,5},{9,10},{10,9},{13,14},{14,13},{17,18},{18,... | collective-permute-start | bytes 466952 | tf_op jit(solution)/shard_map/ppermute | solution.py:256
  26.9 1.0 %near_rows.1.own_ref = f32[80,128,256]{2,1,0:T(8,128)S(1)} custom-call(f32[80,128,256]{2,1,0:T(8,128)S(1)} %own_sums.1.own_ref.refs_0_, bf16[80,32,256]{2,1,0:T(8,128)(2,1)S(1)} %collective-permute-done.1.rows_ref, bf16[256,256]{1,0:T(8,128)(2,1)S(1)} %copy-done, bf16[2,256,256]{2,1,0:T(8,128)(2,1)S(1)} %copy-done.1), custom_call_target="tpu_custom_call", output_to_operand_aliasing={{}: (0, {})} | custom-call | tf_op jit(solution)/shard_map/near_rows/pallas_call | solution.py:276
  27.9 2.2 %collective-permute-done.2.rows_ref = bf16[80,32,256]{2,1,0:T(8,128)(2,1)S(1)} collective-permute-done((bf16[80,32,256]{2,1,0:T(8,128)(2,1)S(1)}, bf16[80,32,256]{2,1,0:T(8,128)(2,1)S(1)}, u32[]{:S(2)}, u32[]{:S(2)}) %collective-permute-start.2) | collective-permute-done | bytes 1310752 | tf_op jit(solution)/shard_map/ppermute | solution.py:256
  30.2 1.0 %far_rows.1.after_ref.acc_ref = f32[80,128,256]{2,1,0:T(8,128)S(1)} custom-call(f32[80,128,256]{2,1,0:T(8,128)S(1)} %near_rows.1.own_ref, bf16[80,32,256]{2,1,0:T(8,128)(2,1)S(1)} %collective-permute-done.2.rows_ref, bf16[256,256]{1,0:T(8,128)(2,1)S(1)} %copy-done, bf16[2,256,256]{2,1,0:T(8,128)(2,1)S(1)} %copy-done.1), custom_call_target="tpu_custom_call", output_to_operand_aliasing={{}: (0, {})} | custom-call | tf_op jit(solution)/shard_map/far_rows/pallas_call | solution.py:276
  31.2 1.4 %collective-permute-done.3.inner_ref = bf16[19,64,128]{2,1,0:T(8,128)(2,1)S(1)} collective-permute-done((bf16[19,64,128]{2,1,0:T(8,128)(2,1)S(1)}, bf16[19,64,128]{2,1,0:T(8,128)(2,1)S(1)}, u32[]{:S(2)}, u32[]{:S(2)}) %collective-permute-start.3) | collective-permute-done | bytes 311328 | tf_op jit(solution)/shard_map/ppermute | solution.py:246
  32.6 0.3 first_lat_sums.1.done_ref
  33.0 2.8 %edge_sums.1 = bf16[80,128,256]{2,1,0:T(8,128)(2,1)} custom-call(f32[80,128,256]{2,1,0:T(8,128)S(1)} %far_rows.1.after_ref.acc_ref, bf16[19,128,128]{2,1,0:T(8,128)(2,1)S(1)} %first_lat_sums.1.done_ref, bf16[19,128,128]{2,1,0:T(8,128)(2,1)S(1)} %collective-permute-done.8.tiles_ref, bf16[8,256,256]{2,1,0:T(8,128)(2,1)S(1)} %copy-done.2), custom_call_target="tpu_custom_call" | custom-call | tf_op jit(solution)/shard_map/edge_sums/pallas_call | solution.py:276
  (13 shorter events, 0.0 us)
Async XLA Ops:
  2.9 15.5 %collective-permute-start = (bf16[19,64,128]{2,1,0:T(8,128)(2,1)S(1)}, bf16[19,64,128]{2,1,0:T(8,128)(2,1)S(1)}, u32[]{:S(2)}, u32[]{:S(2)}) collective-permute-start(bf16[19,64,128]{2,1,0:T(8,128)(2,1)S(1)} %get-tuple-element.25), channel_id=1, source_target_pairs={{0,4},{4,0},{8,12},{12,8},{16,20},{20,16},{24,28},{28,24},{1,5},{5... | collective-permute-start | bytes 933896 | tf_op jit(solution)/shard_map/ppermute | solution.py:246
  5.0 5.9 %collective-permute-start.6 = (bf16[19,32,128]{2,1,0:T(8,128)(2,1)S(1)}, bf16[19,32,128]{2,1,0:T(8,128)(2,1)S(1)}, u32[]{:S(2)}, u32[]{:S(2)}) collective-permute-start(bf16[19,32,128]{2,1,0:T(8,128)(2,1)S(1)} %get-tuple-element.33), channel_id=1, source_target_pairs={{0,1},{1,0},{2,3},{3,2},{4,5},{5,4},{6,7},{7,6},{8,9},{9,8},{10,11... | collective-permute-start | bytes 466952 | tf_op jit(solution)/shard_map/ppermute | solution.py:246
  6.1 7.2 %collective-permute-start.7 = (bf16[19,32,128]{2,1,0:T(8,128)(2,1)S(1)}, bf16[19,32,128]{2,1,0:T(8,128)(2,1)S(1)}, u32[]{:S(2)}, u32[]{:S(2)}) collective-permute-start(bf16[19,32,128]{2,1,0:T(8,128)(2,1)S(1)} %get-tuple-element.34), channel_id=1, source_target_pairs={{1,2},{2,1},{5,6},{6,5},{9,10},{10,9},{13,14},{14,13},{17,18},{18,... | collective-permute-start | bytes 466952 | tf_op jit(solution)/shard_map/ppermute | solution.py:256
  9.1 4.1 %copy-start.3 = (bf16[128,192]{1,0:T(8,128)(2,1)S(1)}, bf16[128,192]{1,0:T(8,128)(2,1)}, u32[]{:S(2)}) copy-start(bf16[128,192]{1,0:T(8,128)(2,1)} %constant.11.clone.lat_ref) | copy-start | bytes 147460
  10.3 8.1 %copy-start = (bf16[256,256]{1,0:T(8,128)(2,1)S(1)}, bf16[256,256]{1,0:T(8,128)(2,1)}, u32[]{:S(2)}) copy-start(bf16[256,256]{1,0:T(8,128)(2,1)} %constant.8.clone.center_ref) | copy-start | bytes 393220
  10.3 22.3 %collective-permute-start.3 = (bf16[19,64,128]{2,1,0:T(8,128)(2,1)S(1)}, bf16[19,64,128]{2,1,0:T(8,128)(2,1)S(1)}, u32[]{:S(2)}, u32[]{:S(2)}) collective-permute-start(bf16[19,64,128]{2,1,0:T(8,128)(2,1)S(1)} %get-tuple-element.29), channel_id=1, source_target_pairs={{0,4},{4,0},{8,12},{12,8},{16,20},{20,16},{24,28},{28,24},{1,5},{5... | collective-permute-start | bytes 933896 | tf_op jit(solution)/shard_map/ppermute | solution.py:246
  10.8 12.8 %collective-permute-start.1 = (bf16[80,32,256]{2,1,0:T(8,128)(2,1)S(1)}, bf16[80,32,256]{2,1,0:T(8,128)(2,1)S(1)}, u32[]{:S(2)}, u32[]{:S(2)}) collective-permute-start(bf16[80,32,256]{2,1,0:T(8,128)(2,1)S(1)} %get-tuple-element.27), channel_id=1, source_target_pairs={{0,1},{1,0},{2,3},{3,2},{4,5},{5,4},{6,7},{7,6},{8,9},{9,8},{10,11... | collective-permute-start | bytes 3932168 | tf_op jit(solution)/shard_map/ppermute | solution.py:246
  10.9 19.2 %collective-permute-start.2 = (bf16[80,32,256]{2,1,0:T(8,128)(2,1)S(1)}, bf16[80,32,256]{2,1,0:T(8,128)(2,1)S(1)}, u32[]{:S(2)}, u32[]{:S(2)}) collective-permute-start(bf16[80,32,256]{2,1,0:T(8,128)(2,1)S(1)} %get-tuple-element.28), channel_id=1, source_target_pairs={{1,2},{2,1},{5,6},{6,5},{9,10},{10,9},{13,14},{14,13},{17,18},{18,... | collective-permute-start | bytes 3932168 | tf_op jit(solution)/shard_map/ppermute | solution.py:256
  13.6 19.4 %collective-permute-start.8 = (bf16[19,128,128]{2,1,0:T(8,128)(2,1)S(1)}, bf16[19,128,128]{2,1,0:T(8,128)(2,1)S(1)}, u32[]{:S(2)}, u32[]{:S(2)}) collective-permute-start(bf16[19,128,128]{2,1,0:T(8,128)(2,1)S(1)} %edge_lat_sums.1), channel_id=1, source_target_pairs={{0,28},{4,8},{8,4},{12,16},{16,12},{20,24},{24,20},{28,0},{1,29},{... | collective-permute-start | bytes 1867784 | tf_op jit(solution)/shard_map/ppermute | solution.py:256
  23.5 3.4 %copy-start.1 = (bf16[2,256,256]{2,1,0:T(8,128)(2,1)S(1)}, bf16[2,256,256]{2,1,0:T(8,128)(2,1)}, u32[]{:S(2)}) copy-start(bf16[2,256,256]{2,1,0:T(8,128)(2,1)} %constant.10.clone.border_ref) | copy-start | bytes 786436
  23.6 9.1 %collective-permute-start.4 = (bf16[19,32,128]{2,1,0:T(8,128)(2,1)S(1)}, bf16[19,32,128]{2,1,0:T(8,128)(2,1)S(1)}, u32[]{:S(2)}, u32[]{:S(2)}) collective-permute-start(bf16[19,32,128]{2,1,0:T(8,128)(2,1)S(1)} %get-tuple-element.30), channel_id=1, source_target_pairs={{0,1},{1,0},{2,3},{3,2},{4,5},{5,4},{6,7},{7,6},{8,9},{9,8},{10,11... | collective-permute-start | bytes 466952 | tf_op jit(solution)/shard_map/ppermute | solution.py:246
  23.6 9.0 %collective-permute-start.5 = (bf16[19,32,128]{2,1,0:T(8,128)(2,1)S(1)}, bf16[19,32,128]{2,1,0:T(8,128)(2,1)S(1)}, u32[]{:S(2)}, u32[]{:S(2)}) collective-permute-start(bf16[19,32,128]{2,1,0:T(8,128)(2,1)S(1)} %get-tuple-element.31), channel_id=1, source_target_pairs={{1,2},{2,1},{5,6},{6,5},{9,10},{10,9},{13,14},{14,13},{17,18},{18,... | collective-permute-start | bytes 466952 | tf_op jit(solution)/shard_map/ppermute | solution.py:256
  31.2 1.8 %copy-start.2 = (bf16[8,256,256]{2,1,0:T(8,128)(2,1)S(1)}, bf16[8,256,256]{2,1,0:T(8,128)(2,1)}, u32[]{:S(2)}) copy-start(bf16[8,256,256]{2,1,0:T(8,128)(2,1)} %constant.9.clone.spread_ref) | copy-start | bytes 3145732

commit v7 on v6

--- a/solution.py
+++ b/solution.py
@@ -104,7 +104,7 @@
     for f in range(first, first + count):
         level = f % gvm_ref.shape[0]
         grad = jnp.concatenate([gvm_ref[level, row : row + n] for row, n in pieces], axis=0)
-        prod_ref[f] = (raw_ref[f].astype(jnp.float32) * grad.astype(jnp.float32)).astype(BF)
+        prod_ref[f] = raw_ref[f] * grad
     for start, n, extra, tile in all_units(CHUNKS):
         if first <= start < first + count:
             tiles = pack(prod_ref, (start, n, extra), select_ref)

time: 36.5 us -> 36.5 us (level)
  no operation moved by 1% of the time
where the time goes in v7:
time: 36.5 us; the launch traced here: 36 us
  starting transfers between devices  17 us (47%)
  Pallas kernels  14.8 us (41%)
  waiting for transfers between devices  3.75 us (10%)
    pallas_call x11, Pallas kernels, call(): pl.pallas_call(kernel, in_specs=specs or [IN_VMEM] * len(args), out_specs...  14.8 us
    ppermute x4, starting transfers between devices, second_partner(): return lax.ppermute(x, axis, pairs)  13.4 us
    ppermute x5, starting transfers between devices, first_partner(): lax.ppermute(x, axis, [(i, i ^ 1) for i in range(lax.axis_size(axis))])  3.58 us
    ppermute x4, waiting for transfers between devices, second_partner(): return lax.ppermute(x, axis, pairs)  2.24 us
    ppermute x5, waiting for transfers between devices, first_partner(): lax.ppermute(x, axis, [(i, i ^ 1) for i in range(lax.axis_size(axis))])  1.51 us
  transfers between devices with their start and end apart: 9, of which 2 were waited for; matrix products, arithmetic and copies ran while one was open for 0% of the time, Pallas kernels for 26%

profile of v7, /device:TPU:1, one launch (start us, length us, event | category | flops | bytes accessed | tf_op | source)
XLA Modules:
  0.0 36.0 jit_solution(4231993201491071987)
XLA Ops:
  0.0 2.8 %pack_edge_rows.1 = (bf16[19,64,128]{2,1,0:T(8,128)(2,1)S(1)}, bf16[19,64,128]{2,1,0:T(8,128)(2,1)S(1)}, bf16[80,64,256]{2,1,0:T(8,128)(2,1)S(1)}, bf16[8,256,25...) custom-call(bf16[80,128,256]{2,1,0:T(8,128)(2,1)} %bitcast.2, ...), custom_call_target="tpu_custom_call" | custom-call | tf_op jit(solution)/shard_map/pack_edge_rows/pallas_call | solution.py:276
  2.8 2.1 %collective-permute-start = (bf16[19,64,128]{2,1,0:T(8,128)(2,1)S(1)}, bf16[19,64,128]{2,1,0:T(8,128)(2,1)S(1)}, u32[]{:S(2)}, u32[]{:S(2)}) collective-permute-start(bf16[19,64,128]{2,1,0:T(8,128)(2,1)S(1)} %get-tuple-element.25), channel_id=1, source_target_pairs={{0,4},{4,0},{8,12},{12,8},{16,20},{20,16},{24,28},{28,24},{1,5},{5... | collective-permute-start | bytes 933896 | tf_op jit(solution)/shard_map/ppermute | solution.py:246
  4.9 0.1 packed_rows.1
  5.0 1.0 %collective-permute-start.6 = (bf16[19,32,128]{2,1,0:T(8,128)(2,1)S(1)}, bf16[19,32,128]{2,1,0:T(8,128)(2,1)S(1)}, u32[]{:S(2)}, u32[]{:S(2)}) collective-permute-start(bf16[19,32,128]{2,1,0:T(8,128)(2,1)S(1)} %get-tuple-element.33), channel_id=1, source_target_pairs={{0,1},{1,0},{2,3},{3,2},{4,5},{5,4},{6,7},{7,6},{8,9},{9,8},{10,11... | collective-permute-start | bytes 466952 | tf_op jit(solution)/shard_map/ppermute | solution.py:246
  6.0 3.0 %collective-permute-start.7 = (bf16[19,32,128]{2,1,0:T(8,128)(2,1)S(1)}, bf16[19,32,128]{2,1,0:T(8,128)(2,1)S(1)}, u32[]{:S(2)}, u32[]{:S(2)}) collective-permute-start(bf16[19,32,128]{2,1,0:T(8,128)(2,1)S(1)} %get-tuple-element.34), channel_id=1, source_target_pairs={{1,2},{2,1},{5,6},{6,5},{9,10},{10,9},{13,14},{14,13},{17,18},{18,... | collective-permute-start | bytes 466952 | tf_op jit(solution)/shard_map/ppermute | solution.py:256
  9.1 0.0 copy-start.3
  9.1 1.2 %pack_inner_rows.1 = (bf16[19,64,128]{2,1,0:T(8,128)(2,1)S(1)}, bf16[19,64,128]{2,1,0:T(8,128)(2,1)S(1)}, bf16[80,64,256]{2,1,0:T(8,128)(2,1)S(1)}) custom-call(bf16[80,64,256]{2,1,0:T(8,128)(2,1)S(1)} %get-tuple-element.21.raw_ref, bf16[2,128,256]{2,1,0:T(8,128)(2,1)S(1)} %get-tuple-element.22.gvm_ref, bf16[8,256,256]{2,1,0:T(8,128)(2,1)S(1)} %get-tuple-element.23.select_ref), custom_call_target="tpu_custom_call" | custom-call | tf_op jit(solution)/shard_map/pack_inner_rows/pallas_call | solution.py:276
  10.2 0.3 collective-permute-start.3
  10.6 0.2 edge_rows.1
  10.7 0.1 collective-permute-start.1
  10.8 2.3 %collective-permute-start.2 = (bf16[80,32,256]{2,1,0:T(8,128)(2,1)S(1)}, bf16[80,32,256]{2,1,0:T(8,128)(2,1)S(1)}, u32[]{:S(2)}, u32[]{:S(2)}) collective-permute-start(bf16[80,32,256]{2,1,0:T(8,128)(2,1)S(1)} %get-tuple-element.28), channel_id=1, source_target_pairs={{1,2},{2,1},{5,6},{6,5},{9,10},{10,9},{13,14},{14,13},{17,18},{18,... | collective-permute-start | bytes 3932168 | tf_op jit(solution)/shard_map/ppermute | solution.py:256
  13.1 0.3 edge_lat_sums.1
  13.5 4.8 %collective-permute-start.8 = (bf16[19,128,128]{2,1,0:T(8,128)(2,1)S(1)}, bf16[19,128,128]{2,1,0:T(8,128)(2,1)S(1)}, u32[]{:S(2)}, u32[]{:S(2)}) collective-permute-start(bf16[19,128,128]{2,1,0:T(8,128)(2,1)S(1)} %edge_lat_sums.1), channel_id=1, source_target_pairs={{0,28},{4,8},{8,4},{12,16},{16,12},{20,24},{24,20},{28,0},{1,29},{... | collective-permute-start | bytes 1867784 | tf_op jit(solution)/shard_map/ppermute | solution.py:256
  18.3 5.0 %own_sums.1.own_ref.refs_0_ = f32[80,128,256]{2,1,0:T(8,128)S(1)} custom-call(bf16[80,64,256]{2,1,0:T(8,128)(2,1)S(1)} %get-tuple-element.20.edge_ref.ref, bf16[80,64,256]{2,1,0:T(8,128)(2,1)S(1)} %get-tuple-element.24.inner_ref, bf16[256,256]{1,0:T(8,128)(2,1)S(1)} %copy-done, bf16[128,192]{1,0:T(8,128)(2,1)S(1)} %copy-done.3, ...), custom_call_target="tpu_custom_call" | custom-call | tf_op jit(solution)/shard_map/own_sums/pallas_call | solution.py:276
  23.4 0.0 copy-start.1
  23.4 0.1 tile_rows.1
  23.5 0.1 collective-permute-start.4
  23.6 3.2 %collective-permute-start.5 = (bf16[19,32,128]{2,1,0:T(8,128)(2,1)S(1)}, bf16[19,32,128]{2,1,0:T(8,128)(2,1)S(1)}, u32[]{:S(2)}, u32[]{:S(2)}) collective-permute-start(bf16[19,32,128]{2,1,0:T(8,128)(2,1)S(1)} %get-tuple-element.31), channel_id=1, source_target_pairs={{1,2},{2,1},{5,6},{6,5},{9,10},{10,9},{13,14},{14,13},{17,18},{18,... | collective-permute-start | bytes 466952 | tf_op jit(solution)/shard_map/ppermute | solution.py:256
  26.8 1.0 %near_rows.1.own_ref = f32[80,128,256]{2,1,0:T(8,128)S(1)} custom-call(f32[80,128,256]{2,1,0:T(8,128)S(1)} %own_sums.1.own_ref.refs_0_, bf16[80,32,256]{2,1,0:T(8,128)(2,1)S(1)} %collective-permute-done.1.rows_ref, bf16[256,256]{1,0:T(8,128)(2,1)S(1)} %copy-done, bf16[2,256,256]{2,1,0:T(8,128)(2,1)S(1)} %copy-done.1), custom_call_target="tpu_custom_call", output_to_operand_aliasing={{}: (0, {})} | custom-call | tf_op jit(solution)/shard_map/near_rows/pallas_call | solution.py:276
  27.8 2.2 %collective-permute-done.2.rows_ref = bf16[80,32,256]{2,1,0:T(8,128)(2,1)S(1)} collective-permute-done((bf16[80,32,256]{2,1,0:T(8,128)(2,1)S(1)}, bf16[80,32,256]{2,1,0:T(8,128)(2,1)S(1)}, u32[]{:S(2)}, u32[]{:S(2)}) %collective-permute-start.2) | collective-permute-done | bytes 1310752 | tf_op jit(solution)/shard_map/ppermute | solution.py:256
  30.1 1.0 %far_rows.1.after_ref.acc_ref = f32[80,128,256]{2,1,0:T(8,128)S(1)} custom-call(f32[80,128,256]{2,1,0:T(8,128)S(1)} %near_rows.1.own_ref, bf16[80,32,256]{2,1,0:T(8,128)(2,1)S(1)} %collective-permute-done.2.rows_ref, bf16[256,256]{1,0:T(8,128)(2,1)S(1)} %copy-done, bf16[2,256,256]{2,1,0:T(8,128)(2,1)S(1)} %copy-done.1), custom_call_target="tpu_custom_call", output_to_operand_aliasing={{}: (0, {})} | custom-call | tf_op jit(solution)/shard_map/far_rows/pallas_call | solution.py:276
  31.1 1.5 %collective-permute-done.3.inner_ref = bf16[19,64,128]{2,1,0:T(8,128)(2,1)S(1)} collective-permute-done((bf16[19,64,128]{2,1,0:T(8,128)(2,1)S(1)}, bf16[19,64,128]{2,1,0:T(8,128)(2,1)S(1)}, u32[]{:S(2)}, u32[]{:S(2)}) %collective-permute-start.3) | collective-permute-done | bytes 311328 | tf_op jit(solution)/shard_map/ppermute | solution.py:246
  32.6 0.3 first_lat_sums.1.done_ref
  33.0 2.8 %edge_sums.1 = bf16[80,128,256]{2,1,0:T(8,128)(2,1)} custom-call(f32[80,128,256]{2,1,0:T(8,128)S(1)} %far_rows.1.after_ref.acc_ref, bf16[19,128,128]{2,1,0:T(8,128)(2,1)S(1)} %first_lat_sums.1.done_ref, bf16[19,128,128]{2,1,0:T(8,128)(2,1)S(1)} %collective-permute-done.8.tiles_ref, bf16[8,256,256]{2,1,0:T(8,128)(2,1)S(1)} %copy-done.2), custom_call_target="tpu_custom_call" | custom-call | tf_op jit(solution)/shard_map/edge_sums/pallas_call | solution.py:276
  (13 shorter events, 0.0 us)
Async XLA Ops:
  2.8 15.5 %collective-permute-start = (bf16[19,64,128]{2,1,0:T(8,128)(2,1)S(1)}, bf16[19,64,128]{2,1,0:T(8,128)(2,1)S(1)}, u32[]{:S(2)}, u32[]{:S(2)}) collective-permute-start(bf16[19,64,128]{2,1,0:T(8,128)(2,1)S(1)} %get-tuple-element.25), channel_id=1, source_target_pairs={{0,4},{4,0},{8,12},{12,8},{16,20},{20,16},{24,28},{28,24},{1,5},{5... | collective-permute-start | bytes 933896 | tf_op jit(solution)/shard_map/ppermute | solution.py:246
  5.0 5.8 %collective-permute-start.6 = (bf16[19,32,128]{2,1,0:T(8,128)(2,1)S(1)}, bf16[19,32,128]{2,1,0:T(8,128)(2,1)S(1)}, u32[]{:S(2)}, u32[]{:S(2)}) collective-permute-start(bf16[19,32,128]{2,1,0:T(8,128)(2,1)S(1)} %get-tuple-element.33), channel_id=1, source_target_pairs={{0,1},{1,0},{2,3},{3,2},{4,5},{5,4},{6,7},{7,6},{8,9},{9,8},{10,11... | collective-permute-start | bytes 466952 | tf_op jit(solution)/shard_map/ppermute | solution.py:246
  6.0 7.1 %collective-permute-start.7 = (bf16[19,32,128]{2,1,0:T(8,128)(2,1)S(1)}, bf16[19,32,128]{2,1,0:T(8,128)(2,1)S(1)}, u32[]{:S(2)}, u32[]{:S(2)}) collective-permute-start(bf16[19,32,128]{2,1,0:T(8,128)(2,1)S(1)} %get-tuple-element.34), channel_id=1, source_target_pairs={{1,2},{2,1},{5,6},{6,5},{9,10},{10,9},{13,14},{14,13},{17,18},{18,... | collective-permute-start | bytes 466952 | tf_op jit(solution)/shard_map/ppermute | solution.py:256
  9.1 4.1 %copy-start.3 = (bf16[128,192]{1,0:T(8,128)(2,1)S(1)}, bf16[128,192]{1,0:T(8,128)(2,1)}, u32[]{:S(2)}) copy-start(bf16[128,192]{1,0:T(8,128)(2,1)} %constant.11.clone.lat_ref) | copy-start | bytes 147460
  10.2 8.1 %copy-start = (bf16[256,256]{1,0:T(8,128)(2,1)S(1)}, bf16[256,256]{1,0:T(8,128)(2,1)}, u32[]{:S(2)}) copy-start(bf16[256,256]{1,0:T(8,128)(2,1)} %constant.8.clone.center_ref) | copy-start | bytes 393220
  10.2 22.3 %collective-permute-start.3 = (bf16[19,64,128]{2,1,0:T(8,128)(2,1)S(1)}, bf16[19,64,128]{2,1,0:T(8,128)(2,1)S(1)}, u32[]{:S(2)}, u32[]{:S(2)}) collective-permute-start(bf16[19,64,128]{2,1,0:T(8,128)(2,1)S(1)} %get-tuple-element.29), channel_id=1, source_target_pairs={{0,4},{4,0},{8,12},{12,8},{16,20},{20,16},{24,28},{28,24},{1,5},{5... | collective-permute-start | bytes 933896 | tf_op jit(solution)/shard_map/ppermute | solution.py:246
  10.7 12.8 %collective-permute-start.1 = (bf16[80,32,256]{2,1,0:T(8,128)(2,1)S(1)}, bf16[80,32,256]{2,1,0:T(8,128)(2,1)S(1)}, u32[]{:S(2)}, u32[]{:S(2)}) collective-permute-start(bf16[80,32,256]{2,1,0:T(8,128)(2,1)S(1)} %get-tuple-element.27), channel_id=1, source_target_pairs={{0,1},{1,0},{2,3},{3,2},{4,5},{5,4},{6,7},{7,6},{8,9},{9,8},{10,11... | collective-permute-start | bytes 3932168 | tf_op jit(solution)/shard_map/ppermute | solution.py:246
  10.8 19.2 %collective-permute-start.2 = (bf16[80,32,256]{2,1,0:T(8,128)(2,1)S(1)}, bf16[80,32,256]{2,1,0:T(8,128)(2,1)S(1)}, u32[]{:S(2)}, u32[]{:S(2)}) collective-permute-start(bf16[80,32,256]{2,1,0:T(8,128)(2,1)S(1)} %get-tuple-element.28), channel_id=1, source_target_pairs={{1,2},{2,1},{5,6},{6,5},{9,10},{10,9},{13,14},{14,13},{17,18},{18,... | collective-permute-start | bytes 3932168 | tf_op jit(solution)/shard_map/ppermute | solution.py:256
  13.5 19.5 %collective-permute-start.8 = (bf16[19,128,128]{2,1,0:T(8,128)(2,1)S(1)}, bf16[19,128,128]{2,1,0:T(8,128)(2,1)S(1)}, u32[]{:S(2)}, u32[]{:S(2)}) collective-permute-start(bf16[19,128,128]{2,1,0:T(8,128)(2,1)S(1)} %edge_lat_sums.1), channel_id=1, source_target_pairs={{0,28},{4,8},{8,4},{12,16},{16,12},{20,24},{24,20},{28,0},{1,29},{... | collective-permute-start | bytes 1867784 | tf_op jit(solution)/shard_map/ppermute | solution.py:256
  23.4 3.4 %copy-start.1 = (bf16[2,256,256]{2,1,0:T(8,128)(2,1)S(1)}, bf16[2,256,256]{2,1,0:T(8,128)(2,1)}, u32[]{:S(2)}) copy-start(bf16[2,256,256]{2,1,0:T(8,128)(2,1)} %constant.10.clone.border_ref) | copy-start | bytes 786436
  23.5 9.1 %collective-permute-start.4 = (bf16[19,32,128]{2,1,0:T(8,128)(2,1)S(1)}, bf16[19,32,128]{2,1,0:T(8,128)(2,1)S(1)}, u32[]{:S(2)}, u32[]{:S(2)}) collective-permute-start(bf16[19,32,128]{2,1,0:T(8,128)(2,1)S(1)} %get-tuple-element.30), channel_id=1, source_target_pairs={{0,1},{1,0},{2,3},{3,2},{4,5},{5,4},{6,7},{7,6},{8,9},{9,8},{10,11... | collective-permute-start | bytes 466952 | tf_op jit(solution)/shard_map/ppermute | solution.py:246
  23.6 9.0 %collective-permute-start.5 = (bf16[19,32,128]{2,1,0:T(8,128)(2,1)S(1)}, bf16[19,32,128]{2,1,0:T(8,128)(2,1)S(1)}, u32[]{:S(2)}, u32[]{:S(2)}) collective-permute-start(bf16[19,32,128]{2,1,0:T(8,128)(2,1)S(1)} %get-tuple-element.31), channel_id=1, source_target_pairs={{1,2},{2,1},{5,6},{6,5},{9,10},{10,9},{13,14},{14,13},{17,18},{18,... | collective-permute-start | bytes 466952 | tf_op jit(solution)/shard_map/ppermute | solution.py:256
  31.1 1.9 %copy-start.2 = (bf16[8,256,256]{2,1,0:T(8,128)(2,1)S(1)}, bf16[8,256,256]{2,1,0:T(8,128)(2,1)}, u32[]{:S(2)}) copy-start(bf16[8,256,256]{2,1,0:T(8,128)(2,1)} %constant.9.clone.spread_ref) | copy-start | bytes 3145732
